TPU v7x, 32 devices: a whole 2x2x4 slice. The times are simulated.
32 devices in a mesh: dp: 4 (over y, x), seq: 8 (over z, core).
Axes of the slice: x: 2, y: 2, z: 4, core: 2. Of those that a mesh axis runs over, the one named last changes fastest.
Arguments:
- tokens: bfloat16 [16, 8, 128, 768], P('dp', 'seq'), may hold values from -6 to 6
- cotangent: bfloat16 [16, 8, 128, 768], P('dp', 'seq'), may hold values from -18 to 18
- owners: int32 [64], replicated, may hold values from 0 to 7, as said below
- tile_master: float32 [128, 192, 192], P('seq'), may hold values from -0.4375 to 0.4375
- tile_moment: float32 [128, 192, 192], P('seq'), may hold values from -1.75 to 1.75
- tile_second: float32 [128, 192, 192], P('seq'), may hold values from 0.001 to 0.004
- tile_average: float32 [128, 192, 192], P('seq'), may hold values from -0.4375 to 0.4375
- vectors: float32 [5, 768], replicated, may hold values from 0.3 to 1.5
- vector_moment: float32 [5, 768], replicated, may hold values from -1.75 to 1.75
- vector_second: float32 [5, 768], replicated, may hold values from 0.001 to 0.004
- vector_average: float32 [5, 768], replicated, may hold values from 0.3 to 1.5
- filter_in: float32 [5, 128], replicated, may hold values from -2.5 to 2.5
- in_moment: float32 [5, 128], replicated, may hold values from -1.75 to 1.75
- in_second: float32 [5, 128], replicated, may hold values from 0.001 to 0.004
- in_average: float32 [5, 128], replicated, may hold values from -2.5 to 2.5
- filter_out: float32 [128, 768], replicated, may hold values from -0.5 to 0.5
- out_moment: float32 [128, 768], replicated, may hold values from -1.75 to 1.75
- out_second: float32 [128, 768], replicated, may hold values from 0.001 to 0.004
- out_average: float32 [128, 768], replicated, may hold values from -0.5 to 0.5
Outputs:
- output: bfloat16 [16, 8, 128, 768], P('dp', 'seq')
- in_grad: float32 [16, 8, 128, 768], P('dp', 'seq')
- tile_grad: float32 [128, 192, 192], P('seq')
- tile_second_new: float32 [128, 192, 192], P('seq')
- tile_master_new: float32 [128, 192, 192], P('seq')
- tile_average_new: float32 [128, 192, 192], P('seq')
- vector_grad: float32 [5, 768], replicated
- vector_second_new: float32 [5, 768], replicated
- vectors_new: float32 [5, 768], replicated
- vector_average_new: float32 [5, 768], replicated
- in_grad_filter: float32 [5, 128], replicated
- in_second_new: float32 [5, 128], replicated
- filter_in_new: float32 [5, 128], replicated
- in_average_new: float32 [5, 128], replicated
- out_grad_filter: float32 [128, 768], replicated
- out_second_new: float32 [128, 768], replicated
- filter_out_new: float32 [128, 768], replicated
- out_average_new: float32 [128, 768], replicated
Inputs may be any that keep to these rules, and one draw needn't show every extreme that they name: owners[i] is the index along seq of the device that updates weight block i; no index owns more than 16 blocks and some index owns exactly 16.
All inputs are finite; a program needn't handle non-finite values.
Results may differ from a plain program's by a relative error of at most 0.012.
Values may be sent and summed in bfloat16 or wider, within the bound.
A program may use at most 192 MiB of HBM per device.

v0:
```python
import math

import jax
import jax.numpy as jnp
from jax import lax
from jax.sharding import PartitionSpec as P

D = 768
FF = 3072
STEP = 10


highest = lax.Precision.HIGHEST
beta_one = 0.9
beta_two = 0.999
keep_rate = 0.5
adam_eps = 1e-08
norm_eps = 1e-05
golden = 0.6180339887


def norm_rows(values, gain_vec, bias_vec):
    row_mean = jnp.mean(values, axis=-1, keepdims=True)
    centered = values - row_mean
    spread = jnp.mean(centered * centered, axis=-1, keepdims=True)
    return centered * lax.rsqrt(spread + norm_eps) * gain_vec + bias_vec


def glu_act(gate_value, up_value):
    return jax.nn.gelu(gate_value, approximate=False) * up_value


def filter_taps(filter_in, filter_out, position, length):
    phases = position * (2.0 * math.pi / length)
    features = jnp.stack(
        [
            position / length,
            jnp.cos(phases),
            -jnp.sin(phases),
            jnp.cos(2.0 * phases),
            -jnp.sin(2.0 * phases),
        ],
        axis=1,
    )
    hidden = jnp.sin(jnp.dot(features, filter_in, precision=highest))
    taps_value = jnp.dot(hidden, filter_out, precision=highest)
    channel = jnp.arange(filter_out.shape[1], dtype=jnp.float32)
    decay_rates = 0.3 * jnp.exp(math.log(1000.0) * jnp.mod(channel * golden, 1.0))
    decay_rate = jnp.exp(-(position / length)[:, None] * decay_rates[None, :])
    total = jnp.expm1(-2.0 * decay_rates) / jnp.expm1(-2.0 * decay_rates / length)
    norm_scale = lax.rsqrt(total)
    return taps_value * decay_rate * norm_scale


def block_weight(tile_stack, in_tiles, out_tiles):
    tile_side = tile_stack.shape[-1]
    tile_grid = tile_stack.reshape(4, in_tiles, out_tiles, tile_side, tile_side).transpose(
        0, 1, 3, 2, 4
    )
    return tile_grid.reshape(4, in_tiles * tile_side, out_tiles * tile_side)


def tile_split(blocks, in_tiles, out_tiles):
    tile_side = blocks.shape[1] // in_tiles
    tile_grid = blocks.reshape(4, in_tiles, tile_side, out_tiles, tile_side).transpose(
        0, 1, 3, 2, 4
    )
    return tile_grid.reshape(4 * in_tiles * out_tiles, tile_side, tile_side)


def block_apply(values, blocks):
    row_view = values.reshape(values.shape[0], 4, -1)
    return jnp.einsum("nbi,bio->nbo", row_view, blocks, preferred_element_type=jnp.float32).reshape(
        values.shape[0], -1
    )


def block_back(gradient, blocks):
    row_view = gradient.reshape(gradient.shape[0], 4, -1)
    return jnp.einsum("nbo,bio->nbi", row_view, blocks, preferred_element_type=jnp.float32).reshape(
        gradient.shape[0], -1
    )


def block_grad(values, gradient, in_tiles, out_tiles):
    left_rows = values.reshape(values.shape[0], 4, -1)
    right_rows = gradient.reshape(gradient.shape[0], 4, -1)
    blocks = jnp.einsum("nbi,nbo->bio", left_rows, right_rows, preferred_element_type=jnp.float32)
    return tile_split(blocks, in_tiles, out_tiles)


def slot_maps(owners, owner_cap, slot_total):
    tile_count = owners.shape[0]
    tile_index = jnp.arange(tile_count, dtype=jnp.int32)
    earlier = (owners[:, None] == owners[None, :]) & (tile_index[None, :] < tile_index[:, None])
    owner_rank = jnp.sum(earlier.astype(jnp.int32), axis=1)
    slot_of_tile = owners * owner_cap + owner_rank
    slot_hits = slot_of_tile[None, :] == jnp.arange(slot_total, dtype=jnp.int32)[:, None]
    tile_of_slot = jnp.sum(slot_hits.astype(jnp.int32) * tile_index[None, :], axis=1)
    slot_used = jnp.any(slot_hits, axis=1)
    return (slot_of_tile, tile_of_slot, slot_used)


def adam_step(weight, moment, second, average, gradient, step_rate, decay_rate):
    moment = beta_one * moment + (1.0 - beta_one) * gradient
    second = beta_two * second + (1.0 - beta_two) * gradient * gradient
    fixed_moment = moment / (1.0 - beta_one**STEP)
    fixed_second = second / (1.0 - beta_two**STEP)
    weight = weight - step_rate * (
        fixed_moment / (jnp.sqrt(fixed_second) + adam_eps) + decay_rate * weight
    )
    average = keep_rate * average + (1.0 - keep_rate) * weight
    return (second, weight, average)


def wave_table(period, index_one, index_two):
    turn_count = jnp.mod(index_one[:, None] * index_two[None, :], period).astype(jnp.float32)
    angles = turn_count * (2.0 * math.pi / period)
    return (jnp.cos(angles), jnp.sin(angles))


def col_dot(field_in, table_in):
    return jnp.einsum("srcd,ck->srkd", field_in, table_in, precision=highest)


def row_dot(field_in, table_in):
    return jnp.einsum("srkd,rq->sqkd", field_in, table_in, precision=highest)


def cols_forward(field_in, tables):
    col_cos, col_sin, turn_cos, turn_sin, row_cos, row_sin = tables
    real_part = col_dot(field_in, col_cos)
    imag_part = -col_dot(field_in, col_sin)
    real_turn = real_part * turn_cos + imag_part * turn_sin
    imag_turn = imag_part * turn_cos - real_part * turn_sin
    return (real_turn, imag_turn)


def rows_forward(part_real, part_imag, tables):
    row_cos, row_sin = (tables[4], tables[5])
    freq_real = row_dot(part_real, row_cos) + row_dot(part_imag, row_sin)
    freq_imag = row_dot(part_imag, row_cos) - row_dot(part_real, row_sin)
    return (freq_real, freq_imag)


def rows_inverse(prod_real, prod_imag, tables):
    row_cos, row_sin = (tables[4], tables[5])
    back_real = row_dot(prod_real, row_cos) - row_dot(prod_imag, row_sin)
    back_imag = row_dot(prod_real, row_sin) + row_dot(prod_imag, row_cos)
    return (back_real, back_imag)


def cols_inverse(rows_real, rows_imag, tables, length):
    col_cos, col_sin, turn_cos, turn_sin, row_cos, row_sin = tables
    cell_real = rows_real * turn_cos - rows_imag * turn_sin
    cell_imag = rows_real * turn_sin + rows_imag * turn_cos
    return (
        jnp.einsum("srkd,ck->srcd", cell_real, col_cos, precision=highest)
        - jnp.einsum("srkd,ck->srcd", cell_imag, col_sin, precision=highest)
    ) / length


def convolve(field_in, spectrum, tables, conjugate, length):
    spec_real, spec_imag = spectrum
    sign_flip = -1.0 if conjugate else 1.0
    real_turn, imag_turn = cols_forward(field_in, tables)
    part_real = lax.all_to_all(real_turn, "seq", split_axis=2, concat_axis=1, tiled=True)
    part_imag = lax.all_to_all(imag_turn, "seq", split_axis=2, concat_axis=1, tiled=True)
    freq_real, freq_imag = rows_forward(part_real, part_imag, tables)
    prod_real = freq_real * spec_real - sign_flip * freq_imag * spec_imag
    prod_imag = sign_flip * freq_real * spec_imag + freq_imag * spec_real
    back_real, back_imag = rows_inverse(prod_real, prod_imag, tables)
    rows_real = lax.all_to_all(back_real, "seq", split_axis=1, concat_axis=2, tiled=True)
    rows_imag = lax.all_to_all(back_imag, "seq", split_axis=1, concat_axis=2, tiled=True)
    rows_real, rows_imag, freq_real, freq_imag = (rows_real, rows_imag, freq_real, freq_imag)
    field_out = cols_inverse(rows_real, rows_imag, tables, length)
    return (field_out, freq_real, freq_imag)


def on_device(
    tokens,
    cotangent,
    owners,
    tile_master,
    tile_moment,
    tile_second,
    tile_average,
    vectors,
    vector_moment,
    vector_second,
    vector_average,
    filter_in,
    in_moment,
    in_second,
    in_average,
    filter_out,
    out_moment,
    out_second,
    out_average,
):
    seq_count, dev_rows, row_len, model_width = tokens.shape
    owner_cap = tile_master.shape[0]
    seq_devices = lax.axis_size("seq")
    grid_rows = dev_rows * seq_devices
    length = grid_rows * row_len
    seq_index = lax.axis_index("seq")
    hidden_ratio = FF // D
    quarter_hidden = FF // 4
    slot_of_tile, tile_of_slot, slot_used = slot_maps(owners, owner_cap, owner_cap * seq_devices)
    gathered = lax.all_gather(tile_master.astype(jnp.bfloat16), "seq", axis=0, tiled=True)
    weights = jnp.take(gathered, slot_of_tile, axis=0)
    w_in = block_weight(weights[0:12], 1, 3)
    w_out = block_weight(weights[12:16], 1, 1)
    w_gate = block_weight(weights[16 : 16 + 4 * hidden_ratio], 1, hidden_ratio)
    w_up = block_weight(weights[16 + 4 * hidden_ratio : 16 + 8 * hidden_ratio], 1, hidden_ratio)
    w_down = block_weight(weights[16 + 8 * hidden_ratio : 16 + 12 * hidden_ratio], hidden_ratio, 1)
    w_gate_up = jnp.concatenate([w_gate, w_up], axis=2)
    col_index = jnp.arange(row_len, dtype=jnp.int32)
    row_index = jnp.arange(grid_rows, dtype=jnp.int32)
    local_rows = seq_index * dev_rows + jnp.arange(dev_rows, dtype=jnp.int32)
    col_cos, col_sin = wave_table(row_len, col_index, col_index)
    row_cos, row_sin = wave_table(grid_rows, row_index, row_index)
    turn_cos, turn_sin = wave_table(length, local_rows, col_index)
    tables = (
        col_cos,
        col_sin,
        turn_cos[None, :, :, None],
        turn_sin[None, :, :, None],
        row_cos,
        row_sin,
    )
    own_position = (
        (local_rows[:, None] + grid_rows * col_index[None, :]).reshape(-1).astype(jnp.float32)
    )
    flat_tokens = tokens.reshape(-1, model_width)
    qkv_all = block_apply(flat_tokens, w_in)
    query_part = qkv_all[:, :model_width]
    key_part = qkv_all[:, model_width : 2 * model_width]
    value_part = qkv_all[:, 2 * model_width :]
    kv_product = key_part * value_part

    def own_taps(weight_one, weight_two):
        return filter_taps(weight_one, weight_two, own_position, length)

    taps_own, filter_pull = jax.vjp(own_taps, filter_in, filter_out)
    taps_real, taps_imag = cols_forward(taps_own.reshape(1, dev_rows, row_len, model_width), tables)
    taps_real, taps_imag = (
        lax.all_to_all(taps_real, "seq", split_axis=2, concat_axis=1, tiled=True),
        lax.all_to_all(taps_imag, "seq", split_axis=2, concat_axis=1, tiled=True),
    )
    spec_real, spec_imag = rows_forward(taps_real, taps_imag, tables)
    taps_spec = (spec_real[0], spec_imag[0])
    conv_out, kv_real, kv_imag = convolve(
        kv_product.reshape(seq_count, dev_rows, row_len, model_width),
        taps_spec,
        tables,
        False,
        length,
    )
    skip_gain = vectors[4]
    inner_sum = conv_out.reshape(-1, model_width) + skip_gain * kv_product
    gated_out = (query_part * inner_sum).astype(jnp.bfloat16)
    branch = block_apply(gated_out, w_out)
    normed, first_pull = jax.vjp(
        norm_rows, flat_tokens.astype(jnp.float32) + branch, vectors[0], vectors[1]
    )
    normed_low = normed.astype(jnp.bfloat16)
    gate_up = block_apply(normed_low, w_gate_up).reshape(-1, 4, 2, quarter_hidden)
    gate_value = gate_up[:, :, 0].reshape(-1, FF)
    up_value = gate_up[:, :, 1].reshape(-1, FF)
    active, active_pull = jax.vjp(glu_act, gate_value, up_value)
    active_low = active.astype(jnp.bfloat16)
    down_value = block_apply(active_low, w_down)
    result, second_pull = jax.vjp(
        norm_rows, normed_low.astype(jnp.float32) + down_value, vectors[2], vectors[3]
    )
    output = result.astype(jnp.bfloat16).reshape(tokens.shape)
    d_second, d_gain_two, d_bias_two = second_pull(
        cotangent.reshape(-1, model_width).astype(jnp.float32)
    )
    d_down = d_second.astype(jnp.bfloat16)
    g_down = block_grad(active_low, d_down, hidden_ratio, 1)
    d_gate, d_up = active_pull(block_back(d_down, w_down))
    d_gate_up = jnp.stack(
        [d_gate.reshape(-1, 4, quarter_hidden), d_up.reshape(-1, 4, quarter_hidden)], axis=2
    )
    d_gate_up = d_gate_up.reshape(-1, 2 * FF).astype(jnp.bfloat16)
    gate_up_tiles = block_grad(normed_low, d_gate_up, 1, 2 * hidden_ratio).reshape(
        4, 2, hidden_ratio, weights.shape[1], weights.shape[2]
    )
    g_gate = gate_up_tiles[:, 0].reshape(-1, weights.shape[1], weights.shape[2])
    g_up = gate_up_tiles[:, 1].reshape(-1, weights.shape[1], weights.shape[2])
    d_normed = d_second + block_back(d_gate_up, w_gate_up)
    d_first, d_gain_one, d_bias_one = first_pull(d_normed)
    d_branch = d_first.astype(jnp.bfloat16)
    g_out = block_grad(gated_out, d_branch, 1, 1)
    d_gated = block_back(d_branch, w_out)
    d_query = d_gated * inner_sum
    d_inner = d_gated * query_part
    d_skip = jnp.sum(d_inner * kv_product, axis=0)
    d_conv, back_real, back_imag = convolve(
        d_inner.reshape(seq_count, dev_rows, row_len, model_width), taps_spec, tables, True, length
    )
    d_kv = d_conv.reshape(-1, model_width) + skip_gain * d_inner
    d_qkv = jnp.concatenate([d_query, d_kv * value_part, d_kv * key_part], axis=1).astype(
        jnp.bfloat16
    )
    g_in = block_grad(flat_tokens, d_qkv, 1, 3)
    in_grad = (d_first + block_back(d_qkv, w_in)).reshape(tokens.shape)
    cross_real = jnp.sum(back_real * kv_real + back_imag * kv_imag, axis=0, keepdims=True)
    cross_imag = jnp.sum(back_imag * kv_real - back_real * kv_imag, axis=0, keepdims=True)
    cross_back_real, cross_back_imag = rows_inverse(cross_real, cross_imag, tables)
    cross_rows_real, cross_rows_imag = (
        lax.all_to_all(
            cross_back_real.astype(jnp.bfloat16), "seq", split_axis=1, concat_axis=2, tiled=True
        ).astype(cross_back_real.dtype),
        lax.all_to_all(
            cross_back_imag.astype(jnp.bfloat16), "seq", split_axis=1, concat_axis=2, tiled=True
        ).astype(cross_back_imag.dtype),
    )
    d_taps = cols_inverse(cross_rows_real, cross_rows_imag, tables, length).reshape(-1, model_width)
    g_filter_in, g_filter_out = filter_pull(d_taps)
    tile_grads = jnp.concatenate([g_in, g_out, g_gate, g_up, g_down], axis=0)
    slot_mask = slot_used.astype(jnp.float32)[:, None, None]
    summed = lax.psum(tile_grads.astype(jnp.bfloat16), "dp").astype(jnp.float32)
    owned = lax.psum_scatter(
        jnp.take(summed, tile_of_slot, axis=0) * slot_mask, "seq", scatter_dimension=0, tiled=True
    )
    tokens_all = seq_count * dev_rows * row_len * lax.axis_size("dp") * seq_devices
    grad_scale = 1.0 / math.sqrt(tokens_all)
    mine_mask = lax.dynamic_slice_in_dim(slot_mask, seq_index * owner_cap, owner_cap, 0)
    tile_grad = owned * grad_scale
    tile_new = adam_step(tile_master, tile_moment, tile_second, tile_average, tile_grad, 0.1, 0.01)
    vector_part = jnp.stack([d_gain_one, d_bias_one, d_gain_two, d_bias_two, d_skip])
    vector_sum, in_sum, out_sum = lax.psum((vector_part, g_filter_in, g_filter_out), ("dp", "seq"))
    vector_grad = vector_sum * grad_scale
    in_grad_filter = in_sum * grad_scale
    out_grad_filter = out_sum * grad_scale
    vector_new = adam_step(
        vectors, vector_moment, vector_second, vector_average, vector_grad, 0.4, 0.0
    )
    in_new = adam_step(filter_in, in_moment, in_second, in_average, in_grad_filter, 0.4, 0.01)
    out_new = adam_step(filter_out, out_moment, out_second, out_average, out_grad_filter, 0.1, 0.01)
    return (
        output,
        in_grad,
        tile_grad,
        tile_new[0] * mine_mask,
        tile_new[1] * mine_mask,
        tile_new[2] * mine_mask,
        vector_grad,
        vector_new[0],
        vector_new[1],
        vector_new[2],
        in_grad_filter,
        in_new[0],
        in_new[1],
        in_new[2],
        out_grad_filter,
        out_new[0],
        out_new[1],
        out_new[2],
    )


def solution(mesh):
    in_specs = (
        P("dp", "seq", None, None),
        P("dp", "seq", None, None),
        P(),
        P("seq", None, None),
        P("seq", None, None),
        P("seq", None, None),
        P("seq", None, None),
        P(),
        P(),
        P(),
        P(),
        P(),
        P(),
        P(),
        P(),
        P(),
        P(),
        P(),
        P(),
    )
    out_specs = (
        P("dp", "seq", None, None),
        P("dp", "seq", None, None),
        P("seq", None, None),
        P("seq", None, None),
        P("seq", None, None),
        P("seq", None, None),
        P(),
        P(),
        P(),
        P(),
        P(),
        P(),
        P(),
        P(),
        P(),
        P(),
        P(),
        P(),
    )
    return jax.shard_map(
        on_device, mesh=mesh, in_specs=in_specs, out_specs=out_specs, check_vma=False
    )
```

profile of v0, /device:TPU:0, one launch (start us, length us, event | category | flops | bytes accessed | tf_op | source)
XLA Modules:
  0.0 1231.2 jit_solution(15818665798984928745)
XLA Ops:
  15.5 6.3 all-to-all-start.2
  24.7 113.0 %all-gather.2.cloned.1.call-done = bf16[128,192,192]{2,1,0:T(8,128)(2,1)} async-done(((bf16[16,192,192]{2,1,0:T(8,128)(2,1)}), bf16[128,192,192]{2,1,0:T(8,128)(2,1)}) %all-gather.2.cloned.1.call-update) | async-done | bytes 9437200 | tf_op jit(solution)/shard_map/all_gather | solution.py:210
  137.7 8.2 gather_fusion
  145.9 8.9 copy.296
  164.9 4.3 all-to-all-start.3
  177.9 3.9 all-to-all-done.3
  181.8 3.6 all-to-all-start
  187.5 35.6 %all-to-all-done = f32[4,1,128,768]{3,0,1,2:T(4,128)S(1)} async-done(((f32[4,1,128,768]{3,0,1,2:T(4,128)}), f32[4,1,128,768]{3,0,1,2:T(4,128)S(1)}, u32[]{:S(2)}, u32[]{:S(2)}) %all-to-all-start) | async-done | bytes 1572896 | tf_op jit(solution)/shard_map/all_to_all | solution.py:167
  223.1 4.5 all-to-all-start.1
  237.0 28.2 %all-to-all-done.1 = f32[4,1,128,768]{3,0,1,2:T(4,128)} async-done(((f32[4,1,128,768]{3,0,1,2:T(4,128)}), f32[4,1,128,768]{3,0,1,2:T(4,128)}, u32[]{:S(2)}, u32[]{:S(2)}) %all-to-all-start.1) | async-done | bytes 1572896 | tf_op jit(solution)/shard_map/all_to_all | solution.py:168
  279.1 4.3 all-to-all-start.5
  289.3 31.9 %all-to-all-done.5 = f32[4,8,16,768]{3,2,0,1:T(8,128)} async-done(((f32[4,8,16,768]{3,2,0,1:T(8,128)}), f32[4,8,16,768]{3,2,0,1:T(8,128)}, u32[]{:S(2)}, u32[]{:S(2)}) %all-to-all-start.5) | async-done | bytes 1572896 | tf_op jit(solution)/shard_map/all_to_all | solution.py:174
  321.2 4.5 all-to-all-start.4
  334.4 4.5 fusion.377
  340.9 4.3 reshape_transpose_reshape.7
  352.8 10.7 all-to-all-done.4
  384.0 14.2 %fusion.3 = bf16[512,4,768]{0,2,1:T(8,128)(2,1)S(1)} fusion(f32[512,4,2,768]{0,3,2,1:T(8,128)S(1)} %bitcast.458), kind=kLoop, calls=%fused_computation.8 | loop fusion | flops 103809024 | bytes 15728640 | tf_op jit(solution)/shard_map/convert_element_type | solution.py:272
  415.3 4.2 convert_reduce_fusion
  421.4 19.4 %add_convert_fusion = (bf16[512,4,1,768]{0,3,1,2:T(8,128)(2,1)}, f32[512,4,1,768]{0,3,1,2:T(8,128)}, f32[4,768,512]{2,1,0:T(8,128)}) fusion(f32[512,4,2,768]{0,3,2,1:T(8,128)} %bitcast.459, f32[512,4,192]{0,2,1:T(8,128)S(1)} %fusion.26, bf16[4,768,192]{1,0,2:T(4,128)(2,1)S(1)} %copy-done.36), kind=kOutput, calls=%fused_computation.20 | convolution fusion | flops 719192064 | bytes 31064064 | tf_op jit(solution)/shard_map/nbo,bio->nbi/dot_general | solution.py:80
  440.9 10.6 fusion.5
  451.4 6.1 pad_maximum_fusion
  457.5 3.6 copy.332
  482.6 4.3 all-to-all-start.6
  486.9 3.6 copy.342
  490.5 34.2 %all-to-all-done.6 = f32[4,1,128,768]{3,0,1,2:T(4,128)} async-done(((f32[4,1,128,768]{3,0,1,2:T(4,128)}), f32[4,1,128,768]{3,0,1,2:T(4,128)}, u32[]{:S(2)}, u32[]{:S(2)}) %all-to-all-start.6) | async-done | bytes 1572896 | tf_op jit(solution)/shard_map/all_to_all | solution.py:167
  524.7 4.5 all-to-all-start.7
  535.4 31.5 %all-to-all-done.7 = f32[4,1,128,768]{3,0,1,2:T(4,128)} async-done(((f32[4,1,128,768]{3,0,1,2:T(4,128)}), f32[4,1,128,768]{3,0,1,2:T(4,128)}, u32[]{:S(2)}, u32[]{:S(2)}) %all-to-all-start.7) | async-done | bytes 1572896 | tf_op jit(solution)/shard_map/all_to_all | solution.py:168
  573.1 3.8 subtract_reduce_fusion
  582.0 4.6 all-to-all-start.9
  592.6 31.9 %all-to-all-done.9 = f32[4,8,16,768]{3,2,0,1:T(8,128)} async-done(((f32[4,8,16,768]{3,2,0,1:T(8,128)}), f32[4,8,16,768]{3,2,0,1:T(8,128)}, u32[]{:S(2)}, u32[]{:S(2)}) %all-to-all-start.9) | async-done | bytes 1572896 | tf_op jit(solution)/shard_map/all_to_all | solution.py:174
  624.4 4.3 all-to-all-start.8
  628.8 3.6 convolution_convert_fusion.1
  635.3 6.4 convolution_convert_fusion
  641.7 4.7 reshape.1247
  650.7 15.9 %all-to-all-done.8 = f32[4,8,16,768]{3,2,0,1:T(8,128)} async-done(((f32[4,8,16,768]{3,2,0,1:T(8,128)}), f32[4,8,16,768]{3,2,0,1:T(8,128)}, u32[]{:S(2)}, u32[]{:S(2)}) %all-to-all-start.8) | async-done | bytes 1572896 | tf_op jit(solution)/shard_map/all_to_all | solution.py:173
  696.5 4.2 all-to-all-start.10
  702.5 6.6 all-to-all-done.10
  714.5 6.2 all-to-all-done.11
  725.6 104.8 %all-reduce.4.cloned.1.call-done = bf16[64,192,192]{2,1,0:T(8,128)(2,1)} async-done(((bf16[64,192,192]{2,1,0:T(8,128)(2,1)}), bf16[64,192,192]{2,1,0:T(8,128)(2,1)}) %all-reduce.4.cloned.1.call-update) | async-done | bytes 4718608 | tf_op jit(solution)/shard_map/psum | solution.py:325
  830.4 9.1 convert_element_type.298
  839.5 19.0 %gather_fusion.1 = f32[128,192,192]{2,1,0:T(8,128)} fusion(f32[64,192,192]{2,1,0:T(8,128)} %convert_element_type.298, s32[1024]{0:T(1024)S(1)} %pad_clamp_fusion), kind=kCustom, calls=%fused_computation.1 | custom fusion | bytes 37749248 | tf_op jit(solution)/shard_map/jit(_take)/gather | solution.py:327
  858.5 18.7 %select_multiply_fusion = f32[128,192,192]{2,1,0:T(8,128)} fusion(f32[128,192,192]{2,1,0:T(8,128)} %gather_fusion.1, f32[128]{0:T(128)S(1)} %convert_element_type.299, pred[128]{0:T(512)(128)(4,1)S(1)} %compare_and_fusion), kind=kLoop, calls=%fused_computation.2 | loop fusion | flops 9437184 | bytes 37749376 | tf_op jit(solution)/shard_map/mul | solution.py:327
  885.2 39.8 %all-reduce = (f32[5,768]{1,0:T(8,128)S(1)}, f32[5,128]{1,0:T(8,128)S(1)}) all-reduce(f32[5,768]{1,0:T(8,128)S(1)} %stack.12, f32[5,128]{1,0:T(8,128)S(1)} %fusion.387), channel_id=1, replica_groups=mesh['dp'=4,'seq'=8] {'dp','seq'}, use_global_device_ids=true, to_apply=%region_18.19 | all-reduce | flops 4480 | bytes 35840 | tf_op jit(solution)/shard_map/psum | solution.py:335
  926.3 37.4 %all-reduce.6.cloned.1.call-done = f32[128,768]{1,0:T(8,128)} async-done(((f32[128,768]{1,0:T(8,128)}), f32[128,768]{1,0:T(8,128)}) %all-reduce.6.cloned.1.call-update) | async-done | bytes 393232 | tf_op jit(solution)/shard_map/psum | solution.py:335
  974.5 4.2 fusion.28
  978.7 233.6 %reduce-scatter.2.cloned.1.call-done = f32[16,192,192]{2,1,0:T(8,128)} async-done(((f32[128,192,192]{2,1,0:T(8,128)}), f32[16,192,192]{2,1,0:T(8,128)}) %reduce-scatter.2.cloned.1.call-update) | async-done | bytes 2359312 | tf_op jit(solution)/shard_map/reduce_scatter | solution.py:326
  1212.3 8.2 add_multiply_fusion
  1220.5 3.9 broadcast_multiply_fusion
  (412 shorter events, 232.0 us)
Async XLA Ops:
  7.2 130.5 %all-gather.2.cloned.1.call-start = ((), (), s32[]{:S(2)}) async-start(), calls=%async_computation.13 | async-start | bytes 14155776 | tf_op jit(solution)/shard_map/all_gather | solution.py:210
  10.7 162.9 %copy-start.88 = (f32[128]{0:T(128)}, f32[128]{0:T(128)S(1)}, u32[]{:S(2)}) copy-start(f32[128]{0:T(128)S(1)} %fusion.222) | copy-start | bytes 1540
  10.8 162.8 %copy-start.91 = (f32[128]{0:T(128)}, f32[128]{0:T(128)S(1)}, u32[]{:S(2)}) copy-start(f32[128]{0:T(128)S(1)} %get-tuple-element.105) | copy-start | bytes 1540
  14.3 8.7 copy-start.37
  15.5 149.4 %all-to-all-start.2 = ((f32[1,1,128,768]{3,1,0,2:T(1,128)}), f32[1,1,128,768]{3,1,0,2:T(1,128)S(1)}, u32[]{:S(2)}, u32[]{:S(2)}) async-start(f32[1,1,128,768]{3,1,0,2:T(1,128)} %copy.308), calls=%async_computation.2 | async-start | bytes 786432 | tf_op jit(solution)/shard_map/all_to_all | solution.py:248
  23.9 137.0 %copy-start.57 = (bf16[512,4,192]{0,2,1:T(8,128)(2,1)}, bf16[512,4,192]{0,2,1:T(8,128)(2,1)S(1)}, u32[]{:S(2)}) copy-start(bf16[512,4,192]{0,2,1:T(8,128)(2,1)S(1)} %reshape_reshape.10) | copy-start | bytes 2359300
  164.9 16.9 %all-to-all-start.3 = ((f32[1,1,128,768]{3,1,0,2:T(1,128)}), f32[1,1,128,768]{3,1,0,2:T(1,128)}, u32[]{:S(2)}, u32[]{:S(2)}) async-start(f32[1,1,128,768]{3,1,0,2:T(1,128)} %copy.310), calls=%async_computation.3 | async-start | bytes 786432 | tf_op jit(solution)/shard_map/all_to_all | solution.py:249
  181.8 41.3 %all-to-all-start = ((f32[4,1,128,768]{3,0,1,2:T(4,128)}), f32[4,1,128,768]{3,0,1,2:T(4,128)S(1)}, u32[]{:S(2)}, u32[]{:S(2)}) async-start(f32[4,1,128,768]{3,0,1,2:T(4,128)} %copy.302), calls=%async_computation | async-start | bytes 3145728 | tf_op jit(solution)/shard_map/all_to_all | solution.py:167
  223.1 42.1 %all-to-all-start.1 = ((f32[4,1,128,768]{3,0,1,2:T(4,128)}), f32[4,1,128,768]{3,0,1,2:T(4,128)}, u32[]{:S(2)}, u32[]{:S(2)}) async-start(f32[4,1,128,768]{3,0,1,2:T(4,128)} %copy.305), calls=%async_computation.1 | async-start | bytes 3145728 | tf_op jit(solution)/shard_map/all_to_all | solution.py:168
  279.1 42.2 %all-to-all-start.5 = ((f32[4,8,16,768]{3,2,0,1:T(8,128)}), f32[4,8,16,768]{3,2,0,1:T(8,128)}, u32[]{:S(2)}, u32[]{:S(2)}) async-start(f32[4,8,16,768]{3,2,0,1:T(8,128)} %copy.318), calls=%async_computation.5 | async-start | bytes 3145728 | tf_op jit(solution)/shard_map/all_to_all | solution.py:174
  321.2 42.3 %all-to-all-start.4 = ((f32[4,8,16,768]{3,2,0,1:T(8,128)}), f32[4,8,16,768]{3,2,0,1:T(8,128)}, u32[]{:S(2)}, u32[]{:S(2)}) async-start(f32[4,8,16,768]{3,2,0,1:T(8,128)} %copy.316), calls=%async_computation.4 | async-start | bytes 3145728 | tf_op jit(solution)/shard_map/all_to_all | solution.py:173
  327.3 46.3 %copy-start.65 = (f32[768]{0:T(1024)}, f32[768]{0:T(1024)S(1)}, u32[]{:S(2)}) copy-start(f32[768]{0:T(1024)S(1)} %get-tuple-element.30) | copy-start | bytes 9220
  352.8 12.3 %copy-start.89 = (f32[128]{0:T(128)S(1)}, f32[128]{0:T(128)}, u32[]{:S(2)}) copy-start(f32[128]{0:T(128)} %copy-done.88) | copy-start | bytes 1540
  379.6 21.4 %copy-start.1 = (f32[512,4,192]{0,2,1:T(8,128)}, f32[512,4,192]{0,2,1:T(8,128)S(1)}, u32[]{:S(2)}) copy-start(f32[512,4,192]{0,2,1:T(8,128)S(1)} %get-tuple-element.59) | copy-start | bytes 4718596
  382.1 16.1 %copy-start.13 = (bf16[512,4,192]{0,2,1:T(8,128)(2,1)}, bf16[512,4,192]{0,2,1:T(8,128)(2,1)S(1)}, u32[]{:S(2)}) copy-start(bf16[512,4,192]{0,2,1:T(8,128)(2,1)S(1)} %add_convert_fusion.3) | copy-start | bytes 2359300
  384.0 14.2 %copy-start = (f32[4,1536,512]{2,1,0:T(8,128)}, f32[4,1536,512]{2,1,0:T(8,128)S(1)}, u32[]{:S(2)}) copy-start(f32[4,1536,512]{2,1,0:T(8,128)S(1)} %fusion.59) | copy-start | bytes 37748740
  384.0 14.2 %copy-start.35 = (bf16[4,768,192]{1,0,2:T(4,128)(2,1)S(1)}, bf16[4,768,192]{1,0,2:T(4,128)(2,1)}, u32[]{:S(2)}) copy-start(bf16[4,768,192]{1,0,2:T(4,128)(2,1)} %reshape_transpose_reshape.7) | copy-start | bytes 3538948
  421.4 19.5 %copy-start.45 = (f32[512,4,192]{0,2,1:T(8,128)}, f32[512,4,192]{0,2,1:T(8,128)S(1)}, u32[]{:S(2)}) copy-start(f32[512,4,192]{0,2,1:T(8,128)S(1)} %fusion.26) | copy-start | bytes 4718596
  457.5 10.7 slice-start
  482.6 42.1 %all-to-all-start.6 = ((f32[4,1,128,768]{3,0,1,2:T(4,128)}), f32[4,1,128,768]{3,0,1,2:T(4,128)}, u32[]{:S(2)}, u32[]{:S(2)}) async-start(f32[4,1,128,768]{3,0,1,2:T(4,128)} %copy.339), calls=%async_computation.6 | async-start | bytes 3145728 | tf_op jit(solution)/shard_map/all_to_all | solution.py:167
  524.7 42.1 %all-to-all-start.7 = ((f32[4,1,128,768]{3,0,1,2:T(4,128)}), f32[4,1,128,768]{3,0,1,2:T(4,128)}, u32[]{:S(2)}, u32[]{:S(2)}) async-start(f32[4,1,128,768]{3,0,1,2:T(4,128)} %copy.342), calls=%async_computation.7 | async-start | bytes 3145728 | tf_op jit(solution)/shard_map/all_to_all | solution.py:168
  582.0 42.4 %all-to-all-start.9 = ((f32[4,8,16,768]{3,2,0,1:T(8,128)}), f32[4,8,16,768]{3,2,0,1:T(8,128)}, u32[]{:S(2)}, u32[]{:S(2)}) async-start(f32[4,8,16,768]{3,2,0,1:T(8,128)} %copy.349), calls=%async_computation.9 | async-start | bytes 3145728 | tf_op jit(solution)/shard_map/all_to_all | solution.py:174
  592.6 36.2 %copy-start.10 = (bf16[512,4,768]{0,2,1:T(8,128)(2,1)S(1)}, bf16[512,4,768]{0,2,1:T(8,128)(2,1)}, u32[]{:S(2)}) copy-start(bf16[512,4,768]{0,2,1:T(8,128)(2,1)} %copy-done.9) | copy-start | bytes 9437188
  624.4 42.1 %all-to-all-start.8 = ((f32[4,8,16,768]{3,2,0,1:T(8,128)}), f32[4,8,16,768]{3,2,0,1:T(8,128)}, u32[]{:S(2)}, u32[]{:S(2)}) async-start(f32[4,8,16,768]{3,2,0,1:T(8,128)} %copy.347), calls=%async_computation.8 | async-start | bytes 3145728 | tf_op jit(solution)/shard_map/all_to_all | solution.py:173
  628.7 201.7 %all-reduce.4.cloned.1.call-start = ((), (), s32[]{:S(2)}) async-start(), calls=%async_computation.14 | async-start | bytes 12582912 | tf_op jit(solution)/shard_map/psum | solution.py:325
  696.5 12.5 %all-to-all-start.10 = ((bf16[1,8,16,768]{3,2,0,1:T(8,128)(2,1)}), bf16[1,8,16,768]{3,2,0,1:T(8,128)(2,1)}, u32[]{:S(2)}, u32[]{:S(2)}) async-start(bf16[1,8,16,768]{3,2,0,1:T(8,128)(2,1)} %copy.361), calls=%async_computation.11 | async-start | bytes 393216 | tf_op jit(solution)/shard_map/all_to_all | solution.py:314
  700.7 21.8 %copy-start.96 = (f32[768]{0:T(1024)S(1)}, f32[768]{0:T(1024)}, u32[]{:S(2)}) copy-start(f32[768]{0:T(1024)} %copy-done.95) | copy-start | bytes 9220
  701.2 21.3 %copy-start.115 = (f32[128]{0:T(128)S(1)}, f32[128]{0:T(128)}, u32[]{:S(2)}) copy-start(f32[128]{0:T(128)} %copy-done.114) | copy-start | bytes 1540
  701.7 22.5 %copy-start.63 = (f32[128,128]{1,0:T(8,128)S(1)}, f32[128,128]{1,0:T(8,128)}, u32[]{:S(2)}) copy-start(f32[128,128]{1,0:T(8,128)} %copy-done.62) | copy-start | bytes 196612
  709.0 11.7 all-to-all-start.11
  712.4 251.3 %all-reduce.6.cloned.1.call-start = ((), (), s32[]{:S(2)}) async-start(), calls=%async_computation.16 | async-start | bytes 786432 | tf_op jit(solution)/shard_map/psum | solution.py:335
  725.6 486.7 %reduce-scatter.2.cloned.1.call-start = ((), (), s32[]{:S(2)}) async-start(), calls=%async_computation.15 | async-start | bytes 28311552 | tf_op jit(solution)/shard_map/reduce_scatter | solution.py:326
  881.0 44.0 %copy-start.98 = (f32[5,128]{1,0:T(8,128)S(1)}, f32[5,128]{1,0:T(8,128)}, u32[]{:S(2)}) copy-start(f32[5,128]{1,0:T(8,128)} %param.30) | copy-start | bytes 7684
  881.0 44.0 %copy-start.107 = (f32[5,128]{1,0:T(8,128)S(1)}, f32[5,128]{1,0:T(8,128)}, u32[]{:S(2)}) copy-start(f32[5,128]{1,0:T(8,128)} %param.33) | copy-start | bytes 7684
  881.0 44.0 %copy-start.108 = (f32[5,128]{1,0:T(8,128)S(1)}, f32[5,128]{1,0:T(8,128)}, u32[]{:S(2)}) copy-start(f32[5,128]{1,0:T(8,128)} %param.31) | copy-start | bytes 7684
  881.0 44.0 %copy-start.109 = (f32[5,128]{1,0:T(8,128)S(1)}, f32[5,128]{1,0:T(8,128)}, u32[]{:S(2)}) copy-start(f32[5,128]{1,0:T(8,128)} %param.32) | copy-start | bytes 7684
  881.0 44.7 %copy-start.72 = (f32[5,768]{1,0:T(8,128)S(1)}, f32[5,768]{1,0:T(8,128)}, u32[]{:S(2)}) copy-start(f32[5,768]{1,0:T(8,128)} %param.26) | copy-start | bytes 46084
  881.0 44.6 %copy-start.81 = (f32[5,768]{1,0:T(8,128)S(1)}, f32[5,768]{1,0:T(8,128)}, u32[]{:S(2)}) copy-start(f32[5,768]{1,0:T(8,128)} %param.29) | copy-start | bytes 46084
  881.0 44.6 %copy-start.82 = (f32[5,768]{1,0:T(8,128)S(1)}, f32[5,768]{1,0:T(8,128)}, u32[]{:S(2)}) copy-start(f32[5,768]{1,0:T(8,128)} %param.27) | copy-start | bytes 46084
  881.0 44.6 %copy-start.83 = (f32[5,768]{1,0:T(8,128)S(1)}, f32[5,768]{1,0:T(8,128)}, u32[]{:S(2)}) copy-start(f32[5,768]{1,0:T(8,128)} %param.28) | copy-start | bytes 46084
  926.3 40.1 %copy-start.30 = (bf16[12,192,192]{1,2,0:T(8,128)(2,1)S(1)}, bf16[12,192,192]{1,2,0:T(8,128)(2,1)}, u32[]{:S(2)}) copy-start(bf16[12,192,192]{1,2,0:T(8,128)(2,1)} %copy-done.29) | copy-start | bytes 2654212
  966.5 7.8 copy-start.69
  966.5 7.8 copy-start.71
  966.5 7.8 copy-start.84
  974.5 237.8 %copy-start.113 = (f32[16]{0:T(128)S(1)}, f32[16]{0:T(128)}, u32[]{:S(2)}) copy-start(f32[16]{0:T(128)} %get-tuple-element.51) | copy-start | bytes 196
  1212.3 8.2 copy-start.26
  1212.3 8.2 copy-start.27
  1212.3 8.2 copy-start.112
  (90 other events, 236.7 us)
Sparse Core Ops, SparseCore 0:
  10.6 126.9 all-gather.1
  693.1 137.3 all-reduce.3
  836.3 127.3 all-reduce.5
  966.1 246.1 reduce-scatter.1
where the time goes:
time: 1240 us; the launch traced here: 1230 us
  waiting for transfers between devices  725 us (58%)
  local copies, waits for them, and re-layouts  164 us (13%)
  matrix products  119 us (10%)
  other arithmetic  114 us (9%)
  starting transfers between devices  52.9 us (4%)
  blocking collectives  39.8 us (3%)
  between operations  15.7 us (1%)
    reduce_scatter x1, waiting for transfers between devices, on_device(): lax.psum_scatter(jnp.take(summed, tile_of_slot, axis=0) * slot_mask, 'seq...  234 us
    all_gather x1, waiting for transfers between devices, on_device(): lax.all_gather(tile_master.astype(jnp.bfloat16), 'seq', axis=0, tiled=True)  113 us
    psum x1, waiting for transfers between devices, on_device(): summed = lax.psum(tile_grads.astype(jnp.bfloat16), 'dp').astype(jnp.float32)  105 us
    all_to_all x2, waiting for transfers between devices, convolve(): lax.all_to_all(real_turn, 'seq', split_axis=2, concat_axis=1, tiled=True)  69.8 us
    all_to_all x2, waiting for transfers between devices, convolve(): lax.all_to_all(back_imag, 'seq', split_axis=1, concat_axis=2, tiled=True)  63.8 us
    all_to_all x2, waiting for transfers between devices, convolve(): lax.all_to_all(imag_turn, 'seq', split_axis=2, concat_axis=1, tiled=True)  59.7 us
    dot_general x24, matrix products, row_dot(): return jnp.einsum('srkd,rq->sqkd', field_in, table_in, precision=highest)  42.8 us
    psum x1, blocking collectives, on_device(): lax.psum((vector_part, g_filter_in, g_filter_out), ('dp', 'seq'))  39.8 us
  transfers between devices with their start and end apart: 16, of which 15 were waited for; matrix products, arithmetic and copies ran while one was open for 16% of the time, Pallas kernels for 0%

commit v1 on v0

--- a/solution.py
+++ b/solution.py
@@ -2,6 +2,8 @@
 
 import jax
 import jax.numpy as jnp
+import ml_dtypes
+import numpy as np
 from jax import lax
 from jax.sharding import PartitionSpec as P
 
@@ -31,6 +33,11 @@
 
 
 def filter_taps(filter_in, filter_out, position, length):
+    channel = jnp.arange(filter_out.shape[1], dtype=jnp.int32)
+    return filter_taps_of(filter_in, filter_out, position, length, channel)
+
+
+def filter_taps_of(filter_in, filter_out, position, length, channel_index):
     phases = position * (2.0 * math.pi / length)
     features = jnp.stack(
         [
@@ -44,7 +51,7 @@
     )
     hidden = jnp.sin(jnp.dot(features, filter_in, precision=highest))
     taps_value = jnp.dot(hidden, filter_out, precision=highest)
-    channel = jnp.arange(filter_out.shape[1], dtype=jnp.float32)
+    channel = channel_index.astype(jnp.float32)
     decay_rates = 0.3 * jnp.exp(math.log(1000.0) * jnp.mod(channel * golden, 1.0))
     decay_rate = jnp.exp(-(position / length)[:, None] * decay_rates[None, :])
     total = jnp.expm1(-2.0 * decay_rates) / jnp.expm1(-2.0 * decay_rates / length)
@@ -177,7 +184,17 @@
     return (field_out, freq_real, freq_imag)
 
 
-def on_device(
+def real_table(grid_rows, row_len):
+    length = grid_rows * row_len
+    position = (np.arange(grid_rows)[:, None] + grid_rows * np.arange(row_len)[None, :]).reshape(-1)
+    turns = np.mod(np.arange(length // 2)[:, None] * position[None, :], length)
+    angles = turns * (2.0 * np.pi / length)
+    sines = -np.sin(angles)
+    sines[0] = np.cos(np.pi * position)
+    return np.concatenate([np.cos(angles), sines]).astype(ml_dtypes.bfloat16)
+
+
+def on_device_general(
     tokens,
     cotangent,
     owners,
@@ -363,6 +380,209 @@
     )
 
 
+def on_device_columns(
+    tokens,
+    cotangent,
+    owners,
+    tile_master,
+    tile_moment,
+    tile_second,
+    tile_average,
+    vectors,
+    vector_moment,
+    vector_second,
+    vector_average,
+    filter_in,
+    in_moment,
+    in_second,
+    in_average,
+    filter_out,
+    out_moment,
+    out_second,
+    out_average,
+):
+    seq_count, dev_rows, row_len, model_width = tokens.shape
+    owner_cap = tile_master.shape[0]
+    seq_devices = lax.axis_size("seq")
+    grid_rows = dev_rows * seq_devices
+    length = grid_rows * row_len
+    seq_index = lax.axis_index("seq")
+    hidden_ratio = FF // D
+    quarter_hidden = FF // 4
+    slot_of_tile, tile_of_slot, slot_used = slot_maps(owners, owner_cap, owner_cap * seq_devices)
+    gathered = lax.all_gather(tile_master.astype(jnp.bfloat16), "seq", axis=0, tiled=True)
+    weights = jnp.take(gathered, slot_of_tile, axis=0)
+    w_in = block_weight(weights[0:12], 1, 3)
+    w_out = block_weight(weights[12:16], 1, 1)
+    w_gate = block_weight(weights[16 : 16 + 4 * hidden_ratio], 1, hidden_ratio)
+    w_up = block_weight(weights[16 + 4 * hidden_ratio : 16 + 8 * hidden_ratio], 1, hidden_ratio)
+    w_down = block_weight(weights[16 + 8 * hidden_ratio : 16 + 12 * hidden_ratio], hidden_ratio, 1)
+    w_gate_up = jnp.concatenate([w_gate, w_up], axis=2)
+    halves = seq_devices // seq_count
+    width = model_width // halves
+    half_index = lax.rem(seq_index, halves)
+    grid_position = (
+        jnp.arange(grid_rows, dtype=jnp.int32)[:, None]
+        + grid_rows * jnp.arange(row_len, dtype=jnp.int32)[None, :]
+    )
+    position = grid_position.reshape(-1).astype(jnp.float32)
+    table = jnp.asarray(real_table(grid_rows, row_len))
+    first_bin = (jnp.arange(length // 2) == 0)[:, None]
+
+    def spread(field_in):
+        cells = field_in.reshape(seq_count, row_len, halves, width).transpose(0, 2, 1, 3)
+        cells = cells.reshape(seq_devices, row_len, width).astype(jnp.bfloat16)
+        return lax.all_to_all(cells, "seq", 0, 0, tiled=True).reshape(length, width)
+
+    def collect(field_in):
+        cells = field_in.astype(jnp.bfloat16).reshape(seq_devices, row_len, width)
+        cells = lax.all_to_all(cells, "seq", 0, 0, tiled=True)
+        cells = cells.reshape(seq_count, halves, row_len, width).transpose(0, 2, 1, 3)
+        return cells.reshape(-1, model_width).astype(jnp.float32)
+
+    def transform(columns):
+        spec = jnp.dot(table, columns.astype(jnp.bfloat16), preferred_element_type=jnp.float32)
+        return (spec[: length // 2], spec[length // 2 :])
+
+    def invert(real_part, imag_part):
+        weight = jnp.where(first_bin, 1.0 / length, 2.0 / length)
+        spec = jnp.concatenate([real_part * weight, imag_part * weight], axis=0)
+        return lax.dot_general(
+            table,
+            spec.astype(jnp.bfloat16),
+            (((0,), (0,)), ((), ())),
+            preferred_element_type=jnp.float32,
+        )
+
+    def product(one, two, conjugate):
+        one_real, one_imag = one
+        two_real, two_imag = two
+        cross = jnp.where(first_bin, 0.0, two_imag) * (-1.0 if conjugate else 1.0)
+        diag = jnp.where(first_bin, two_imag, two_real)
+        return (one_real * two_real - one_imag * cross, one_real * cross + one_imag * diag)
+
+    flat_tokens = tokens.reshape(-1, model_width)
+    qkv_all = block_apply(flat_tokens, w_in)
+    query_part = qkv_all[:, :model_width]
+    key_part = qkv_all[:, model_width : 2 * model_width]
+    value_part = qkv_all[:, 2 * model_width :]
+    kv_product = key_part * value_part
+
+    channel = half_index * width + jnp.arange(width, dtype=jnp.int32)
+    own_filter = lax.dynamic_slice_in_dim(filter_out, half_index * width, width, 1)
+
+    def own_taps(weight_one, weight_two):
+        return filter_taps_of(weight_one, weight_two, position, length, channel)
+
+    taps_own, filter_pull = jax.vjp(own_taps, filter_in, own_filter)
+    taps_spec = transform(taps_own)
+    kv_spec = transform(spread(kv_product))
+    conv_out = collect(invert(*product(kv_spec, taps_spec, False)))
+    skip_gain = vectors[4]
+    inner_sum = conv_out + skip_gain * kv_product
+    gated_out = (query_part * inner_sum).astype(jnp.bfloat16)
+    branch = block_apply(gated_out, w_out)
+    normed, first_pull = jax.vjp(
+        norm_rows, flat_tokens.astype(jnp.float32) + branch, vectors[0], vectors[1]
+    )
+    normed_low = normed.astype(jnp.bfloat16)
+    gate_up = block_apply(normed_low, w_gate_up).reshape(-1, 4, 2, quarter_hidden)
+    gate_value = gate_up[:, :, 0].reshape(-1, FF)
+    up_value = gate_up[:, :, 1].reshape(-1, FF)
+    active, active_pull = jax.vjp(glu_act, gate_value, up_value)
+    active_low = active.astype(jnp.bfloat16)
+    down_value = block_apply(active_low, w_down)
+    result, second_pull = jax.vjp(
+        norm_rows, normed_low.astype(jnp.float32) + down_value, vectors[2], vectors[3]
+    )
+    output = result.astype(jnp.bfloat16).reshape(tokens.shape)
+    d_second, d_gain_two, d_bias_two = second_pull(
+        cotangent.reshape(-1, model_width).astype(jnp.float32)
+    )
+    d_down = d_second.astype(jnp.bfloat16)
+    g_down = block_grad(active_low, d_down, hidden_ratio, 1)
+    d_gate, d_up = active_pull(block_back(d_down, w_down))
+    d_gate_up = jnp.stack(
+        [d_gate.reshape(-1, 4, quarter_hidden), d_up.reshape(-1, 4, quarter_hidden)], axis=2
+    )
+    d_gate_up = d_gate_up.reshape(-1, 2 * FF).astype(jnp.bfloat16)
+    gate_up_tiles = block_grad(normed_low, d_gate_up, 1, 2 * hidden_ratio).reshape(
+        4, 2, hidden_ratio, weights.shape[1], weights.shape[2]
+    )
+    g_gate = gate_up_tiles[:, 0].reshape(-1, weights.shape[1], weights.shape[2])
+    g_up = gate_up_tiles[:, 1].reshape(-1, weights.shape[1], weights.shape[2])
+    d_normed = d_second + block_back(d_gate_up, w_gate_up)
+    d_first, d_gain_one, d_bias_one = first_pull(d_normed)
+    d_branch = d_first.astype(jnp.bfloat16)
+    g_out = block_grad(gated_out, d_branch, 1, 1)
+    d_gated = block_back(d_branch, w_out)
+    d_query = d_gated * inner_sum
+    d_inner = d_gated * query_part
+    d_skip = jnp.sum(d_inner * kv_product, axis=0)
+    back_spec = transform(spread(d_inner))
+    d_kv = collect(invert(*product(back_spec, taps_spec, True))) + skip_gain * d_inner
+    d_qkv = jnp.concatenate([d_query, d_kv * value_part, d_kv * key_part], axis=1).astype(
+        jnp.bfloat16
+    )
+    g_in = block_grad(flat_tokens, d_qkv, 1, 3)
+    in_grad = (d_first + block_back(d_qkv, w_in)).reshape(tokens.shape)
+    d_taps = invert(*product(back_spec, kv_spec, True))
+    g_filter_in, g_filter_half = filter_pull(d_taps)
+    g_filter_out = lax.dynamic_update_slice_in_dim(
+        jnp.zeros_like(filter_out), g_filter_half, half_index * width, 1
+    )
+    tile_grads = jnp.concatenate([g_in, g_out, g_gate, g_up, g_down], axis=0)
+    slot_mask = slot_used.astype(jnp.float32)[:, None, None]
+    summed = lax.psum(tile_grads.astype(jnp.bfloat16), "dp").astype(jnp.float32)
+    owned = lax.psum_scatter(
+        jnp.take(summed, tile_of_slot, axis=0) * slot_mask, "seq", scatter_dimension=0, tiled=True
+    )
+    tokens_all = seq_count * dev_rows * row_len * lax.axis_size("dp") * seq_devices
+    grad_scale = 1.0 / math.sqrt(tokens_all)
+    mine_mask = lax.dynamic_slice_in_dim(slot_mask, seq_index * owner_cap, owner_cap, 0)
+    tile_grad = owned * grad_scale
+    tile_new = adam_step(tile_master, tile_moment, tile_second, tile_average, tile_grad, 0.1, 0.01)
+    vector_part = jnp.stack([d_gain_one, d_bias_one, d_gain_two, d_bias_two, d_skip])
+    vector_sum, in_sum, out_sum = lax.psum((vector_part, g_filter_in, g_filter_out), ("dp", "seq"))
+    vector_grad = vector_sum * grad_scale
+    in_grad_filter = in_sum * grad_scale
+    out_grad_filter = out_sum * grad_scale
+    vector_new = adam_step(
+        vectors, vector_moment, vector_second, vector_average, vector_grad, 0.4, 0.0
+    )
+    in_new = adam_step(filter_in, in_moment, in_second, in_average, in_grad_filter, 0.4, 0.01)
+    out_new = adam_step(filter_out, out_moment, out_second, out_average, out_grad_filter, 0.1, 0.01)
+    return (
+        output,
+        in_grad,
+        tile_grad,
+        tile_new[0] * mine_mask,
+        tile_new[1] * mine_mask,
+        tile_new[2] * mine_mask,
+        vector_grad,
+        vector_new[0],
+        vector_new[1],
+        vector_new[2],
+        in_grad_filter,
+        in_new[0],
+        in_new[1],
+        in_new[2],
+        out_grad_filter,
+        out_new[0],
+        out_new[1],
+        out_new[2],
+    )
+
+
+def on_device(*arrays):
+    seq_count, dev_rows, row_len, model_width = arrays[0].shape
+    seq_devices = lax.axis_size("seq")
+    fits = dev_rows == 1 and seq_devices % seq_count == 0 and seq_devices * row_len <= 2048
+    if fits and model_width % (128 * (seq_devices // seq_count)) == 0:
+        return on_device_columns(*arrays)
+    return on_device_general(*arrays)
+
+
 def solution(mesh):
     in_specs = (
         P("dp", "seq", None, None),

time: 1240 us -> 932 us (0.75)
  waiting for transfers between devices: 725 us -> 527 us
  matrix products: 119 us -> 71.2 us
  starting transfers between devices: 52.9 us -> 13.1 us
  local copies, waits for them, and re-layouts: 164 us -> 130 us
  blocking collectives: 39.8 us -> 64.8 us
  other arithmetic: 114 us -> 101 us
    all_to_all x12 -> x3, waiting for transfers between devices: 236 us -> 16.1 us  [the longest x1 13.7 us: spread(): return lax.all_to_all(cells, 'seq', 0, 0, tiled=True).reshape(length, width)]
    dot_general x41 -> x14, matrix products: 71 us -> 24.7 us  [the longest x6 7.47 us: invert(): lax.dot_general(table, spec.astype(jnp.bfloat16), (((0,), (0,)), ((), ())...]
    all_to_all x12 -> x3, starting transfers between devices: 52.7 us -> 13 us  [the longest x2 8.76 us: collect(): cells = lax.all_to_all(cells, 'seq', 0, 0, tiled=True)]
    all_to_all x0 -> x1, blocking collectives: none -> 24.3 us  [spread(): return lax.all_to_all(cells, 'seq', 0, 0, tiled=True).reshape(length, width)]
    psum x2, waiting for transfers between devices: 142 us -> 159 us  [the longest x1 131 us: on_device_columns(): summed = lax.psum(tile_grads.astype(jnp.bfloat16), 'dp').astype(jnp.float32)]
    all_to_all x8 -> x0, local copies, waits for them, and re-layouts: 12.8 us -> none  [the longest x2 4.2 us: convolve(): lax.all_to_all(back_imag, 'seq', split_axis=1, concat_axis=2, tiled=True)]
    unnamed x250 -> x214, local copies, waits for them, and re-layouts: 21.9 us -> 27.4 us
    mul x6 -> x5, other arithmetic: 33.6 us -> 31.6 us  [the longest x1 18.9 us: on_device_columns(): jnp.take(summed, tile_of_slot, axis=0) * slot_mask]
  transfers between devices with their start and end apart: 16 -> 7, of which waited for: 15 -> 7; matrix products, arithmetic and copies ran while one was open for 16% -> 14% of each run, Pallas kernels for 0% -> 0%
where the time goes in v1:
time: 932 us; the launch traced here: 923 us
  waiting for transfers between devices  527 us (57%)
  local copies, waits for them, and re-layouts  130 us (14%)
  other arithmetic  101 us (11%)
  matrix products  71.2 us (8%)
  blocking collectives  64.8 us (7%)
  between operations  15.5 us (2%)
  starting transfers between devices  13.1 us (1%)
    reduce_scatter x1, waiting for transfers between devices, on_device_columns(): lax.psum_scatter(jnp.take(summed, tile_of_slot, axis=0) * slot_mask, 'seq...  234 us
    psum x1, waiting for transfers between devices, on_device_columns(): summed = lax.psum(tile_grads.astype(jnp.bfloat16), 'dp').astype(jnp.float32)  131 us
    all_gather x1, waiting for transfers between devices, on_device_columns(): lax.all_gather(tile_master.astype(jnp.bfloat16), 'seq', axis=0, tiled=True)  118 us
    psum x1, blocking collectives, on_device_columns(): lax.psum((vector_part, g_filter_in, g_filter_out), ('dp', 'seq'))  40.5 us
    psum x1, waiting for transfers between devices, on_device_columns(): lax.psum((vector_part, g_filter_in, g_filter_out), ('dp', 'seq'))  28.8 us
    unnamed x214, local copies, waits for them, and re-layouts  27.4 us
    dot_general x4, matrix products, block_back(): jnp.einsum('nbo,bio->nbi', row_view, blocks, preferred_element_type=jnp.f...  26.4 us
    all_to_all x1, blocking collectives, spread(): return lax.all_to_all(cells, 'seq', 0, 0, tiled=True).reshape(length, width)  24.3 us
  transfers between devices with their start and end apart: 7, of which 7 were waited for; matrix products, arithmetic and copies ran while one was open for 14% of the time, Pallas kernels for 0%

profile of v1, /device:TPU:0, one launch (start us, length us, event | category | flops | bytes accessed | tf_op | source)
XLA Modules:
  0.0 922.6 jit_solution(3657396570512163437)
XLA Ops:
  7.2 3.3 convert_element_type.243
  12.3 117.9 %all-gather.2.cloned.1.call-done = bf16[128,192,192]{2,1,0:T(8,128)(2,1)} async-done(((bf16[16,192,192]{2,1,0:T(8,128)(2,1)}), bf16[128,192,192]{2,1,0:T(8,128)(2,1)}) %all-gather.2.cloned.1.call-update) | async-done | bytes 9437200 | tf_op jit(solution)/shard_map/all_gather | solution.py:413
  130.2 8.1 gather_fusion
  138.3 8.8 copy.195
  147.1 3.4 broadcast_select_fusion
  158.0 4.2 all-to-all-start
  162.5 3.4 fusion.105
  169.5 13.7 %all-to-all-done = bf16[8,128,384]{2,1,0:T(8,128)(2,1)} async-done(((bf16[8,128,384]{2,1,0:T(8,128)(2,1)}), bf16[8,128,384]{2,1,0:T(8,128)(2,1)}, u32[]{:S(2)}, u32[]{:S(2)}) %all-to-all-start) | async-done | bytes 786464 | tf_op jit(solution)/shard_map/all_to_all | solution.py:435
  183.2 3.1 fusion.107
  190.0 4.4 all-to-all-start.1
  196.7 2.8 reshape.1090
  199.5 4.0 fusion.103
  205.5 4.2 reshape_transpose_reshape.7
  209.8 2.5 copy.243
  219.5 2.8 fusion.101
  225.9 14.4 %fusion.3 = bf16[512,4,768]{0,2,1:T(8,128)(2,1)S(1)} fusion(f32[512,4,2,768]{0,3,2,1:T(8,128)S(1)} %bitcast.287), kind=kLoop, calls=%fused_computation.8 | loop fusion | flops 103809024 | bytes 15728640 | tf_op jit(solution)/shard_map/convert_element_type | solution.py:493
  246.5 2.7 reshape.1068
  249.3 2.6 copy.202
  251.9 2.6 copy.210
  254.6 3.6 convert_reduce_fusion
  260.0 19.1 %add_convert_fusion = (bf16[512,4,1,768]{0,3,1,2:T(8,128)(2,1)}, f32[512,4,1,768]{0,3,1,2:T(8,128)}, f32[4,768,512]{2,1,0:T(8,128)}) fusion(f32[512,4,2,768]{0,3,2,1:T(8,128)} %bitcast.288, f32[512,4,192]{0,2,1:T(8,128)S(1)} %fusion.26, bf16[4,768,192]{1,0,2:T(4,128)(2,1)S(1)} %copy-done.27), kind=kOutput, calls=%fused_computation.20 | convolution fusion | flops 719192064 | bytes 31064064 | tf_op jit(solution)/shard_map/nbo,bio->nbi/dot_general | solution.py:87
  279.1 8.9 fusion.5
  294.4 3.7 multiply_reduce_fusion.2
  302.3 2.8 multiply_reduce_fusion
  307.8 24.3 %all_to_all.20 = bf16[8,128,384]{2,1,0:T(8,128)(2,1)S(1)} all-to-all(bf16[8,128,384]{2,1,0:T(8,128)(2,1)S(1)} %bitcast.316), channel_id=1, replica_groups=mesh['dp'=4,'seq'=8] {'seq'}, dimensions={0} | all-to-all | bytes 1572864 | tf_op jit(solution)/shard_map/all_to_all | solution.py:435
  337.5 4.3 all-to-all-start.3
  342.0 3.6 convolution_convert_fusion.1
  345.6 2.7 copy.245
  348.3 6.4 convolution_convert_fusion
  354.7 4.7 reshape.1095
  373.1 2.6 constant_dynamic-update-slice_fusion.3
  383.5 3.0 fusion.54
  390.9 130.6 %all-reduce.4.cloned.1.call-done = bf16[64,192,192]{2,1,0:T(8,128)(2,1)} async-done(((bf16[64,192,192]{2,1,0:T(8,128)(2,1)}), bf16[64,192,192]{2,1,0:T(8,128)(2,1)}) %all-reduce.4.cloned.1.call-update) | async-done | bytes 4718608 | tf_op jit(solution)/shard_map/psum | solution.py:536
  521.6 9.1 convert_element_type.282
  530.7 20.2 %gather_fusion.1 = f32[128,192,192]{2,1,0:T(8,128)} fusion(f32[64,192,192]{2,1,0:T(8,128)} %convert_element_type.282, s32[1024]{0:T(1024)S(1)} %pad_clamp_fusion), kind=kCustom, calls=%fused_computation.1 | custom fusion | bytes 37749248 | tf_op jit(solution)/shard_map/jit(_take)/gather | solution.py:538
  550.9 18.9 %select_multiply_fusion = f32[128,192,192]{2,1,0:T(8,128)} fusion(f32[128,192,192]{2,1,0:T(8,128)} %gather_fusion.1, f32[128]{0:T(128)S(1)} %convert_element_type.283, pred[128]{0:T(512)(128)(4,1)S(1)} %compare_and_fusion), kind=kLoop, calls=%fused_computation.2 | loop fusion | flops 9437184 | bytes 37749376 | tf_op jit(solution)/shard_map/mul | solution.py:538
  570.7 2.7 reshape.1075
  573.5 2.6 copy.215
  577.4 4.2 convolution_multiply_fusion
  582.8 40.5 %all-reduce = (f32[5,768]{1,0:T(8,128)}, f32[5,128]{1,0:T(8,128)}) all-reduce(f32[5,768]{1,0:T(8,128)} %stack.12, f32[5,128]{1,0:T(8,128)S(1)} %fusion.110), channel_id=1, replica_groups=mesh['dp'=4,'seq'=8] {'dp','seq'}, use_global_device_ids=true, to_apply=%region_18.19 | all-reduce | flops 4480 | bytes 35840 | tf_op jit(solution)/shard_map/psum | solution.py:546
  626.1 28.8 %all-reduce.6.cloned.1.call-done = f32[128,768]{1,0:T(8,128)} async-done(((f32[128,768]{1,0:T(8,128)}), f32[128,768]{1,0:T(8,128)}) %all-reduce.6.cloned.1.call-update) | async-done | bytes 393232 | tf_op jit(solution)/shard_map/psum | solution.py:546
  654.9 2.7 add_multiply_fusion.2
  659.6 2.7 reshape.1079
  662.3 3.0 copy.222
  665.6 4.2 fusion.28
  669.8 233.6 %reduce-scatter.2.cloned.1.call-done = f32[16,192,192]{2,1,0:T(8,128)} async-done(((f32[128,192,192]{2,1,0:T(8,128)}), f32[16,192,192]{2,1,0:T(8,128)}) %reduce-scatter.2.cloned.1.call-update) | async-done | bytes 2359312 | tf_op jit(solution)/shard_map/reduce_scatter | solution.py:537
  903.4 8.2 add_multiply_fusion
  911.6 3.9 broadcast_multiply_fusion
  (315 shorter events, 92.4 us)
Async XLA Ops:
  7.2 123.0 %all-gather.2.cloned.1.call-start = ((), (), s32[]{:S(2)}) async-start(), calls=%async_computation.5 | async-start | bytes 14155776 | tf_op jit(solution)/shard_map/all_gather | solution.py:413
  11.5 139.1 %copy-start.52 = (bf16[512,4,192]{0,2,1:T(8,128)(2,1)}, bf16[512,4,192]{0,2,1:T(8,128)(2,1)S(1)}, u32[]{:S(2)}) copy-start(bf16[512,4,192]{0,2,1:T(8,128)(2,1)S(1)} %reshape_reshape.10) | copy-start | bytes 2359300
  155.6 61.5 %copy-start.12 = (f32[512,768]{0,1:T(8,128)}, f32[512,768]{0,1:T(8,128)S(1)}, u32[]{:S(2)}) copy-start(f32[512,768]{0,1:T(8,128)S(1)} %get-tuple-element.59) | copy-start | bytes 4718596
  155.8 6.6 copy-start.78
  157.0 9.7 %copy-start.61 = (f32[128,768]{1,0:T(8,128)S(1)}, f32[128,768]{1,0:T(8,128)}, u32[]{:S(2)}) copy-start(f32[128,768]{1,0:T(8,128)} %param.35) | copy-start | bytes 1179652
  158.0 25.2 %all-to-all-start = ((bf16[8,128,384]{2,1,0:T(8,128)(2,1)}), bf16[8,128,384]{2,1,0:T(8,128)(2,1)}, u32[]{:S(2)}, u32[]{:S(2)}) async-start(bf16[8,128,384]{2,1,0:T(8,128)(2,1)} %bitcast.7), calls=%async_computation | async-start | bytes 1572864 | tf_op jit(solution)/shard_map/all_to_all | solution.py:435
  162.3 7.2 copy-start.90
  162.4 5.8 copy-start.103
  162.4 172.3 %copy-start.81 = (pred[512]{0:T(512)(128)(4,1)}, pred[512]{0:T(512)(128)(4,1)S(1)}, u32[]{:S(2)}) copy-start(pred[512]{0:T(512)(128)(4,1)S(1)} %iota_compare_fusion.2) | copy-start | bytes 1540
  162.4 7.0 copy-start.96
  162.5 7.0 copy-start.98
  169.5 17.8 %copy-start.36 = (f32[1024,384]{1,0:T(8,128)}, f32[1024,384]{1,0:T(8,128)S(1)}, u32[]{:S(2)}) copy-start(f32[1024,384]{1,0:T(8,128)S(1)} %fusion.108) | copy-start | bytes 4718596
  189.0 5.5 copy-start.70
  189.0 6.3 copy-start.29
  190.0 25.4 %all-to-all-start.1 = ((bf16[8,128,384]{1,2,0:T(8,128)(2,1)}), bf16[8,128,384]{1,2,0:T(8,128)(2,1)}, u32[]{:S(2)}, u32[]{:S(2)}) async-start(bf16[8,128,384]{1,2,0:T(8,128)(2,1)} %bitcast.286), calls=%async_computation.1 | async-start | bytes 1572864 | tf_op jit(solution)/shard_map/all_to_all | solution.py:439
  195.1 59.4 %copy-start.64 = (f32[768]{0:T(1024)}, f32[768]{0:T(1024)S(1)}, u32[]{:S(2)}) copy-start(f32[768]{0:T(1024)S(1)} %get-tuple-element.25) | copy-start | bytes 9220
  195.1 59.4 %copy-start.66 = (f32[768]{0:T(1024)}, f32[768]{0:T(1024)S(1)}, u32[]{:S(2)}) copy-start(f32[768]{0:T(1024)S(1)} %get-tuple-element.26) | copy-start | bytes 9220
  195.1 59.4 %copy-start.68 = (f32[768]{0:T(1024)}, f32[768]{0:T(1024)S(1)}, u32[]{:S(2)}) copy-start(f32[768]{0:T(1024)S(1)} %get-tuple-element.27) | copy-start | bytes 9220
  222.3 32.2 %copy-start.71 = (f32[4,128]{1,0:T(4,128)}, f32[4,128]{1,0:T(4,128)S(1)}, u32[]{:S(2)}) copy-start(f32[4,128]{1,0:T(4,128)S(1)} %get-tuple-element.78) | copy-start | bytes 6148
  222.6 31.9 %copy-start.75 = (f32[4,128]{1,0:T(4,128)}, f32[4,128]{1,0:T(4,128)S(1)}, u32[]{:S(2)}) copy-start(f32[4,128]{1,0:T(4,128)S(1)} %bitcast_rsqrt_fusion.1) | copy-start | bytes 6148
  223.9 16.3 %copy-start.6 = (bf16[512,4,192]{0,2,1:T(8,128)(2,1)}, bf16[512,4,192]{0,2,1:T(8,128)(2,1)S(1)}, u32[]{:S(2)}) copy-start(bf16[512,4,192]{0,2,1:T(8,128)(2,1)S(1)} %add_convert_fusion.5) | copy-start | bytes 2359300
  225.9 14.4 %copy-start = (f32[4,1536,512]{2,1,0:T(8,128)}, f32[4,1536,512]{2,1,0:T(8,128)S(1)}, u32[]{:S(2)}) copy-start(f32[4,1536,512]{2,1,0:T(8,128)S(1)} %fusion.31) | copy-start | bytes 37748740
  225.9 14.4 %copy-start.26 = (bf16[4,768,192]{1,0,2:T(4,128)(2,1)S(1)}, bf16[4,768,192]{1,0,2:T(4,128)(2,1)}, u32[]{:S(2)}) copy-start(bf16[4,768,192]{1,0,2:T(4,128)(2,1)} %reshape_transpose_reshape.7) | copy-start | bytes 3538948
  242.0 12.6 %copy-start.73 = (f32[4,128]{1,0:T(4,128)}, f32[4,128]{1,0:T(4,128)S(1)}, u32[]{:S(2)}) copy-start(f32[4,128]{1,0:T(4,128)S(1)} %get-tuple-element.80) | copy-start | bytes 6148
  244.9 9.7 %copy-start.76 = (f32[4,128]{1,0:T(4,128)}, f32[4,128]{1,0:T(4,128)S(1)}, u32[]{:S(2)}) copy-start(f32[4,128]{1,0:T(4,128)S(1)} %get-tuple-element.76) | copy-start | bytes 6148
  244.9 9.7 %copy-start.77 = (f32[4,128]{1,0:T(4,128)}, f32[4,128]{1,0:T(4,128)S(1)}, u32[]{:S(2)}) copy-start(f32[4,128]{1,0:T(4,128)S(1)} %get-tuple-element.77) | copy-start | bytes 6148
  260.0 19.1 %copy-start.38 = (f32[512,4,192]{0,2,1:T(8,128)}, f32[512,4,192]{0,2,1:T(8,128)S(1)}, u32[]{:S(2)}) copy-start(f32[512,4,192]{0,2,1:T(8,128)S(1)} %fusion.26) | copy-start | bytes 4718596
  290.9 7.1 copy-start.4
  307.7 24.4 %copy-start.104 = (bf16[1024,1024]{1,0:T(8,128)(2,1)S(1)}, bf16[1024,1024]{1,0:T(8,128)(2,1)}, u32[]{:S(2)}) copy-start(bf16[1024,1024]{1,0:T(8,128)(2,1)} %constant.236.clone) | copy-start | bytes 6291460
  336.5 5.4 copy-start.3
  337.5 25.3 %all-to-all-start.3 = ((bf16[8,128,384]{1,2,0:T(8,128)(2,1)}), bf16[8,128,384]{1,2,0:T(8,128)(2,1)}, u32[]{:S(2)}, u32[]{:S(2)}) async-start(bf16[8,128,384]{1,2,0:T(8,128)(2,1)} %bitcast.313), calls=%async_computation.3 | async-start | bytes 1572864 | tf_op jit(solution)/shard_map/all_to_all | solution.py:439
  341.9 179.7 %all-reduce.4.cloned.1.call-start = ((), (), s32[]{:S(2)}) async-start(), calls=%async_computation.6 | async-start | bytes 12582912 | tf_op jit(solution)/shard_map/psum | solution.py:536
  382.3 272.6 %all-reduce.6.cloned.1.call-start = ((), (), s32[]{:S(2)}) async-start(), calls=%async_computation.8 | async-start | bytes 786432 | tf_op jit(solution)/shard_map/psum | solution.py:546
  390.9 512.5 %reduce-scatter.2.cloned.1.call-start = ((), (), s32[]{:S(2)}) async-start(), calls=%async_computation.7 | async-start | bytes 28311552 | tf_op jit(solution)/shard_map/reduce_scatter | solution.py:537
  576.1 47.2 %copy-start.79 = (f32[5,128]{1,0:T(8,128)S(1)}, f32[5,128]{1,0:T(8,128)}, u32[]{:S(2)}) copy-start(f32[5,128]{1,0:T(8,128)} %param.31) | copy-start | bytes 7684
  576.1 47.2 %copy-start.88 = (f32[5,128]{1,0:T(8,128)S(1)}, f32[5,128]{1,0:T(8,128)}, u32[]{:S(2)}) copy-start(f32[5,128]{1,0:T(8,128)} %param.34) | copy-start | bytes 7684
  576.1 47.2 %copy-start.89 = (f32[5,128]{1,0:T(8,128)S(1)}, f32[5,128]{1,0:T(8,128)}, u32[]{:S(2)}) copy-start(f32[5,128]{1,0:T(8,128)} %param.32) | copy-start | bytes 7684
  581.6 76.0 %copy-start.22 = (bf16[12,192,192]{1,2,0:T(8,128)(2,1)S(1)}, bf16[12,192,192]{1,2,0:T(8,128)(2,1)}, u32[]{:S(2)}) copy-start(bf16[12,192,192]{1,2,0:T(8,128)(2,1)} %copy-done.21) | copy-start | bytes 2654212
  657.6 7.8 copy-start.67
  657.6 7.8 copy-start.69
  657.6 7.8 copy-start.72
  657.6 7.8 copy-start.74
  659.6 5.8 copy-start.83
  659.6 5.8 copy-start.85
  665.6 237.8 %copy-start.95 = (f32[16]{0:T(128)S(1)}, f32[16]{0:T(128)}, u32[]{:S(2)}) copy-start(f32[16]{0:T(128)} %get-tuple-element.49) | copy-start | bytes 196
  903.4 8.2 copy-start.18
  903.4 8.2 copy-start.19
  903.4 8.2 copy-start.94
  (64 other events, 147.3 us)
Sparse Core Ops, SparseCore 0:
  10.7 119.4 all-gather.1
  382.4 139.1 all-reduce.3
  527.5 127.3 all-reduce.5
  657.2 246.1 reduce-scatter.1

commit v2 on v1

--- a/solution.py
+++ b/solution.py
@@ -1,3 +1,4 @@
+import functools
 import math
 
 import jax
@@ -5,11 +6,14 @@
 import ml_dtypes
 import numpy as np
 from jax import lax
+from jax.experimental import pallas as pl
+from jax.experimental.pallas import tpu as pltpu
 from jax.sharding import PartitionSpec as P
 
 D = 768
 FF = 3072
 STEP = 10
+NTILES = 64
 
 
 highest = lax.Precision.HIGHEST
@@ -380,6 +384,371 @@
     )
 
 
+MESH = pl.DeviceIdType.MESH
+VMEM_LIMIT = 56 * 2**20
+
+
+class Links:
+    def __init__(self, send_sem, recv_sem):
+        self.send_sem, self.recv_sem, self.used = send_sem, recv_sem, 0
+        self.dp, self.seq = lax.axis_index("dp"), lax.axis_index("seq")
+        self.deep = lax.axis_size("seq") // 2
+        self.z, self.core = lax.div(self.seq, 2), lax.rem(self.seq, 2)
+        self.partner = (self.dp, self.seq + 1 - 2 * self.core)
+        low, high = lax.rem(self.dp, 2), lax.div(self.dp, 2)
+        across_x = self.dp + 1 - 2 * low
+        across_y = self.dp + 2 - 4 * high
+        self.near = across_x + self.core * (across_y - across_x)
+        self.far = across_y + self.core * (across_x - across_y)
+        self.diagonal = 3 - self.dp
+        self.to_near, self.to_far = (self.near, self.seq), (self.far, self.seq)
+        self.to_left, self.to_right = (self.dp, self.seq - 2), (self.dp, self.seq + 2)
+        self.has_left, self.has_right = self.z > 0, self.z < self.deep - 1
+
+    def meet(self):
+        barrier = pltpu.get_barrier_semaphore()
+        for peer in (self.partner, self.to_near, self.to_far):
+            pl.semaphore_signal(barrier, inc=1, device_id=peer, device_id_type=MESH)
+
+        @pl.when(self.has_left)
+        def _():
+            pl.semaphore_signal(barrier, inc=1, device_id=self.to_left, device_id_type=MESH)
+
+        @pl.when(self.has_right)
+        def _():
+            pl.semaphore_signal(barrier, inc=1, device_id=self.to_right, device_id_type=MESH)
+
+        ends = jnp.where(self.has_left, 1, 0) + jnp.where(self.has_right, 1, 0)
+        pl.semaphore_wait(barrier, 3 + ends)
+
+    def copy(self, source, target, device):
+        at = self.used
+        self.used += 1
+        return pltpu.make_async_remote_copy(
+            src_ref=source,
+            dst_ref=target,
+            send_sem=self.send_sem.at[at],
+            recv_sem=self.recv_sem.at[at],
+            device_id=device,
+            device_id_type=MESH,
+        )
+
+
+def chain_copies(links, buffers, lanes):
+    left_in, right_in, left_out, right_out = buffers
+    rightward = links.copy(right_out.at[:, lanes], left_in.at[:, lanes], links.to_right)
+    leftward = links.copy(left_out.at[:, lanes], right_in.at[:, lanes], links.to_left)
+    return (rightward, leftward)
+
+
+def chain_step(links, buffers, copies, lanes, base):
+    left_in, right_in, left_out, right_out = buffers
+    rightward, leftward = copies
+
+    @pl.when(links.has_left)
+    def _():
+        rightward.wait_recv()
+
+    @pl.when(jnp.logical_not(links.has_left))
+    def _():
+        left_in[:, lanes] = jnp.zeros(base.shape, left_in.dtype)
+
+    from_left = left_in[:, lanes].astype(jnp.float32)
+
+    @pl.when(links.has_right)
+    def _():
+        right_out[:, lanes] = (base + from_left).astype(right_out.dtype)
+        rightward.start()
+        leftward.wait_recv()
+
+    @pl.when(jnp.logical_not(links.has_right))
+    def _():
+        right_in[:, lanes] = jnp.zeros(base.shape, right_in.dtype)
+
+    from_right = right_in[:, lanes].astype(jnp.float32)
+
+    @pl.when(links.has_left)
+    def _():
+        left_out[:, lanes] = (base + from_right).astype(left_out.dtype)
+        leftward.start()
+
+    return base + from_left + from_right
+
+
+def chain_end(links, copies):
+    rightward, leftward = copies
+
+    @pl.when(links.has_right)
+    def _():
+        rightward.wait_send()
+
+    @pl.when(links.has_left)
+    def _():
+        leftward.wait_send()
+
+
+def half_tiles(half):
+    order = []
+    for first, per_block in ((0, 3), (12, 1), (16, 4), (32, 4), (48, 4)):
+        order += range(first + 2 * half * per_block, first + 2 * (half + 1) * per_block)
+    return order
+
+
+def gather_kernel(
+    chunks, owners, master, full, own, got, left_in, right_in, left_out, right_out, send_sem, recv_sem
+):
+    links = Links(send_sem, recv_sem)
+    quarter = full.shape[1] // 4
+    tile_count, side = owners.shape[0], master.shape[2]
+    most = master.shape[0] - 1
+    rows = pl.ds(pl.multiple_of(links.dp * quarter, quarter), quarter)
+    rank, place = jnp.int32(0), []
+    for i in range(tile_count):
+        mine = owners[i] == links.seq
+        place.append((jnp.minimum(rank, most), mine))
+        rank = rank + jnp.where(mine, 1, 0)
+    for half in range(2):
+        order = half_tiles(half)
+        for j in range(0, len(order), 2):
+            pair = []
+            for i in order[j : j + 2]:
+                at, mine = place[i]
+                pair.append(jnp.where(mine, master[at, rows, :], 0.0))
+            own[half, :, j * side : (j + 2) * side] = jnp.concatenate(pair, axis=1).astype(own.dtype)
+    links.meet()
+    buffers = (left_in, right_in, left_out, right_out)
+    swaps = [
+        links.copy(own.at[1 - links.core, :, lanes], got.at[:, lanes], links.partner)
+        for lanes in chunks
+    ]
+    for swap in swaps:
+        swap.start()
+    chains = [chain_copies(links, buffers, lanes) for lanes in chunks]
+    planes = []
+    for swap, chain, lanes in zip(swaps, chains, chunks):
+        swap.wait()
+        base = own[links.core, :, lanes].astype(jnp.float32) + got[:, lanes].astype(jnp.float32)
+        total = chain_step(links, buffers, chain, lanes, base)
+        full[links.core, rows, lanes] = total.astype(full.dtype)
+        mine = full.at[links.core, rows, lanes]
+        other = full.at[
+            links.core, pl.ds(pl.multiple_of(links.near * quarter, quarter), quarter), lanes
+        ]
+        first = links.copy(mine, mine, links.to_near)
+        second = links.copy(mine, mine, links.to_far)
+        relay = links.copy(other, other, links.to_far)
+        share = links.copy(
+            full.at[links.core, :, lanes], full.at[links.core, :, lanes], links.partner
+        )
+        first.start()
+        second.start()
+        planes.append((first, second, relay, share))
+    for first, second, relay, share in planes:
+        first.wait_recv()
+        relay.start()
+    for first, second, relay, share in planes:
+        second.wait_recv()
+        relay.wait_recv()
+        share.start()
+    for chain, (first, second, relay, share) in zip(chains, planes):
+        chain_end(links, chain)
+        first.wait_send()
+        second.wait_send()
+        relay.wait_send()
+        share.wait()
+
+
+def gather_weights(owners, master):
+    slots, side, _ = master.shape
+    width = owners.shape[0] // 2 * side
+    step = side * 2
+    chunks = (pl.ds(0, 3 * step), pl.ds(3 * step, 5 * step), pl.ds(8 * step, 8 * step))
+    low = jnp.bfloat16
+    part = pltpu.VMEM((side // 4, width), low)
+    count = 7 * len(chunks)
+    return pl.pallas_call(
+        functools.partial(gather_kernel, chunks),
+        out_shape=jax.ShapeDtypeStruct((2, side, width), low),
+        in_specs=[
+            pl.BlockSpec(memory_space=pltpu.SMEM),
+            pl.BlockSpec(memory_space=pltpu.VMEM),
+        ],
+        out_specs=pl.BlockSpec(memory_space=pltpu.VMEM),
+        scratch_shapes=[
+            pltpu.VMEM((2, side // 4, width), low),
+            part,
+            part,
+            part,
+            part,
+            part,
+            pltpu.SemaphoreType.DMA((count,)),
+            pltpu.SemaphoreType.DMA((count,)),
+        ],
+        compiler_params=pltpu.CompilerParams(
+            collective_id=0, has_side_effects=True, vmem_limit_bytes=VMEM_LIMIT
+        ),
+        name="gather_weights",
+    )(owners, master)
+
+
+def reduce_kernel(
+    chunks,
+    tile_of_slot,
+    used,
+    grads,
+    spread,
+    mine_sum,
+    got,
+    near_in,
+    far_in,
+    far_out,
+    left_in,
+    right_in,
+    left_out,
+    right_out,
+    total,
+    by_tile,
+    send_sem,
+    recv_sem,
+):
+    links = Links(send_sem, recv_sem)
+    side = grads.shape[1]
+    quarter = side // 4
+    wide = jnp.float32
+
+    def rows_of(index):
+        return pl.ds(pl.multiple_of(index * quarter, quarter), quarter)
+
+    links.meet()
+    buffers = (left_in, right_in, left_out, right_out)
+    swaps = [
+        links.copy(grads.at[1 - links.core, :, lanes], got.at[:, lanes], links.partner)
+        for lanes in chunks
+    ]
+    nears = [
+        (
+            links.copy(mine_sum.at[rows_of(links.near), lanes], near_in.at[0, :, lanes], links.to_near),
+            links.copy(
+                mine_sum.at[rows_of(links.diagonal), lanes], near_in.at[1, :, lanes], links.to_near
+            ),
+        )
+        for lanes in chunks
+    ]
+    fars = [links.copy(far_out.at[:, lanes], far_in.at[:, lanes], links.to_far) for lanes in chunks]
+    chains = [chain_copies(links, buffers, lanes) for lanes in chunks]
+    for swap in swaps:
+        swap.start()
+    for swap, near, lanes in zip(swaps, nears, chunks):
+        swap.wait()
+        mine_sum[:, lanes] = (
+            grads[links.core, :, lanes].astype(wide) + got[:, lanes].astype(wide)
+        ).astype(mine_sum.dtype)
+        near[1].start()
+        near[0].start()
+    for near, far, lanes in zip(nears, fars, chunks):
+        near[1].wait_recv()
+        far_out[:, lanes] = (
+            mine_sum[rows_of(links.far), lanes].astype(wide) + near_in[1, :, lanes].astype(wide)
+        ).astype(far_out.dtype)
+        far.start()
+    shares = []
+    for near, far, chain, lanes in zip(nears, fars, chains, chunks):
+        near[0].wait_recv()
+        far.wait_recv()
+        base = (
+            mine_sum[rows_of(links.dp), lanes].astype(wide)
+            + near_in[0, :, lanes].astype(wide)
+            + far_in[:, lanes].astype(wide)
+        )
+        total[links.core, :, lanes] = chain_step(links, buffers, chain, lanes, base).astype(
+            total.dtype
+        )
+        part = total.at[links.core, :, lanes]
+        share = links.copy(part, part, links.partner)
+        share.start()
+        shares.append(share)
+    for share in shares:
+        share.wait()
+    for half in range(2):
+        for j, i in enumerate(half_tiles(half)):
+            by_tile[i] = total[half, :, j * side : (j + 1) * side].astype(wide)
+    slots = tile_of_slot.shape[0]
+    tiles_wide = slots * side
+    at_home = spread.at[rows_of(links.dp), :]
+    for s in range(0, slots, 2):
+        pair = [
+            jnp.where(used[k] > 0, by_tile[tile_of_slot[k]], 0.0) for k in (s, s + 1)
+        ]
+        spread[rows_of(links.dp), s * side : (s + 2) * side] = jnp.concatenate(pair, axis=1).astype(
+            spread.dtype
+        )
+    first_extra = by_tile.shape[0] // 2 * side
+    extra = total.shape[2] - first_extra
+    for half in range(2):
+        begin = tiles_wide + half * extra
+        spread[rows_of(links.dp), begin : begin + extra] = total[half, :, first_extra:]
+    other = spread.at[rows_of(links.near), :]
+    first = links.copy(at_home, at_home, links.to_near)
+    second = links.copy(at_home, at_home, links.to_far)
+    relay = links.copy(other, other, links.to_far)
+    first.start()
+    second.start()
+    first.wait_recv()
+    relay.start()
+    second.wait_recv()
+    relay.wait()
+    first.wait_send()
+    second.wait_send()
+    for near, far, chain in zip(nears, fars, chains):
+        near[0].wait_send()
+        near[1].wait_send()
+        far.wait_send()
+        chain_end(links, chain)
+
+
+def reduce_grads(tile_of_slot, used, grads):
+    _, side, width = grads.shape
+    slots = tile_of_slot.shape[0]
+    tile_count = NTILES
+    extra = width - tile_count // 2 * side
+    step = side * 2
+    cuts = (0, 6 * step, 11 * step, width)
+    chunks = tuple(pl.ds(a, b - a) for a, b in zip(cuts[:-1], cuts[1:]))
+    low = jnp.bfloat16
+    quarter = side // 4
+    part = pltpu.VMEM((quarter, width), low)
+    count = 7 * len(chunks) + 3
+    return pl.pallas_call(
+        functools.partial(reduce_kernel, chunks),
+        out_shape=jax.ShapeDtypeStruct((side, slots * side + 2 * extra), low),
+        in_specs=[
+            pl.BlockSpec(memory_space=pltpu.SMEM),
+            pl.BlockSpec(memory_space=pltpu.SMEM),
+            pl.BlockSpec(memory_space=pltpu.VMEM),
+        ],
+        out_specs=pl.BlockSpec(memory_space=pltpu.VMEM),
+        scratch_shapes=[
+            pltpu.VMEM((side, width), low),
+            pltpu.VMEM((side, width), low),
+            pltpu.VMEM((2, quarter, width), low),
+            part,
+            part,
+            part,
+            part,
+            part,
+            part,
+            pltpu.VMEM((2, quarter, width), low),
+            pltpu.VMEM((tile_count, quarter, side), jnp.float32),
+            pltpu.SemaphoreType.DMA((count,)),
+            pltpu.SemaphoreType.DMA((count,)),
+        ],
+        compiler_params=pltpu.CompilerParams(
+            collective_id=1, has_side_effects=True, vmem_limit_bytes=VMEM_LIMIT
+        ),
+        name="reduce_grads",
+    )(tile_of_slot, used, grads)
+
+
 def on_device_columns(
     tokens,
     cotangent,
@@ -410,14 +779,19 @@
     hidden_ratio = FF // D
     quarter_hidden = FF // 4
     slot_of_tile, tile_of_slot, slot_used = slot_maps(owners, owner_cap, owner_cap * seq_devices)
-    gathered = lax.all_gather(tile_master.astype(jnp.bfloat16), "seq", axis=0, tiled=True)
-    weights = jnp.take(gathered, slot_of_tile, axis=0)
-    w_in = block_weight(weights[0:12], 1, 3)
-    w_out = block_weight(weights[12:16], 1, 1)
-    w_gate = block_weight(weights[16 : 16 + 4 * hidden_ratio], 1, hidden_ratio)
-    w_up = block_weight(weights[16 + 4 * hidden_ratio : 16 + 8 * hidden_ratio], 1, hidden_ratio)
-    w_down = block_weight(weights[16 + 8 * hidden_ratio : 16 + 12 * hidden_ratio], hidden_ratio, 1)
-    w_gate_up = jnp.concatenate([w_gate, w_up], axis=2)
+    packed = gather_weights(owners, tile_master)
+    side = tile_master.shape[1]
+    lanes = 2 * side
+
+    def blocks_of(first, per_block):
+        part = packed[:, :, first * lanes : (first + per_block) * lanes]
+        part = part.reshape(2, side, 2, per_block * side).transpose(0, 2, 1, 3)
+        return part.reshape(4, side, per_block * side)
+
+    w_in, w_out = blocks_of(0, 3), blocks_of(3, 1)
+    w_gate_up = jnp.concatenate([blocks_of(4, 4), blocks_of(8, 4)], axis=2)
+    w_down = blocks_of(12, 4).reshape(4, side, 4, side).transpose(0, 2, 1, 3)
+    w_down = w_down.reshape(4, 4 * side, side)
     halves = seq_devices // seq_count
     width = model_width // halves
     half_index = lax.rem(seq_index, halves)
@@ -507,10 +881,10 @@
     )
     d_gate_up = d_gate_up.reshape(-1, 2 * FF).astype(jnp.bfloat16)
     gate_up_tiles = block_grad(normed_low, d_gate_up, 1, 2 * hidden_ratio).reshape(
-        4, 2, hidden_ratio, weights.shape[1], weights.shape[2]
-    )
-    g_gate = gate_up_tiles[:, 0].reshape(-1, weights.shape[1], weights.shape[2])
-    g_up = gate_up_tiles[:, 1].reshape(-1, weights.shape[1], weights.shape[2])
+        4, 2, hidden_ratio, side, side
+    )
+    g_gate = gate_up_tiles[:, 0].reshape(-1, side, side)
+    g_up = gate_up_tiles[:, 1].reshape(-1, side, side)
     d_normed = d_second + block_back(d_gate_up, w_gate_up)
     d_first, d_gain_one, d_bias_one = first_pull(d_normed)
     d_branch = d_first.astype(jnp.bfloat16)
@@ -528,22 +902,38 @@
     in_grad = (d_first + block_back(d_qkv, w_in)).reshape(tokens.shape)
     d_taps = invert(*product(back_spec, kv_spec, True))
     g_filter_in, g_filter_half = filter_pull(d_taps)
-    g_filter_out = lax.dynamic_update_slice_in_dim(
-        jnp.zeros_like(filter_out), g_filter_half, half_index * width, 1
-    )
-    tile_grads = jnp.concatenate([g_in, g_out, g_gate, g_up, g_down], axis=0)
+    def pack(tiles):
+        per_half = tiles.shape[0] // 2
+        return tiles.reshape(2, per_half, side, side).transpose(0, 2, 1, 3).reshape(2, side, -1)
+
     slot_mask = slot_used.astype(jnp.float32)[:, None, None]
-    summed = lax.psum(tile_grads.astype(jnp.bfloat16), "dp").astype(jnp.float32)
-    owned = lax.psum_scatter(
-        jnp.take(summed, tile_of_slot, axis=0) * slot_mask, "seq", scatter_dimension=0, tiled=True
-    )
+    first_slot = seq_index * owner_cap
+    vector_part = jnp.stack([d_gain_one, d_bias_one, d_gain_two, d_bias_two, d_skip])
+    order = filter_in.shape[1]
+    both = jnp.zeros((2, side, width), jnp.float32)
+    both = lax.dynamic_update_slice(both, g_filter_half[None], (half_index, 0, 0))
+    both = lax.dynamic_update_slice(
+        both, vector_part.reshape(5, 2, width).transpose(1, 0, 2), (0, order, 0)
+    )
+    both = lax.dynamic_update_slice(both, g_filter_in[None], (0, order + 8, 0))
+    packed_grads = jnp.concatenate(
+        [pack(g).astype(jnp.bfloat16) for g in (g_in, g_out, g_gate, g_up, g_down, )]
+        + [both.astype(jnp.bfloat16)],
+        axis=2,
+    )
+    own_tile = lax.dynamic_slice_in_dim(tile_of_slot, first_slot, owner_cap, 0)
+    own_used = lax.dynamic_slice_in_dim(slot_used.astype(jnp.int32), first_slot, owner_cap, 0)
+    reduced = reduce_grads(own_tile, own_used, packed_grads).astype(jnp.float32)
+    owned = reduced[:, : owner_cap * side].reshape(side, owner_cap, side).transpose(1, 0, 2)
+    extra = reduced[:, owner_cap * side :].reshape(side, 2, width).transpose(1, 0, 2)
+    out_sum = extra[:, :order].transpose(1, 0, 2).reshape(order, model_width)
+    vector_sum = extra[:, order : order + 5].transpose(1, 0, 2).reshape(5, model_width)
+    in_sum = extra[0, order + 8 : order + 13, :order]
     tokens_all = seq_count * dev_rows * row_len * lax.axis_size("dp") * seq_devices
     grad_scale = 1.0 / math.sqrt(tokens_all)
     mine_mask = lax.dynamic_slice_in_dim(slot_mask, seq_index * owner_cap, owner_cap, 0)
     tile_grad = owned * grad_scale
     tile_new = adam_step(tile_master, tile_moment, tile_second, tile_average, tile_grad, 0.1, 0.01)
-    vector_part = jnp.stack([d_gain_one, d_bias_one, d_gain_two, d_bias_two, d_skip])
-    vector_sum, in_sum, out_sum = lax.psum((vector_part, g_filter_in, g_filter_out), ("dp", "seq"))
     vector_grad = vector_sum * grad_scale
     in_grad_filter = in_sum * grad_scale
     out_grad_filter = out_sum * grad_scale
@@ -578,6 +968,7 @@
     seq_count, dev_rows, row_len, model_width = arrays[0].shape
     seq_devices = lax.axis_size("seq")
     fits = dev_rows == 1 and seq_devices % seq_count == 0 and seq_devices * row_len <= 2048
+    fits = fits and lax.axis_size("dp") == 4 and seq_devices == 2 * seq_count == 8
     if fits and model_width % (128 * (seq_devices // seq_count)) == 0:
         return on_device_columns(*arrays)
     return on_device_general(*arrays)

time: 932 us -> 572 us (0.61)
  waiting for transfers between devices: 527 us -> 14.3 us
  Pallas kernels: 0 us -> 245 us
  blocking collectives: 64.8 us -> 0 us
  other arithmetic: 101 us -> 79.8 us
  between operations: 15.5 us -> 2.61 us
    pallas_call x0 -> x2, Pallas kernels: none -> 245 us  [the longest x1 134 us: reduce_grads(): pl.pallas_call(functools.partial(reduce_kernel, chunks), out_shape=jax.Sh...]
    reduce_scatter x1 -> x0, waiting for transfers between devices: 234 us -> none  [on_device_columns(): lax.psum_scatter(jnp.take(summed, tile_of_slot, axis=0) * slot_mask, 'seq...]
    psum x2 -> x0, waiting for transfers between devices: 159 us -> none  [the longest x1 131 us: on_device_columns(): summed = lax.psum(tile_grads.astype(jnp.bfloat16), 'dp').astype(jnp.float32)]
    all_gather x1 -> x0, waiting for transfers between devices: 118 us -> none  [on_device_columns(): lax.all_gather(tile_master.astype(jnp.bfloat16), 'seq', axis=0, tiled=True)]
    psum x1 -> x0, blocking collectives: 40.5 us -> none  [on_device_columns(): lax.psum((vector_part, g_filter_in, g_filter_out), ('dp', 'seq'))]
    gather x3 -> x0, local copies, waits for them, and re-layouts: 37.1 us -> none  [the longest x1 20.2 us: on_device_columns(): jnp.take(summed, tile_of_slot, axis=0) * slot_mask]
    all_to_all x1 -> x0, blocking collectives: 24.3 us -> none  [spread(): return lax.all_to_all(cells, 'seq', 0, 0, tiled=True).reshape(length, width)]
    convert_element_type x0 -> x13, local copies, waits for them, and re-layouts: none -> 20.1 us  [on_device_columns(): pack(g).astype(jnp.bfloat16)]
  transfers between devices with their start and end apart: 7 -> 4, of which waited for: 7 -> 2; matrix products, arithmetic and copies ran while one was open for 14% -> 16% of each run, Pallas kernels for 0% -> 0%
where the time goes in v2:
time: 572 us; the launch traced here: 566 us
  Pallas kernels  245 us (43%)
  local copies, waits for them, and re-layouts  136 us (24%)
  other arithmetic  79.8 us (14%)
  matrix products  69.6 us (12%)
  starting transfers between devices  18.9 us (3%)
  waiting for transfers between devices  14.3 us (2%)
    pallas_call x1, Pallas kernels, reduce_grads(): pl.pallas_call(functools.partial(reduce_kernel, chunks), out_shape=jax.Sh...  134 us
    pallas_call x1, Pallas kernels, gather_weights(): pl.pallas_call(functools.partial(gather_kernel, chunks), out_shape=jax.Sh...  111 us
    dot_general x4, matrix products, block_back(): jnp.einsum('nbo,bio->nbi', row_view, blocks, preferred_element_type=jnp.f...  25.3 us
    unnamed x260, local copies, waits for them, and re-layouts  23.9 us
    convert_element_type x13, local copies, waits for them, and re-layouts, on_device_columns(): pack(g).astype(jnp.bfloat16)  20.1 us
    convert_element_type x1, other arithmetic, on_device_columns(): active_low = active.astype(jnp.bfloat16)  14.4 us
    mul x2, other arithmetic, on_device_columns(): tile_new[2] * mine_mask  13.6 us
    another operation x4, other arithmetic  12.8 us
  transfers between devices with their start and end apart: 4, of which 2 were waited for; matrix products, arithmetic and copies ran while one was open for 16% of the time, Pallas kernels for 0%

profile of v2, /device:TPU:0, one launch (start us, length us, event | category | flops | bytes accessed | tf_op | source)
XLA Modules:
  0.0 565.8 jit_solution(1086031936707107037)
XLA Ops:
  2.5 110.7 %gather_weights.1 = bf16[2,192,6144]{2,1,0:T(8,128)(2,1)} custom-call(s32[64]{0:T(128)} %owners.1, f32[16,192,192]{2,1,0:T(8,128)} %master.1), custom_call_target="tpu_custom_call" | custom-call | tf_op jit(solution)/shard_map/gather_weights/pallas_call | solution.py:569
  124.3 4.1 all-to-all-start
  133.1 4.2 fusion.120
  140.3 2.4 fusion.123
  142.7 6.6 %all-to-all-done = bf16[8,128,384]{2,1,0:T(8,128)(2,1)S(1)} async-done(((bf16[8,128,384]{2,1,0:T(8,128)(2,1)}), bf16[8,128,384]{2,1,0:T(8,128)(2,1)S(1)}, u32[]{:S(2)}, u32[]{:S(2)}) %all-to-all-start) | async-done | bytes 786464 | tf_op jit(solution)/shard_map/all_to_all | solution.py:809
  149.3 3.0 fusion.122
  156.0 4.4 all-to-all-start.1
  165.0 2.9 reshape.1108
  169.0 4.4 reshape_reshape.15
  173.4 4.3 copy.232
  177.7 4.0 reshape.1092
  189.4 2.2 multiply_convert_fusion.2
  197.2 14.4 %fusion.3 = bf16[512,4,768]{0,2,1:T(8,128)(2,1)S(1)} fusion(f32[512,4,2,768]{0,3,2,1:T(8,128)S(1)} %bitcast.382), kind=kLoop, calls=%fused_computation.5 | loop fusion | flops 103809024 | bytes 15728640 | tf_op jit(solution)/shard_map/convert_element_type | solution.py:867
  217.2 2.8 reshape.1090
  220.0 2.6 copy.230
  222.6 2.8 copy.236
  225.5 3.5 convert_reduce_fusion
  230.9 19.4 %add_convert_fusion = (bf16[512,4,1,768]{0,3,1,2:T(8,128)(2,1)}, f32[512,4,1,768]{0,3,1,2:T(8,128)}, f32[4,768,512]{2,1,0:T(8,128)}) fusion(f32[512,4,2,768]{0,3,2,1:T(8,128)} %bitcast.383, bf16[4,768,192]{1,2,0:T(8,128)(2,1)S(1)} %copy-done.27, f32[512,4,192]{0,2,1:T(8,128)S(1)} %fusion.32), kind=kOutput, calls=%fused_computation.17 | convolution fusion | flops 719192064 | bytes 31064064 | tf_op jit(solution)/shard_map/nbo,bio->nbi/dot_general | solution.py:91
  250.3 8.9 %fusion.5 = bf16[512,4,1,768]{0,3,1,2:T(8,128)(2,1)S(1)} fusion(f32[4,768,512]{2,1,0:T(8,128)} %get-tuple-element.105, f32[512,4,1,768]{0,3,1,2:T(8,128)} %get-tuple-element.51, f32[512,4,2,768]{0,3,2,1:T(8,128)} %bitcast.384), kind=kLoop, calls=%fused_computation.11 | loop fusion | flops 6291456 | bytes 22020096 | tf_op jit(solution)/shard_map/convert.19
  259.2 2.5 pad_maximum_fusion
  265.5 3.6 multiply_reduce_fusion.2
  272.6 3.4 multiply_reduce_fusion
  278.3 3.4 copy.275
  283.9 5.3 all-to-all-start.2
  289.2 3.6 convolution_convert_fusion.1
  297.1 3.1 copy.256
  300.2 3.9 convert_element_type.354
  308.0 6.4 %convolution_convert_fusion = bf16[4,192,1536]{2,1,0:T(8,128)(2,1)} fusion(bf16[512,4,192]{0,2,1:T(8,128)(2,1)S(1)} %copy-done.6, bf16[512,4,1536]{0,2,1:T(8,128)(2,1)} %bitcast.390), kind=kOutput, calls=%fused_computation.45 | convolution fusion | flops 1209139200 | bytes 9437184 | tf_op jit(solution)/shard_map/nbi,nbo->bio/dot_general | solution.py:99
  314.3 4.7 reshape.1113
  321.0 2.2 convert_element_type.350
  324.1 2.2 convert_element_type.347
  330.4 3.2 fusion.124
  337.3 5.1 all-to-all-start.3
  342.4 2.9 fusion.58
  348.7 3.9 convolution_multiply_fusion
  353.0 2.7 dynamic_update_slice.11
  355.6 7.7 %all-to-all-done.3 = bf16[8,128,384]{1,2,0:T(8,128)(2,1)S(1)} async-done(((bf16[8,128,384]{1,2,0:T(8,128)(2,1)}), bf16[8,128,384]{1,2,0:T(8,128)(2,1)S(1)}, u32[]{:S(2)}, u32[]{:S(2)}) %all-to-all-start.3) | async-done | bytes 786464 | tf_op jit(solution)/shard_map/all_to_all | solution.py:813
  364.0 2.3 multiply_convert_fusion.1
  377.8 133.8 %reduce_grads.1 = bf16[192,3840]{1,0:T(8,128)(2,1)} custom-call(s32[16]{0:T(128)} %dynamic_slice.13.tile_of_slot, s32[16]{0:T(128)} %dynamic_slice.14.used, bf16[2,192,6528]{2,1,0:T(8,128)(2,1)} %copy-done.35), custom_call_target="tpu_custom_call" | custom-call | tf_op jit(solution)/shard_map/reduce_grads/pallas_call | solution.py:721
  514.7 2.7 reshape.1101
  517.5 2.6 copy.245
  524.3 3.3 slice_multiply_fusion.2
  527.6 4.1 mul.988
  531.7 3.1 mul.994
  534.8 4.1 mul.1003
  540.3 13.0 %add_multiply_fusion = (f32[16,192,192]{2,1,0:T(8,128)}, f32[16,192,192]{2,1,0:T(8,128)S(1)}, f32[16,192,192]{2,1,0:T(8,128)S(1)}) fusion(f32[16,192,192]{2,1,0:T(8,128)} %param.26, f32[16]{0:T(128)S(1)} %copy-done.117, f32[16,192,192]{2,1,0:T(8,128)} %master.1, f32[192,16,192]{2,1,0:T(8,128)S(1)} %mul.994, f32[16,192,192]{2,1,0:T(8,128)} %param.25, ...), kind=kLoop, calls=%fused_computation.55 | loop fusion | flops 8847360 | bytes 23593024 | tf_op jit(solution)/shard_map/mul | solution.py:951
  553.5 5.9 %broadcast_multiply_fusion = (f32[16,192,192]{2,1,0:T(8,128)}, f32[16,192,192]{2,1,0:T(8,128)}) fusion(f32[16,192,192]{2,1,0:T(8,128)S(1)} %get-tuple-element.41, f32[16]{0:T(128)S(1)} %copy-done.116, f32[16,192,192]{2,1,0:T(8,128)S(1)} %get-tuple-element.42, f32[192,16,192]{2,1,0:T(8,128)S(1)} %mul.994, f32[16,192,192]{2,1,0:T(8,128)S(1)} %copy-done.19), kind=kLoop, calls=%fused_computation.77 | loop fusion | flops 2949120 | bytes 14155840 | tf_op jit(solution)/shard_map/mul | solution.py:950
  559.7 3.9 fusion.34
  (372 shorter events, 107.1 us)
Async XLA Ops:
  2.5 189.2 %copy-start.28 = (bf16[512,4,192]{0,2,1:T(8,128)(2,1)}, bf16[512,4,192]{0,2,1:T(8,128)(2,1)S(1)}, u32[]{:S(2)}) copy-start(bf16[512,4,192]{0,2,1:T(8,128)(2,1)S(1)} %reshape_reshape.14) | copy-start | bytes 2359300
  118.2 71.2 %copy-start.17 = (f32[512,768]{0,1:T(8,128)}, f32[512,768]{0,1:T(8,128)S(1)}, u32[]{:S(2)}) copy-start(f32[512,768]{0,1:T(8,128)S(1)} %get-tuple-element.55) | copy-start | bytes 4718596
  120.3 8.1 %copy-start.122 = (s32[64]{0:T(128)S(1)}, s32[64]{0:T(128)}, u32[]{:S(2)}) copy-start(s32[64]{0:T(128)} %owners.1) | copy-start | bytes 772
  124.3 8.8 %copy-start.102 = (f32[5,128]{1,0:T(8,128)S(1)}, f32[5,128]{1,0:T(8,128)}, u32[]{:S(2)}) copy-start(f32[5,128]{1,0:T(8,128)} %param.31) | copy-start | bytes 7684
  124.3 25.0 %all-to-all-start = ((bf16[8,128,384]{2,1,0:T(8,128)(2,1)}), bf16[8,128,384]{2,1,0:T(8,128)(2,1)S(1)}, u32[]{:S(2)}, u32[]{:S(2)}) async-start(bf16[8,128,384]{2,1,0:T(8,128)(2,1)} %bitcast.6), calls=%async_computation | async-start | bytes 1572864 | tf_op jit(solution)/shard_map/all_to_all | solution.py:809
  128.4 9.7 %copy-start.67 = (f32[128,768]{1,0:T(8,128)S(1)}, f32[128,768]{1,0:T(8,128)}, u32[]{:S(2)}) copy-start(f32[128,768]{1,0:T(8,128)} %param.35) | copy-start | bytes 1179652
  133.0 7.2 %copy-start.124 = (bf16[1024,1024]{1,0:T(8,128)(2,1)S(1)}, bf16[1024,1024]{1,0:T(8,128)(2,1)}, u32[]{:S(2)}) copy-start(bf16[1024,1024]{1,0:T(8,128)(2,1)} %constant.65.clone) | copy-start | bytes 6291460
  133.1 20.1 %copy-start.104 = (pred[512]{0:T(512)(128)(4,1)}, pred[512]{0:T(512)(128)(4,1)S(1)}, u32[]{:S(2)}) copy-start(pred[512]{0:T(512)(128)(4,1)S(1)} %iota_compare_fusion.2) | copy-start | bytes 1540
  154.9 6.6 %copy-start.83 = (f32[5,768]{1,0:T(8,128)S(1)}, f32[5,768]{1,0:T(8,128)}, u32[]{:S(2)}) copy-start(f32[5,768]{1,0:T(8,128)} %param.27) | copy-start | bytes 46084
  154.9 8.6 %copy-start.33 = (bf16[4,1,128,768]{3,2,1,0:T(8,128)(2,1)S(1)}, bf16[4,1,128,768]{3,2,1,0:T(8,128)(2,1)}, u32[]{:S(2)}) copy-start(bf16[4,1,128,768]{3,2,1,0:T(8,128)(2,1)} %param.21) | copy-start | bytes 2359300
  156.0 31.6 %all-to-all-start.1 = ((bf16[8,128,384]{1,2,0:T(8,128)(2,1)}), bf16[8,128,384]{1,2,0:T(8,128)(2,1)}, u32[]{:S(2)}, u32[]{:S(2)}) async-start(bf16[8,128,384]{1,2,0:T(8,128)(2,1)} %bitcast.417), calls=%async_computation.1 | async-start | bytes 1572864 | tf_op jit(solution)/shard_map/all_to_all | solution.py:813
  193.4 32.0 %copy-start.91 = (f32[4,128]{1,0:T(4,128)}, f32[4,128]{1,0:T(4,128)S(1)}, u32[]{:S(2)}) copy-start(f32[4,128]{1,0:T(4,128)S(1)} %get-tuple-element.86) | copy-start | bytes 6148
  193.6 75.5 %copy-start.85 = (f32[512]{0:T(512)}, f32[512]{0:T(512)S(1)}, u32[]{:S(2)}) copy-start(f32[512]{0:T(512)S(1)} %multiply_reduce_fusion.6) | copy-start | bytes 6148
  193.6 31.8 %copy-start.95 = (f32[4,128]{1,0:T(4,128)}, f32[4,128]{1,0:T(4,128)S(1)}, u32[]{:S(2)}) copy-start(f32[4,128]{1,0:T(4,128)S(1)} %bitcast_rsqrt_fusion.1) | copy-start | bytes 6148
  194.0 17.6 %copy-start.5 = (bf16[512,4,192]{0,2,1:T(8,128)(2,1)}, bf16[512,4,192]{0,2,1:T(8,128)(2,1)S(1)}, u32[]{:S(2)}) copy-start(bf16[512,4,192]{0,2,1:T(8,128)(2,1)S(1)} %add_convert_fusion.5) | copy-start | bytes 2359300
  197.1 14.4 %copy-start = (f32[4,1536,512]{2,1,0:T(8,128)}, f32[4,1536,512]{2,1,0:T(8,128)S(1)}, u32[]{:S(2)}) copy-start(f32[4,1536,512]{2,1,0:T(8,128)S(1)} %fusion.37) | copy-start | bytes 37748740
  197.2 14.4 %copy-start.26 = (bf16[4,768,192]{1,2,0:T(8,128)(2,1)S(1)}, bf16[4,768,192]{1,2,0:T(8,128)(2,1)}, u32[]{:S(2)}) copy-start(bf16[4,768,192]{1,2,0:T(8,128)(2,1)} %reshape.1092) | copy-start | bytes 3538948
  213.2 12.2 %copy-start.93 = (f32[4,128]{1,0:T(4,128)}, f32[4,128]{1,0:T(4,128)S(1)}, u32[]{:S(2)}) copy-start(f32[4,128]{1,0:T(4,128)S(1)} %get-tuple-element.88) | copy-start | bytes 6148
  215.6 9.8 %copy-start.97 = (f32[4,128]{1,0:T(4,128)}, f32[4,128]{1,0:T(4,128)S(1)}, u32[]{:S(2)}) copy-start(f32[4,128]{1,0:T(4,128)S(1)} %get-tuple-element.84) | copy-start | bytes 6148
  215.6 9.8 %copy-start.99 = (f32[4,128]{1,0:T(4,128)}, f32[4,128]{1,0:T(4,128)S(1)}, u32[]{:S(2)}) copy-start(f32[4,128]{1,0:T(4,128)S(1)} %get-tuple-element.85) | copy-start | bytes 6148
  230.9 19.4 %copy-start.39 = (f32[512,4,192]{0,2,1:T(8,128)}, f32[512,4,192]{0,2,1:T(8,128)S(1)}, u32[]{:S(2)}) copy-start(f32[512,4,192]{0,2,1:T(8,128)S(1)} %fusion.32) | copy-start | bytes 4718596
  262.1 7.1 %copy-start.4 = (bf16[512,4,2,768]{0,3,2,1:T(8,128)(2,1)}, bf16[512,4,2,768]{0,3,2,1:T(8,128)(2,1)S(1)}, u32[]{:S(2)}) copy-start(bf16[512,4,2,768]{0,3,2,1:T(8,128)(2,1)S(1)} %copy.238) | copy-start | bytes 18874372
  278.3 10.9 %copy-start.3 = (bf16[512,4,768]{0,2,1:T(8,128)(2,1)S(1)}, bf16[512,4,768]{0,2,1:T(8,128)(2,1)}, u32[]{:S(2)}) copy-start(bf16[512,4,768]{0,2,1:T(8,128)(2,1)} %copy-done.2) | copy-start | bytes 9437188
  283.9 46.4 %all-to-all-start.2 = ((bf16[8,128,384]{2,1,0:T(8,128)(2,1)}), bf16[8,128,384]{2,1,0:T(8,128)(2,1)}, u32[]{:S(2)}, u32[]{:S(2)}) async-start(bf16[8,128,384]{2,1,0:T(8,128)(2,1)} %bitcast.416), calls=%async_computation.2 | async-start | bytes 1572864 | tf_op jit(solution)/shard_map/all_to_all | solution.py:809
  337.3 26.1 %all-to-all-start.3 = ((bf16[8,128,384]{1,2,0:T(8,128)(2,1)}), bf16[8,128,384]{1,2,0:T(8,128)(2,1)S(1)}, u32[]{:S(2)}, u32[]{:S(2)}) async-start(bf16[8,128,384]{1,2,0:T(8,128)(2,1)} %bitcast.378), calls=%async_computation.3 | async-start | bytes 1572864 | tf_op jit(solution)/shard_map/all_to_all | solution.py:813
  346.5 6.1 %copy-start.72 = (f32[1024,5]{0,1:T(8,128)S(1)}, f32[1024,5]{0,1:T(8,128)}, u32[]{:S(2)}) copy-start(f32[1024,5]{0,1:T(8,128)} %stack.30) | copy-start | bytes 61444
  352.6 11.3 %copy-start.12 = (f32[512,768]{0,1:T(8,128)S(1)}, f32[512,768]{0,1:T(8,128)}, u32[]{:S(2)}) copy-start(f32[512,768]{0,1:T(8,128)} %copy-done.11) | copy-start | bytes 4718596
  513.6 50.0 %copy-start.73 = (f32[2,5,384]{2,1,0:T(8,128)}, f32[2,5,384]{2,1,0:T(8,128)S(1)}, u32[]{:S(2)}) copy-start(f32[2,5,384]{2,1,0:T(8,128)S(1)} %get-tuple-element.79) | copy-start | bytes 46084
  534.8 5.5 copy-start.117
  540.3 13.0 %copy-start.19 = (f32[16,192,192]{2,1,0:T(8,128)S(1)}, f32[16,192,192]{2,1,0:T(8,128)}, u32[]{:S(2)}) copy-start(f32[16,192,192]{2,1,0:T(8,128)} %param.25) | copy-start | bytes 7077892
  540.3 13.0 %copy-start.116 = (f32[16]{0:T(128)S(1)}, f32[16]{0:T(128)}, u32[]{:S(2)}) copy-start(f32[16]{0:T(128)} %get-tuple-element.44) | copy-start | bytes 196
  553.3 6.1 %copy-start.20 = (f32[16,192,192]{2,1,0:T(8,128)}, f32[16,192,192]{2,1,0:T(8,128)S(1)}, u32[]{:S(2)}) copy-start(f32[16,192,192]{2,1,0:T(8,128)S(1)} %get-tuple-element.42) | copy-start | bytes 7077892
  553.3 6.1 %copy-start.7 = (f32[4,1,128,768]{3,2,1,0:T(8,128)S(1)}, f32[4,1,128,768]{3,2,1,0:T(8,128)}, u32[]{:S(2)}) copy-start(f32[4,1,128,768]{3,2,1,0:T(8,128)} %copy.230) | copy-start | bytes 4718596
  553.3 6.1 %copy-start.8 = (f32[4,1,128,768]{3,2,1,0:T(8,128)S(1)}, f32[4,1,128,768]{3,2,1,0:T(8,128)}, u32[]{:S(2)}) copy-start(f32[4,1,128,768]{3,2,1,0:T(8,128)} %copy.236) | copy-start | bytes 4718596
  553.3 6.1 %copy-start.32 = (bf16[4,1,128,768]{3,2,1,0:T(8,128)(2,1)S(1)}, bf16[4,1,128,768]{3,2,1,0:T(8,128)(2,1)}, u32[]{:S(2)}) copy-start(bf16[4,1,128,768]{3,2,1,0:T(8,128)(2,1)} %param.20) | copy-start | bytes 2359300
  553.3 6.1 %copy-start.34 = (bf16[4,1,128,768]{3,2,1,0:T(8,128)(2,1)S(1)}, bf16[4,1,128,768]{3,2,1,0:T(8,128)(2,1)}, u32[]{:S(2)}) copy-start(bf16[4,1,128,768]{3,2,1,0:T(8,128)(2,1)} %param.21) | copy-start | bytes 2359300
  553.3 6.1 %copy-start.36 = (f32[4,1,128,768]{3,2,1,0:T(8,128)S(1)}, f32[4,1,128,768]{3,2,1,0:T(8,128)}, u32[]{:S(2)}) copy-start(f32[4,1,128,768]{3,2,1,0:T(8,128)} %copy.240) | copy-start | bytes 4718596
  553.3 6.1 %copy-start.76 = (f32[768]{0:T(1024)S(1)}, f32[768]{0:T(1024)}, u32[]{:S(2)}) copy-start(f32[768]{0:T(1024)} %copy-done.74) | copy-start | bytes 9220
  553.4 6.1 %copy-start.79 = (f32[768]{0:T(1024)S(1)}, f32[768]{0:T(1024)}, u32[]{:S(2)}) copy-start(f32[768]{0:T(1024)} %copy-done.77) | copy-start | bytes 9220
  553.4 6.1 %copy-start.82 = (f32[768]{0:T(1024)S(1)}, f32[768]{0:T(1024)}, u32[]{:S(2)}) copy-start(f32[768]{0:T(1024)} %copy-done.80) | copy-start | bytes 9220
  553.4 6.1 %copy-start.92 = (f32[4,128]{1,0:T(4,128)S(1)}, f32[4,128]{1,0:T(4,128)}, u32[]{:S(2)}) copy-start(f32[4,128]{1,0:T(4,128)} %copy-done.91) | copy-start | bytes 6148
  553.4 6.1 %copy-start.94 = (f32[4,128]{1,0:T(4,128)S(1)}, f32[4,128]{1,0:T(4,128)}, u32[]{:S(2)}) copy-start(f32[4,128]{1,0:T(4,128)} %copy-done.93) | copy-start | bytes 6148
  553.4 6.1 %copy-start.96 = (f32[4,128]{1,0:T(4,128)S(1)}, f32[4,128]{1,0:T(4,128)}, u32[]{:S(2)}) copy-start(f32[4,128]{1,0:T(4,128)} %copy-done.95) | copy-start | bytes 6148
  553.4 6.1 %copy-start.98 = (f32[4,128]{1,0:T(4,128)S(1)}, f32[4,128]{1,0:T(4,128)}, u32[]{:S(2)}) copy-start(f32[4,128]{1,0:T(4,128)} %copy-done.97) | copy-start | bytes 6148
  553.4 6.1 %copy-start.100 = (f32[4,128]{1,0:T(4,128)S(1)}, f32[4,128]{1,0:T(4,128)}, u32[]{:S(2)}) copy-start(f32[4,128]{1,0:T(4,128)} %copy-done.99) | copy-start | bytes 6148
  553.4 6.1 %copy-start.101 = (f32[768]{0:T(1024)S(1)}, f32[768]{0:T(1024)}, u32[]{:S(2)}) copy-start(f32[768]{0:T(1024)} %get-tuple-element.29) | copy-start | bytes 9220
  553.4 6.1 %copy-start.108 = (f32[4,128]{1,0:T(4,128)S(1)}, f32[4,128]{1,0:T(4,128)}, u32[]{:S(2)}) copy-start(f32[4,128]{1,0:T(4,128)} %get-tuple-element.80) | copy-start | bytes 6148
  553.5 6.1 %copy-start.109 = (f32[4,128]{1,0:T(4,128)S(1)}, f32[4,128]{1,0:T(4,128)}, u32[]{:S(2)}) copy-start(f32[4,128]{1,0:T(4,128)} %get-tuple-element.82) | copy-start | bytes 6148
  (84 other events, 217.8 us)

commit v3 on v2

--- a/solution.py
+++ b/solution.py
@@ -402,24 +402,22 @@
         self.far = across_y + self.core * (across_x - across_y)
         self.diagonal = 3 - self.dp
         self.to_near, self.to_far = (self.near, self.seq), (self.far, self.seq)
-        self.to_left, self.to_right = (self.dp, self.seq - 2), (self.dp, self.seq + 2)
-        self.has_left, self.has_right = self.z > 0, self.z < self.deep - 1
+        self.outer = lax.div(self.z, self.deep // 2)
+        self.inner = 1 - self.outer
+        self.to_inner = (self.dp, self.seq + 2 - 4 * self.outer)
+        self.to_outer = (self.dp, self.seq - 2 + 4 * self.outer)
+        self.at_end = (self.z == 0) | (self.z == self.deep - 1)
 
     def meet(self):
         barrier = pltpu.get_barrier_semaphore()
-        for peer in (self.partner, self.to_near, self.to_far):
+        for peer in (self.partner, self.to_near, self.to_far, self.to_inner):
             pl.semaphore_signal(barrier, inc=1, device_id=peer, device_id_type=MESH)
 
-        @pl.when(self.has_left)
+        @pl.when(jnp.logical_not(self.at_end))
         def _():
-            pl.semaphore_signal(barrier, inc=1, device_id=self.to_left, device_id_type=MESH)
-
-        @pl.when(self.has_right)
-        def _():
-            pl.semaphore_signal(barrier, inc=1, device_id=self.to_right, device_id_type=MESH)
-
-        ends = jnp.where(self.has_left, 1, 0) + jnp.where(self.has_right, 1, 0)
-        pl.semaphore_wait(barrier, 3 + ends)
+            pl.semaphore_signal(barrier, inc=1, device_id=self.to_outer, device_id_type=MESH)
+
+        pl.semaphore_wait(barrier, jnp.where(self.at_end, 4, 5))
 
     def copy(self, source, target, device):
         at = self.used
@@ -434,57 +432,79 @@
         )
 
 
-def chain_copies(links, buffers, lanes):
-    left_in, right_in, left_out, right_out = buffers
-    rightward = links.copy(right_out.at[:, lanes], left_in.at[:, lanes], links.to_right)
-    leftward = links.copy(left_out.at[:, lanes], right_in.at[:, lanes], links.to_left)
-    return (rightward, leftward)
-
-
-def chain_step(links, buffers, copies, lanes, base):
-    left_in, right_in, left_out, right_out = buffers
-    rightward, leftward = copies
-
-    @pl.when(links.has_left)
-    def _():
-        rightward.wait_recv()
-
-    @pl.when(jnp.logical_not(links.has_left))
-    def _():
-        left_in[:, lanes] = jnp.zeros(base.shape, left_in.dtype)
-
-    from_left = left_in[:, lanes].astype(jnp.float32)
-
-    @pl.when(links.has_right)
-    def _():
-        right_out[:, lanes] = (base + from_left).astype(right_out.dtype)
-        rightward.start()
-        leftward.wait_recv()
-
-    @pl.when(jnp.logical_not(links.has_right))
-    def _():
-        right_in[:, lanes] = jnp.zeros(base.shape, right_in.dtype)
-
-    from_right = right_in[:, lanes].astype(jnp.float32)
-
-    @pl.when(links.has_left)
-    def _():
-        left_out[:, lanes] = (base + from_right).astype(left_out.dtype)
-        leftward.start()
-
-    return base + from_left + from_right
-
-
-def chain_end(links, copies):
-    rightward, leftward = copies
-
-    @pl.when(links.has_right)
-    def _():
-        rightward.wait_send()
-
-    @pl.when(links.has_left)
-    def _():
-        leftward.wait_send()
+class Chain:
+    def __init__(self, links, base, arrived, leaving, send_sem, recv_sem, chunks):
+        self.links, self.base, self.arrived, self.leaving = links, base, arrived, leaving
+        self.send_sem, self.recv_sem, self.chunks = send_sem, recv_sem, chunks
+
+    def send(self, k, side, device):
+        at = self.chunks[k]
+        return pltpu.make_async_remote_copy(
+            src_ref=self.leaving.at[side, :, at],
+            dst_ref=self.arrived.at[1 - side, :, at],
+            send_sem=self.send_sem.at[side, k],
+            recv_sem=self.recv_sem.at[1 - side, k],
+            device_id=device,
+            device_id_type=MESH,
+        )
+
+    def receive(self, k, side, device):
+        at = self.chunks[k]
+        return pltpu.make_async_remote_copy(
+            src_ref=self.leaving.at[side, :, at],
+            dst_ref=self.arrived.at[side, :, at],
+            send_sem=self.send_sem.at[side, k],
+            recv_sem=self.recv_sem.at[side, k],
+            device_id=device,
+            device_id_type=MESH,
+        )
+
+    def read(self, ref, k, *side):
+        return ref[(*side, slice(None), self.chunks[k])].astype(jnp.float32)
+
+    def begin(self, k):
+        links, at = self.links, self.chunks[k]
+
+        @pl.when(links.at_end)
+        def _():
+            own = self.base[:, at].astype(self.leaving.dtype)
+            self.leaving[links.inner, :, at] = own
+            self.arrived[links.outer, :, at] = jnp.zeros_like(own)
+            self.send(k, links.inner, links.to_inner).start()
+
+    def outward(self, k):
+        links, at = self.links, self.chunks[k]
+
+        @pl.when(jnp.logical_not(links.at_end))
+        def _():
+            self.receive(k, links.outer, links.to_outer).wait_recv()
+            total = self.read(self.base, k) + self.read(self.arrived, k, links.outer)
+            self.leaving[links.inner, :, at] = total.astype(self.leaving.dtype)
+            self.send(k, links.inner, links.to_inner).start()
+
+    def inward(self, k):
+        links, at = self.links, self.chunks[k]
+        self.receive(k, links.inner, links.to_inner).wait_recv()
+        total = self.read(self.base, k) + self.read(self.arrived, k, links.inner)
+
+        @pl.when(jnp.logical_not(links.at_end))
+        def _():
+            self.leaving[links.outer, :, at] = total.astype(self.leaving.dtype)
+            self.send(k, links.outer, links.to_outer).start()
+
+        return total + self.read(self.arrived, k, links.outer)
+
+    def finish(self, k):
+        links = self.links
+        self.send(k, links.inner, links.to_inner).wait_send()
+
+        @pl.when(jnp.logical_not(links.at_end))
+        def _():
+            self.send(k, links.outer, links.to_outer).wait_send()
+
+
+def cut(*edges):
+    return tuple(pl.ds(a, b - a) for a, b in zip(edges[:-1], edges[1:]))
 
 
 def half_tiles(half):
@@ -495,13 +515,26 @@
 
 
 def gather_kernel(
-    chunks, owners, master, full, own, got, left_in, right_in, left_out, right_out, send_sem, recv_sem
+    chunks,
+    owners,
+    master,
+    full,
+    own,
+    got,
+    base,
+    arrived,
+    leaving,
+    send_sem,
+    recv_sem,
+    chain_send,
+    chain_recv,
 ):
     links = Links(send_sem, recv_sem)
     quarter = full.shape[1] // 4
     tile_count, side = owners.shape[0], master.shape[2]
     most = master.shape[0] - 1
     rows = pl.ds(pl.multiple_of(links.dp * quarter, quarter), quarter)
+    near_rows = pl.ds(pl.multiple_of(links.near * quarter, quarter), quarter)
     rank, place = jnp.int32(0), []
     for i in range(tile_count):
         mine = owners[i] == links.seq
@@ -516,56 +549,66 @@
                 pair.append(jnp.where(mine, master[at, rows, :], 0.0))
             own[half, :, j * side : (j + 2) * side] = jnp.concatenate(pair, axis=1).astype(own.dtype)
     links.meet()
-    buffers = (left_in, right_in, left_out, right_out)
-    swaps = [
-        links.copy(own.at[1 - links.core, :, lanes], got.at[:, lanes], links.partner)
-        for lanes in chunks
-    ]
-    for swap in swaps:
-        swap.start()
-    chains = [chain_copies(links, buffers, lanes) for lanes in chunks]
-    planes = []
-    for swap, chain, lanes in zip(swaps, chains, chunks):
-        swap.wait()
-        base = own[links.core, :, lanes].astype(jnp.float32) + got[:, lanes].astype(jnp.float32)
-        total = chain_step(links, buffers, chain, lanes, base)
-        full[links.core, rows, lanes] = total.astype(full.dtype)
-        mine = full.at[links.core, rows, lanes]
-        other = full.at[
-            links.core, pl.ds(pl.multiple_of(links.near * quarter, quarter), quarter), lanes
-        ]
-        first = links.copy(mine, mine, links.to_near)
-        second = links.copy(mine, mine, links.to_far)
-        relay = links.copy(other, other, links.to_far)
-        share = links.copy(
-            full.at[links.core, :, lanes], full.at[links.core, :, lanes], links.partner
+    swaps, planes = [], []
+    for at in chunks:
+        swaps.append(
+            links.copy(own.at[1 - links.core, :, at], got.at[:, at], links.partner)
         )
-        first.start()
-        second.start()
-        planes.append((first, second, relay, share))
-    for first, second, relay, share in planes:
-        first.wait_recv()
-        relay.start()
-    for first, second, relay, share in planes:
-        second.wait_recv()
-        relay.wait_recv()
-        share.start()
-    for chain, (first, second, relay, share) in zip(chains, planes):
-        chain_end(links, chain)
-        first.wait_send()
-        second.wait_send()
-        relay.wait_send()
-        share.wait()
+        mine = full.at[links.core, rows, at]
+        other = full.at[links.core, near_rows, at]
+        both = full.at[links.core, :, at]
+        planes.append(
+            (
+                links.copy(mine, mine, links.to_near),
+                links.copy(mine, mine, links.to_far),
+                links.copy(other, other, links.to_far),
+                links.copy(both, both, links.partner),
+            )
+        )
+        swaps[-1].start()
+    chain = Chain(links, base, arrived, leaving, chain_send, chain_recv, chunks)
+
+    def collect(k):
+        at = chunks[k]
+        swaps[k].wait()
+        base[:, at] = own[links.core, :, at] + got[:, at]
+        chain.begin(k)
+
+    def spread(k):
+        full[links.core, rows, chunks[k]] = chain.inward(k).astype(full.dtype)
+        planes[k][0].start()
+        planes[k][1].start()
+
+    def relay(k):
+        planes[k][0].wait_recv()
+        planes[k][2].start()
+
+    def share(k):
+        planes[k][1].wait_recv()
+        planes[k][2].wait_recv()
+        planes[k][3].start()
+
+    count = len(chunks)
+    for k in range(count):
+        collect(k)
+    for k in range(count + 4):
+        for stage, late in ((chain.outward, 0), (spread, 1), (relay, 2), (share, 4)):
+            if 0 <= k - late < count:
+                stage(k - late)
+    for k in range(count):
+        chain.finish(k)
+        for copy in planes[k][:3]:
+            copy.wait_send()
+        planes[k][3].wait()
 
 
 def gather_weights(owners, master):
     slots, side, _ = master.shape
     width = owners.shape[0] // 2 * side
-    step = side * 2
-    chunks = (pl.ds(0, 3 * step), pl.ds(3 * step, 5 * step), pl.ds(8 * step, 8 * step))
+    chunks = cut(0, 640, 1152, 2816, 4480, width)
     low = jnp.bfloat16
-    part = pltpu.VMEM((side // 4, width), low)
-    count = 7 * len(chunks)
+    quarter = side // 4
+    count = len(chunks)
     return pl.pallas_call(
         functools.partial(gather_kernel, chunks),
         out_shape=jax.ShapeDtypeStruct((2, side, width), low),
@@ -575,14 +618,15 @@
         ],
         out_specs=pl.BlockSpec(memory_space=pltpu.VMEM),
         scratch_shapes=[
-            pltpu.VMEM((2, side // 4, width), low),
-            part,
-            part,
-            part,
-            part,
-            part,
-            pltpu.SemaphoreType.DMA((count,)),
-            pltpu.SemaphoreType.DMA((count,)),
+            pltpu.VMEM((2, quarter, width), low),
+            pltpu.VMEM((quarter, width), low),
+            pltpu.VMEM((quarter, width), low),
+            pltpu.VMEM((2, quarter, width), low),
+            pltpu.VMEM((2, quarter, width), low),
+            pltpu.SemaphoreType.DMA((5 * count,)),
+            pltpu.SemaphoreType.DMA((5 * count,)),
+            pltpu.SemaphoreType.DMA((2, count)),
+            pltpu.SemaphoreType.DMA((2, count)),
         ],
         compiler_params=pltpu.CompilerParams(
             collective_id=0, has_side_effects=True, vmem_limit_bytes=VMEM_LIMIT
@@ -602,14 +646,15 @@
     near_in,
     far_in,
     far_out,
-    left_in,
-    right_in,
-    left_out,
-    right_out,
+    base,
+    arrived,
+    leaving,
     total,
     by_tile,
     send_sem,
     recv_sem,
+    chain_send,
+    chain_recv,
 ):
     links = Links(send_sem, recv_sem)
     side = grads.shape[1]
@@ -620,53 +665,61 @@
         return pl.ds(pl.multiple_of(index * quarter, quarter), quarter)
 
     links.meet()
-    buffers = (left_in, right_in, left_out, right_out)
-    swaps = [
-        links.copy(grads.at[1 - links.core, :, lanes], got.at[:, lanes], links.partner)
-        for lanes in chunks
-    ]
-    nears = [
-        (
-            links.copy(mine_sum.at[rows_of(links.near), lanes], near_in.at[0, :, lanes], links.to_near),
+    swaps, nears, diagonals, fars, shares = [], [], [], [], []
+    for at in chunks:
+        swaps.append(links.copy(grads.at[1 - links.core, :, at], got.at[:, at], links.partner))
+        swaps[-1].start()
+        nears.append(
+            links.copy(mine_sum.at[rows_of(links.near), at], near_in.at[0, :, at], links.to_near)
+        )
+        diagonals.append(
             links.copy(
-                mine_sum.at[rows_of(links.diagonal), lanes], near_in.at[1, :, lanes], links.to_near
-            ),
+                mine_sum.at[rows_of(links.diagonal), at], near_in.at[1, :, at], links.to_near
+            )
         )
-        for lanes in chunks
-    ]
-    fars = [links.copy(far_out.at[:, lanes], far_in.at[:, lanes], links.to_far) for lanes in chunks]
-    chains = [chain_copies(links, buffers, lanes) for lanes in chunks]
-    for swap in swaps:
-        swap.start()
-    for swap, near, lanes in zip(swaps, nears, chunks):
-        swap.wait()
-        mine_sum[:, lanes] = (
-            grads[links.core, :, lanes].astype(wide) + got[:, lanes].astype(wide)
+        fars.append(links.copy(far_out.at[:, at], far_in.at[:, at], links.to_far))
+        part = total.at[links.core, :, at]
+        shares.append(links.copy(part, part, links.partner))
+    chain = Chain(links, base, arrived, leaving, chain_send, chain_recv, chunks)
+
+    def merge_cores(k):
+        at = chunks[k]
+        swaps[k].wait()
+        mine_sum[:, at] = (
+            grads[links.core, :, at].astype(wide) + got[:, at].astype(wide)
         ).astype(mine_sum.dtype)
-        near[1].start()
-        near[0].start()
-    for near, far, lanes in zip(nears, fars, chunks):
-        near[1].wait_recv()
-        far_out[:, lanes] = (
-            mine_sum[rows_of(links.far), lanes].astype(wide) + near_in[1, :, lanes].astype(wide)
+        diagonals[k].start()
+        nears[k].start()
+
+    def go_far(k):
+        at = chunks[k]
+        diagonals[k].wait_recv()
+        far_out[:, at] = (
+            mine_sum[rows_of(links.far), at].astype(wide) + near_in[1, :, at].astype(wide)
         ).astype(far_out.dtype)
-        far.start()
-    shares = []
-    for near, far, chain, lanes in zip(nears, fars, chains, chunks):
-        near[0].wait_recv()
-        far.wait_recv()
-        base = (
-            mine_sum[rows_of(links.dp), lanes].astype(wide)
-            + near_in[0, :, lanes].astype(wide)
-            + far_in[:, lanes].astype(wide)
+        fars[k].start()
+
+    def collect(k):
+        at = chunks[k]
+        nears[k].wait_recv()
+        fars[k].wait_recv()
+        base[:, at] = (
+            mine_sum[rows_of(links.dp), at].astype(wide)
+            + near_in[0, :, at].astype(wide)
+            + far_in[:, at].astype(wide)
         )
-        total[links.core, :, lanes] = chain_step(links, buffers, chain, lanes, base).astype(
-            total.dtype
-        )
-        part = total.at[links.core, :, lanes]
-        share = links.copy(part, part, links.partner)
-        share.start()
-        shares.append(share)
+        chain.begin(k)
+
+    def end(k):
+        total[links.core, :, chunks[k]] = chain.inward(k).astype(total.dtype)
+        shares[k].start()
+
+    count = len(chunks)
+    for k in range(count + 4):
+        stages = ((merge_cores, 0), (go_far, 1), (collect, 2), (chain.outward, 3), (end, 4))
+        for stage, late in stages:
+            if 0 <= k - late < count:
+                stage(k - late)
     for share in shares:
         share.wait()
     for half in range(2):
@@ -674,20 +727,16 @@
             by_tile[i] = total[half, :, j * side : (j + 1) * side].astype(wide)
     slots = tile_of_slot.shape[0]
     tiles_wide = slots * side
-    at_home = spread.at[rows_of(links.dp), :]
+    mine = rows_of(links.dp)
     for s in range(0, slots, 2):
-        pair = [
-            jnp.where(used[k] > 0, by_tile[tile_of_slot[k]], 0.0) for k in (s, s + 1)
-        ]
-        spread[rows_of(links.dp), s * side : (s + 2) * side] = jnp.concatenate(pair, axis=1).astype(
-            spread.dtype
-        )
+        pair = [jnp.where(used[k] > 0, by_tile[tile_of_slot[k]], 0.0) for k in (s, s + 1)]
+        spread[mine, s * side : (s + 2) * side] = jnp.concatenate(pair, axis=1).astype(spread.dtype)
     first_extra = by_tile.shape[0] // 2 * side
     extra = total.shape[2] - first_extra
     for half in range(2):
         begin = tiles_wide + half * extra
-        spread[rows_of(links.dp), begin : begin + extra] = total[half, :, first_extra:]
-    other = spread.at[rows_of(links.near), :]
+        spread[mine, begin : begin + extra] = total[half, :, first_extra:]
+    at_home, other = spread.at[mine, :], spread.at[rows_of(links.near), :]
     first = links.copy(at_home, at_home, links.to_near)
     second = links.copy(at_home, at_home, links.to_far)
     relay = links.copy(other, other, links.to_far)
@@ -699,25 +748,21 @@
     relay.wait()
     first.wait_send()
     second.wait_send()
-    for near, far, chain in zip(nears, fars, chains):
-        near[0].wait_send()
-        near[1].wait_send()
-        far.wait_send()
-        chain_end(links, chain)
+    for k in range(count):
+        nears[k].wait_send()
+        diagonals[k].wait_send()
+        fars[k].wait_send()
+        chain.finish(k)
 
 
 def reduce_grads(tile_of_slot, used, grads):
     _, side, width = grads.shape
     slots = tile_of_slot.shape[0]
-    tile_count = NTILES
-    extra = width - tile_count // 2 * side
-    step = side * 2
-    cuts = (0, 6 * step, 11 * step, width)
-    chunks = tuple(pl.ds(a, b - a) for a, b in zip(cuts[:-1], cuts[1:]))
+    extra = width - NTILES // 2 * side
+    chunks = cut(0, 1152, 2304, 3456, 4480, 5504, width)
     low = jnp.bfloat16
     quarter = side // 4
-    part = pltpu.VMEM((quarter, width), low)
-    count = 7 * len(chunks) + 3
+    count = len(chunks)
     return pl.pallas_call(
         functools.partial(reduce_kernel, chunks),
         out_shape=jax.ShapeDtypeStruct((side, slots * side + 2 * extra), low),
@@ -731,16 +776,17 @@
             pltpu.VMEM((side, width), low),
             pltpu.VMEM((side, width), low),
             pltpu.VMEM((2, quarter, width), low),
-            part,
-            part,
-            part,
-            part,
-            part,
-            part,
+            pltpu.VMEM((quarter, width), low),
+            pltpu.VMEM((quarter, width), low),
+            pltpu.VMEM((quarter, width), jnp.float32),
             pltpu.VMEM((2, quarter, width), low),
-            pltpu.VMEM((tile_count, quarter, side), jnp.float32),
-            pltpu.SemaphoreType.DMA((count,)),
-            pltpu.SemaphoreType.DMA((count,)),
+            pltpu.VMEM((2, quarter, width), low),
+            pltpu.VMEM((2, quarter, width), low),
+            pltpu.VMEM((NTILES, quarter, side), jnp.float32),
+            pltpu.SemaphoreType.DMA((5 * count + 3,)),
+            pltpu.SemaphoreType.DMA((5 * count + 3,)),
+            pltpu.SemaphoreType.DMA((2, count)),
+            pltpu.SemaphoreType.DMA((2, count)),
         ],
         compiler_params=pltpu.CompilerParams(
             collective_id=1, has_side_effects=True, vmem_limit_bytes=VMEM_LIMIT

time: 572 us -> 443 us (0.77)
  Pallas kernels: 245 us -> 115 us
    pallas_call x1, Pallas kernels: 134 us -> 67.6 us  [reduce_grads(): pl.pallas_call(functools.partial(reduce_kernel, chunks), out_shape=jax.Sh...]
    pallas_call x1, Pallas kernels: 111 us -> 47.6 us  [gather_weights(): pl.pallas_call(functools.partial(gather_kernel, chunks), out_shape=jax.Sh...]
  transfers between devices with their start and end apart: 4 -> 4, of which waited for: 2 -> 2; matrix products, arithmetic and copies ran while one was open for 16% -> 21% of each run, Pallas kernels for 0% -> 0%
where the time goes in v3:
time: 443 us; the launch traced here: 436 us
  local copies, waits for them, and re-layouts  136 us (31%)
  Pallas kernels  115 us (26%)
  other arithmetic  79.8 us (18%)
  matrix products  69.6 us (16%)
  starting transfers between devices  18.9 us (4%)
  waiting for transfers between devices  14.3 us (3%)
    pallas_call x1, Pallas kernels, reduce_grads(): pl.pallas_call(functools.partial(reduce_kernel, chunks), out_shape=jax.Sh...  67.6 us
    pallas_call x1, Pallas kernels, gather_weights(): pl.pallas_call(functools.partial(gather_kernel, chunks), out_shape=jax.Sh...  47.6 us
    dot_general x4, matrix products, block_back(): jnp.einsum('nbo,bio->nbi', row_view, blocks, preferred_element_type=jnp.f...  25.3 us
    unnamed x260, local copies, waits for them, and re-layouts  23.9 us
    convert_element_type x13, local copies, waits for them, and re-layouts, on_device_columns(): pack(g).astype(jnp.bfloat16)  20.1 us
    convert_element_type x1, other arithmetic, on_device_columns(): active_low = active.astype(jnp.bfloat16)  14.4 us
    mul x2, other arithmetic, on_device_columns(): tile_new[2] * mine_mask  13.6 us
    another operation x4, other arithmetic  12.8 us
  transfers between devices with their start and end apart: 4, of which 2 were waited for; matrix products, arithmetic and copies ran while one was open for 21% of the time, Pallas kernels for 0%

profile of v3, /device:TPU:0, one launch (start us, length us, event | category | flops | bytes accessed | tf_op | source)
XLA Modules:
  0.0 436.5 jit_solution(2454905358920972695)
XLA Ops:
  2.5 47.6 %gather_weights.1 = bf16[2,192,6144]{2,1,0:T(8,128)(2,1)} custom-call(s32[64]{0:T(128)} %owners.1, f32[16,192,192]{2,1,0:T(8,128)} %master.1), custom_call_target="tpu_custom_call" | custom-call | tf_op jit(solution)/shard_map/gather_weights/pallas_call | solution.py:612
  61.1 4.1 all-to-all-start
  70.0 4.2 fusion.120
  77.2 2.4 fusion.123
  79.5 6.6 %all-to-all-done = bf16[8,128,384]{2,1,0:T(8,128)(2,1)S(1)} async-done(((bf16[8,128,384]{2,1,0:T(8,128)(2,1)}), bf16[8,128,384]{2,1,0:T(8,128)(2,1)S(1)}, u32[]{:S(2)}, u32[]{:S(2)}) %all-to-all-start) | async-done | bytes 786464 | tf_op jit(solution)/shard_map/all_to_all | solution.py:855
  86.2 3.0 fusion.122
  92.8 4.4 %all-to-all-start.1 = ((bf16[8,128,384]{1,2,0:T(8,128)(2,1)}), bf16[8,128,384]{1,2,0:T(8,128)(2,1)}, u32[]{:S(2)}, u32[]{:S(2)}) async-start(bf16[8,128,384]{1,2,0:T(8,128)(2,1)} %bitcast.417), calls=%async_computation.1 | async-start | bytes 1572864 | tf_op jit(solution)/shard_map/all_to_all | solution.py:859
  101.8 2.9 reshape.1108
  105.8 4.4 %reshape_reshape.15 = bf16[4,192,4,192]{3,2,1,0:T(4,128)(2,1)} reshape(bf16[2,2,192,768]{3,2,1,0:T(8,128)(2,1)} %bitcast.413) | data formatting | bytes 2359296 | tf_op jit(solution)/shard_map/reshape;reshape | solution.py:839
  110.2 4.3 copy.232
  114.5 4.0 reshape.1092
  126.3 2.2 multiply_convert_fusion.2
  134.0 14.4 %fusion.3 = bf16[512,4,768]{0,2,1:T(8,128)(2,1)S(1)} fusion(f32[512,4,2,768]{0,3,2,1:T(8,128)S(1)} %bitcast.382), kind=kLoop, calls=%fused_computation.5 | loop fusion | flops 103809024 | bytes 15728640 | tf_op jit(solution)/shard_map/convert_element_type | solution.py:913
  154.1 2.8 reshape.1090
  156.9 2.6 copy.230
  159.5 2.8 copy.236
  162.3 3.5 convert_reduce_fusion
  167.7 19.4 %add_convert_fusion = (bf16[512,4,1,768]{0,3,1,2:T(8,128)(2,1)}, f32[512,4,1,768]{0,3,1,2:T(8,128)}, f32[4,768,512]{2,1,0:T(8,128)}) fusion(f32[512,4,2,768]{0,3,2,1:T(8,128)} %bitcast.383, bf16[4,768,192]{1,2,0:T(8,128)(2,1)S(1)} %copy-done.27, f32[512,4,192]{0,2,1:T(8,128)S(1)} %fusion.32), kind=kOutput, calls=%fused_computation.17 | convolution fusion | flops 719192064 | bytes 31064064 | tf_op jit(solution)/shard_map/nbo,bio->nbi/dot_general | solution.py:91
  187.1 8.9 %fusion.5 = bf16[512,4,1,768]{0,3,1,2:T(8,128)(2,1)S(1)} fusion(f32[4,768,512]{2,1,0:T(8,128)} %get-tuple-element.105, f32[512,4,1,768]{0,3,1,2:T(8,128)} %get-tuple-element.51, f32[512,4,2,768]{0,3,2,1:T(8,128)} %bitcast.384), kind=kLoop, calls=%fused_computation.11 | loop fusion | flops 6291456 | bytes 22020096 | tf_op jit(solution)/shard_map/convert.19
  196.0 2.5 pad_maximum_fusion
  202.4 3.6 multiply_reduce_fusion.2
  209.5 3.4 multiply_reduce_fusion
  215.2 3.4 copy.275
  220.7 5.3 %all-to-all-start.2 = ((bf16[8,128,384]{2,1,0:T(8,128)(2,1)}), bf16[8,128,384]{2,1,0:T(8,128)(2,1)}, u32[]{:S(2)}, u32[]{:S(2)}) async-start(bf16[8,128,384]{2,1,0:T(8,128)(2,1)} %bitcast.416), calls=%async_computation.2 | async-start | bytes 1572864 | tf_op jit(solution)/shard_map/all_to_all | solution.py:855
  226.0 3.6 convolution_convert_fusion.1
  233.9 3.1 copy.256
  237.0 3.9 convert_element_type.354
  244.8 6.4 %convolution_convert_fusion = bf16[4,192,1536]{2,1,0:T(8,128)(2,1)} fusion(bf16[512,4,192]{0,2,1:T(8,128)(2,1)S(1)} %copy-done.6, bf16[512,4,1536]{0,2,1:T(8,128)(2,1)} %bitcast.390), kind=kOutput, calls=%fused_computation.45 | convolution fusion | flops 1209139200 | bytes 9437184 | tf_op jit(solution)/shard_map/nbi,nbo->bio/dot_general | solution.py:99
  251.2 4.7 %reshape.1113 = bf16[4,1,192,8,192]{4,3,2,0,1:T(8,128)(2,1)S(1)} reshape(bf16[4,192,1536]{2,1,0:T(8,128)(2,1)} %convolution_convert_fusion) | data formatting | bytes 4718592 | tf_op jit(solution)/shard_map/convert.10
  257.8 2.2 convert_element_type.350
  261.0 2.2 convert_element_type.347
  267.2 3.2 fusion.124
  274.1 5.1 %all-to-all-start.3 = ((bf16[8,128,384]{1,2,0:T(8,128)(2,1)}), bf16[8,128,384]{1,2,0:T(8,128)(2,1)S(1)}, u32[]{:S(2)}, u32[]{:S(2)}) async-start(bf16[8,128,384]{1,2,0:T(8,128)(2,1)} %bitcast.378), calls=%async_computation.3 | async-start | bytes 1572864 | tf_op jit(solution)/shard_map/all_to_all | solution.py:859
  279.2 2.9 fusion.58
  285.6 3.9 convolution_multiply_fusion
  289.8 2.7 dynamic_update_slice.11
  292.5 7.7 %all-to-all-done.3 = bf16[8,128,384]{1,2,0:T(8,128)(2,1)S(1)} async-done(((bf16[8,128,384]{1,2,0:T(8,128)(2,1)}), bf16[8,128,384]{1,2,0:T(8,128)(2,1)S(1)}, u32[]{:S(2)}, u32[]{:S(2)}) %all-to-all-start.3) | async-done | bytes 786464 | tf_op jit(solution)/shard_map/all_to_all | solution.py:859
  300.8 2.3 multiply_convert_fusion.1
  314.6 67.6 %reduce_grads.1 = bf16[192,3840]{1,0:T(8,128)(2,1)} custom-call(s32[16]{0:T(128)} %dynamic_slice.13.tile_of_slot, s32[16]{0:T(128)} %dynamic_slice.14.used, bf16[2,192,6528]{2,1,0:T(8,128)(2,1)} %copy-done.35), custom_call_target="tpu_custom_call" | custom-call | tf_op jit(solution)/shard_map/reduce_grads/pallas_call | solution.py:766
  385.4 2.7 reshape.1101
  388.1 2.6 copy.245
  395.0 3.3 slice_multiply_fusion.2
  398.2 4.1 mul.988
  402.4 3.1 mul.994
  405.5 4.1 mul.1003
  411.0 13.0 %add_multiply_fusion = (f32[16,192,192]{2,1,0:T(8,128)}, f32[16,192,192]{2,1,0:T(8,128)S(1)}, f32[16,192,192]{2,1,0:T(8,128)S(1)}) fusion(f32[16,192,192]{2,1,0:T(8,128)} %param.26, f32[16]{0:T(128)S(1)} %copy-done.117, f32[16,192,192]{2,1,0:T(8,128)} %master.1, f32[192,16,192]{2,1,0:T(8,128)S(1)} %mul.994, f32[16,192,192]{2,1,0:T(8,128)} %param.25, ...), kind=kLoop, calls=%fused_computation.55 | loop fusion | flops 8847360 | bytes 23593024 | tf_op jit(solution)/shard_map/mul | solution.py:997
  424.1 5.9 %broadcast_multiply_fusion = (f32[16,192,192]{2,1,0:T(8,128)}, f32[16,192,192]{2,1,0:T(8,128)}) fusion(f32[16,192,192]{2,1,0:T(8,128)S(1)} %get-tuple-element.41, f32[16]{0:T(128)S(1)} %copy-done.116, f32[16,192,192]{2,1,0:T(8,128)S(1)} %get-tuple-element.42, f32[192,16,192]{2,1,0:T(8,128)S(1)} %mul.994, f32[16,192,192]{2,1,0:T(8,128)S(1)} %copy-done.19), kind=kLoop, calls=%fused_computation.77 | loop fusion | flops 2949120 | bytes 14155840 | tf_op jit(solution)/shard_map/mul | solution.py:996
  430.3 3.9 fusion.34
  (372 shorter events, 107.1 us)
Async XLA Ops:
  2.5 126.0 %copy-start.28 = (bf16[512,4,192]{0,2,1:T(8,128)(2,1)}, bf16[512,4,192]{0,2,1:T(8,128)(2,1)S(1)}, u32[]{:S(2)}) copy-start(bf16[512,4,192]{0,2,1:T(8,128)(2,1)S(1)} %reshape_reshape.14) | copy-start | bytes 2359300
  55.0 71.2 %copy-start.17 = (f32[512,768]{0,1:T(8,128)}, f32[512,768]{0,1:T(8,128)S(1)}, u32[]{:S(2)}) copy-start(f32[512,768]{0,1:T(8,128)S(1)} %get-tuple-element.55) | copy-start | bytes 4718596
  57.1 8.1 %copy-start.122 = (s32[64]{0:T(128)S(1)}, s32[64]{0:T(128)}, u32[]{:S(2)}) copy-start(s32[64]{0:T(128)} %owners.1) | copy-start | bytes 772
  61.1 8.8 %copy-start.102 = (f32[5,128]{1,0:T(8,128)S(1)}, f32[5,128]{1,0:T(8,128)}, u32[]{:S(2)}) copy-start(f32[5,128]{1,0:T(8,128)} %param.31) | copy-start | bytes 7684
  61.1 25.0 %all-to-all-start = ((bf16[8,128,384]{2,1,0:T(8,128)(2,1)}), bf16[8,128,384]{2,1,0:T(8,128)(2,1)S(1)}, u32[]{:S(2)}, u32[]{:S(2)}) async-start(bf16[8,128,384]{2,1,0:T(8,128)(2,1)} %bitcast.6), calls=%async_computation | async-start | bytes 1572864 | tf_op jit(solution)/shard_map/all_to_all | solution.py:855
  65.3 9.7 %copy-start.67 = (f32[128,768]{1,0:T(8,128)S(1)}, f32[128,768]{1,0:T(8,128)}, u32[]{:S(2)}) copy-start(f32[128,768]{1,0:T(8,128)} %param.35) | copy-start | bytes 1179652
  69.9 7.2 %copy-start.124 = (bf16[1024,1024]{1,0:T(8,128)(2,1)S(1)}, bf16[1024,1024]{1,0:T(8,128)(2,1)}, u32[]{:S(2)}) copy-start(bf16[1024,1024]{1,0:T(8,128)(2,1)} %constant.65.clone) | copy-start | bytes 6291460
  69.9 20.1 %copy-start.104 = (pred[512]{0:T(512)(128)(4,1)}, pred[512]{0:T(512)(128)(4,1)S(1)}, u32[]{:S(2)}) copy-start(pred[512]{0:T(512)(128)(4,1)S(1)} %iota_compare_fusion.2) | copy-start | bytes 1540
  91.8 6.6 %copy-start.83 = (f32[5,768]{1,0:T(8,128)S(1)}, f32[5,768]{1,0:T(8,128)}, u32[]{:S(2)}) copy-start(f32[5,768]{1,0:T(8,128)} %param.27) | copy-start | bytes 46084
  91.8 8.6 %copy-start.33 = (bf16[4,1,128,768]{3,2,1,0:T(8,128)(2,1)S(1)}, bf16[4,1,128,768]{3,2,1,0:T(8,128)(2,1)}, u32[]{:S(2)}) copy-start(bf16[4,1,128,768]{3,2,1,0:T(8,128)(2,1)} %param.21) | copy-start | bytes 2359300
  92.8 31.6 %all-to-all-start.1 = ((bf16[8,128,384]{1,2,0:T(8,128)(2,1)}), bf16[8,128,384]{1,2,0:T(8,128)(2,1)}, u32[]{:S(2)}, u32[]{:S(2)}) async-start(bf16[8,128,384]{1,2,0:T(8,128)(2,1)} %bitcast.417), calls=%async_computation.1 | async-start | bytes 1572864 | tf_op jit(solution)/shard_map/all_to_all | solution.py:859
  130.2 32.0 %copy-start.91 = (f32[4,128]{1,0:T(4,128)}, f32[4,128]{1,0:T(4,128)S(1)}, u32[]{:S(2)}) copy-start(f32[4,128]{1,0:T(4,128)S(1)} %get-tuple-element.86) | copy-start | bytes 6148
  130.5 75.5 %copy-start.85 = (f32[512]{0:T(512)}, f32[512]{0:T(512)S(1)}, u32[]{:S(2)}) copy-start(f32[512]{0:T(512)S(1)} %multiply_reduce_fusion.6) | copy-start | bytes 6148
  130.5 31.8 %copy-start.95 = (f32[4,128]{1,0:T(4,128)}, f32[4,128]{1,0:T(4,128)S(1)}, u32[]{:S(2)}) copy-start(f32[4,128]{1,0:T(4,128)S(1)} %bitcast_rsqrt_fusion.1) | copy-start | bytes 6148
  130.8 17.6 %copy-start.5 = (bf16[512,4,192]{0,2,1:T(8,128)(2,1)}, bf16[512,4,192]{0,2,1:T(8,128)(2,1)S(1)}, u32[]{:S(2)}) copy-start(bf16[512,4,192]{0,2,1:T(8,128)(2,1)S(1)} %add_convert_fusion.5) | copy-start | bytes 2359300
  134.0 14.4 %copy-start = (f32[4,1536,512]{2,1,0:T(8,128)}, f32[4,1536,512]{2,1,0:T(8,128)S(1)}, u32[]{:S(2)}) copy-start(f32[4,1536,512]{2,1,0:T(8,128)S(1)} %fusion.37) | copy-start | bytes 37748740
  134.0 14.4 %copy-start.26 = (bf16[4,768,192]{1,2,0:T(8,128)(2,1)S(1)}, bf16[4,768,192]{1,2,0:T(8,128)(2,1)}, u32[]{:S(2)}) copy-start(bf16[4,768,192]{1,2,0:T(8,128)(2,1)} %reshape.1092) | copy-start | bytes 3538948
  150.1 12.2 %copy-start.93 = (f32[4,128]{1,0:T(4,128)}, f32[4,128]{1,0:T(4,128)S(1)}, u32[]{:S(2)}) copy-start(f32[4,128]{1,0:T(4,128)S(1)} %get-tuple-element.88) | copy-start | bytes 6148
  152.4 9.8 %copy-start.97 = (f32[4,128]{1,0:T(4,128)}, f32[4,128]{1,0:T(4,128)S(1)}, u32[]{:S(2)}) copy-start(f32[4,128]{1,0:T(4,128)S(1)} %get-tuple-element.84) | copy-start | bytes 6148
  152.4 9.8 %copy-start.99 = (f32[4,128]{1,0:T(4,128)}, f32[4,128]{1,0:T(4,128)S(1)}, u32[]{:S(2)}) copy-start(f32[4,128]{1,0:T(4,128)S(1)} %get-tuple-element.85) | copy-start | bytes 6148
  167.7 19.4 %copy-start.39 = (f32[512,4,192]{0,2,1:T(8,128)}, f32[512,4,192]{0,2,1:T(8,128)S(1)}, u32[]{:S(2)}) copy-start(f32[512,4,192]{0,2,1:T(8,128)S(1)} %fusion.32) | copy-start | bytes 4718596
  198.9 7.1 %copy-start.4 = (bf16[512,4,2,768]{0,3,2,1:T(8,128)(2,1)}, bf16[512,4,2,768]{0,3,2,1:T(8,128)(2,1)S(1)}, u32[]{:S(2)}) copy-start(bf16[512,4,2,768]{0,3,2,1:T(8,128)(2,1)S(1)} %copy.238) | copy-start | bytes 18874372
  215.2 10.9 %copy-start.3 = (bf16[512,4,768]{0,2,1:T(8,128)(2,1)S(1)}, bf16[512,4,768]{0,2,1:T(8,128)(2,1)}, u32[]{:S(2)}) copy-start(bf16[512,4,768]{0,2,1:T(8,128)(2,1)} %copy-done.2) | copy-start | bytes 9437188
  220.7 46.4 %all-to-all-start.2 = ((bf16[8,128,384]{2,1,0:T(8,128)(2,1)}), bf16[8,128,384]{2,1,0:T(8,128)(2,1)}, u32[]{:S(2)}, u32[]{:S(2)}) async-start(bf16[8,128,384]{2,1,0:T(8,128)(2,1)} %bitcast.416), calls=%async_computation.2 | async-start | bytes 1572864 | tf_op jit(solution)/shard_map/all_to_all | solution.py:855
  274.1 26.1 %all-to-all-start.3 = ((bf16[8,128,384]{1,2,0:T(8,128)(2,1)}), bf16[8,128,384]{1,2,0:T(8,128)(2,1)S(1)}, u32[]{:S(2)}, u32[]{:S(2)}) async-start(bf16[8,128,384]{1,2,0:T(8,128)(2,1)} %bitcast.378), calls=%async_computation.3 | async-start | bytes 1572864 | tf_op jit(solution)/shard_map/all_to_all | solution.py:859
  283.3 6.1 %copy-start.72 = (f32[1024,5]{0,1:T(8,128)S(1)}, f32[1024,5]{0,1:T(8,128)}, u32[]{:S(2)}) copy-start(f32[1024,5]{0,1:T(8,128)} %stack.30) | copy-start | bytes 61444
  289.5 11.3 %copy-start.12 = (f32[512,768]{0,1:T(8,128)S(1)}, f32[512,768]{0,1:T(8,128)}, u32[]{:S(2)}) copy-start(f32[512,768]{0,1:T(8,128)} %copy-done.11) | copy-start | bytes 4718596
  384.2 50.0 %copy-start.73 = (f32[2,5,384]{2,1,0:T(8,128)}, f32[2,5,384]{2,1,0:T(8,128)S(1)}, u32[]{:S(2)}) copy-start(f32[2,5,384]{2,1,0:T(8,128)S(1)} %get-tuple-element.79) | copy-start | bytes 46084
  405.5 5.5 %copy-start.117 = (f32[16]{0:T(128)S(1)}, f32[16]{0:T(128)}, u32[]{:S(2)}) copy-start(f32[16]{0:T(128)} %get-tuple-element.43) | copy-start | bytes 196
  410.9 13.0 %copy-start.19 = (f32[16,192,192]{2,1,0:T(8,128)S(1)}, f32[16,192,192]{2,1,0:T(8,128)}, u32[]{:S(2)}) copy-start(f32[16,192,192]{2,1,0:T(8,128)} %param.25) | copy-start | bytes 7077892
  411.0 13.0 %copy-start.116 = (f32[16]{0:T(128)S(1)}, f32[16]{0:T(128)}, u32[]{:S(2)}) copy-start(f32[16]{0:T(128)} %get-tuple-element.44) | copy-start | bytes 196
  423.9 6.1 %copy-start.20 = (f32[16,192,192]{2,1,0:T(8,128)}, f32[16,192,192]{2,1,0:T(8,128)S(1)}, u32[]{:S(2)}) copy-start(f32[16,192,192]{2,1,0:T(8,128)S(1)} %get-tuple-element.42) | copy-start | bytes 7077892
  423.9 6.1 %copy-start.7 = (f32[4,1,128,768]{3,2,1,0:T(8,128)S(1)}, f32[4,1,128,768]{3,2,1,0:T(8,128)}, u32[]{:S(2)}) copy-start(f32[4,1,128,768]{3,2,1,0:T(8,128)} %copy.230) | copy-start | bytes 4718596
  423.9 6.1 %copy-start.8 = (f32[4,1,128,768]{3,2,1,0:T(8,128)S(1)}, f32[4,1,128,768]{3,2,1,0:T(8,128)}, u32[]{:S(2)}) copy-start(f32[4,1,128,768]{3,2,1,0:T(8,128)} %copy.236) | copy-start | bytes 4718596
  423.9 6.1 %copy-start.32 = (bf16[4,1,128,768]{3,2,1,0:T(8,128)(2,1)S(1)}, bf16[4,1,128,768]{3,2,1,0:T(8,128)(2,1)}, u32[]{:S(2)}) copy-start(bf16[4,1,128,768]{3,2,1,0:T(8,128)(2,1)} %param.20) | copy-start | bytes 2359300
  424.0 6.1 %copy-start.34 = (bf16[4,1,128,768]{3,2,1,0:T(8,128)(2,1)S(1)}, bf16[4,1,128,768]{3,2,1,0:T(8,128)(2,1)}, u32[]{:S(2)}) copy-start(bf16[4,1,128,768]{3,2,1,0:T(8,128)(2,1)} %param.21) | copy-start | bytes 2359300
  424.0 6.1 %copy-start.36 = (f32[4,1,128,768]{3,2,1,0:T(8,128)S(1)}, f32[4,1,128,768]{3,2,1,0:T(8,128)}, u32[]{:S(2)}) copy-start(f32[4,1,128,768]{3,2,1,0:T(8,128)} %copy.240) | copy-start | bytes 4718596
  424.0 6.1 %copy-start.76 = (f32[768]{0:T(1024)S(1)}, f32[768]{0:T(1024)}, u32[]{:S(2)}) copy-start(f32[768]{0:T(1024)} %copy-done.74) | copy-start | bytes 9220
  424.0 6.1 %copy-start.79 = (f32[768]{0:T(1024)S(1)}, f32[768]{0:T(1024)}, u32[]{:S(2)}) copy-start(f32[768]{0:T(1024)} %copy-done.77) | copy-start | bytes 9220
  424.0 6.1 %copy-start.82 = (f32[768]{0:T(1024)S(1)}, f32[768]{0:T(1024)}, u32[]{:S(2)}) copy-start(f32[768]{0:T(1024)} %copy-done.80) | copy-start | bytes 9220
  424.0 6.1 %copy-start.92 = (f32[4,128]{1,0:T(4,128)S(1)}, f32[4,128]{1,0:T(4,128)}, u32[]{:S(2)}) copy-start(f32[4,128]{1,0:T(4,128)} %copy-done.91) | copy-start | bytes 6148
  424.0 6.1 %copy-start.94 = (f32[4,128]{1,0:T(4,128)S(1)}, f32[4,128]{1,0:T(4,128)}, u32[]{:S(2)}) copy-start(f32[4,128]{1,0:T(4,128)} %copy-done.93) | copy-start | bytes 6148
  424.0 6.1 %copy-start.96 = (f32[4,128]{1,0:T(4,128)S(1)}, f32[4,128]{1,0:T(4,128)}, u32[]{:S(2)}) copy-start(f32[4,128]{1,0:T(4,128)} %copy-done.95) | copy-start | bytes 6148
  424.0 6.1 %copy-start.98 = (f32[4,128]{1,0:T(4,128)S(1)}, f32[4,128]{1,0:T(4,128)}, u32[]{:S(2)}) copy-start(f32[4,128]{1,0:T(4,128)} %copy-done.97) | copy-start | bytes 6148
  424.1 6.1 %copy-start.100 = (f32[4,128]{1,0:T(4,128)S(1)}, f32[4,128]{1,0:T(4,128)}, u32[]{:S(2)}) copy-start(f32[4,128]{1,0:T(4,128)} %copy-done.99) | copy-start | bytes 6148
  424.1 6.1 %copy-start.101 = (f32[768]{0:T(1024)S(1)}, f32[768]{0:T(1024)}, u32[]{:S(2)}) copy-start(f32[768]{0:T(1024)} %get-tuple-element.29) | copy-start | bytes 9220
  424.1 6.1 %copy-start.108 = (f32[4,128]{1,0:T(4,128)S(1)}, f32[4,128]{1,0:T(4,128)}, u32[]{:S(2)}) copy-start(f32[4,128]{1,0:T(4,128)} %get-tuple-element.80) | copy-start | bytes 6148
  424.1 6.1 %copy-start.109 = (f32[4,128]{1,0:T(4,128)S(1)}, f32[4,128]{1,0:T(4,128)}, u32[]{:S(2)}) copy-start(f32[4,128]{1,0:T(4,128)} %get-tuple-element.82) | copy-start | bytes 6148
  (84 other events, 217.8 us)

commit v4 on v3

--- a/solution.py
+++ b/solution.py
@@ -795,6 +795,439 @@
     )(tile_of_slot, used, grads)
 
 
+VMEM = pl.BlockSpec(memory_space=pltpu.VMEM)
+SMEM = pl.BlockSpec(memory_space=pltpu.SMEM)
+NN = (((1,), (0,)), ((), ()))
+NT = (((1,), (1,)), ((), ()))
+TN = (((0,), (0,)), ((), ()))
+
+
+def mul(left, right, dims=NN):
+    return lax.dot_general(left, right, dims, preferred_element_type=jnp.float32)
+
+
+def plain_call(kernel, name, out_shape, scratch=(), in_specs=None):
+    def call(*arrays):
+        return pl.pallas_call(
+            kernel,
+            out_shape=out_shape,
+            in_specs=[VMEM] * len(arrays) if in_specs is None else in_specs,
+            out_specs=jax.tree.map(lambda _: VMEM, out_shape),
+            scratch_shapes=list(scratch),
+            compiler_params=pltpu.CompilerParams(vmem_limit_bytes=VMEM_LIMIT),
+            name=name,
+        )(*arrays)
+
+    return call
+
+
+def filter_constants(grid_rows, row_len, width):
+    length = grid_rows * row_len
+    position = (np.arange(grid_rows)[:, None] + grid_rows * np.arange(row_len)[None, :]).reshape(-1)
+    turn = 2.0 * np.pi * position / length
+    rows = [position / length, np.cos(turn), -np.sin(turn), np.cos(2 * turn), -np.sin(2 * turn)]
+    features = np.zeros((length, 8), np.float32)
+    features[:, :5] = np.stack(rows, axis=1)
+    rate = 0.3 * 1000.0 ** np.mod(golden * np.arange(width), 1.0)
+    total = np.expm1(-2.0 * rate) / np.expm1(-2.0 * rate / length)
+    channels = np.stack([rate, 1.0 / np.sqrt(total)]).astype(np.float32)
+    return (features, channels)
+
+
+def phases_of(features, filter_in):
+    total = features[:, 0:1] * filter_in[0:1, :]
+    for i in range(1, filter_in.shape[0]):
+        total += features[:, i : i + 1] * filter_in[i : i + 1, :]
+    return total
+
+
+def first_row(shape):
+    return lax.broadcasted_iota(jnp.int32, shape, 0) == 0
+
+
+def spectrum_product(one_real, one_imag, two_real, two_imag, sign):
+    first = first_row(one_real.shape)
+    cross = jnp.where(first, 0.0, two_imag) * sign
+    diag = jnp.where(first, two_imag, two_real)
+    return (one_real * two_real - one_imag * cross, one_real * cross + one_imag * diag)
+
+
+def decay_of(features, channels, lanes):
+    return jnp.exp(-features[:, 0:1] * channels[0:1, lanes]) * channels[1:2, lanes]
+
+
+def half_lanes(width):
+    half = lax.rem(lax.axis_index("seq"), 2)
+    return pl.ds(pl.multiple_of(half * width, width), width)
+
+
+def taps_kernel(features, channels, filter_in, filter_out, table, spec):
+    length, width = spec.shape
+    lanes = half_lanes(width)
+    hidden = jnp.sin(phases_of(features[...], filter_in[...]))
+    taps = mul(hidden.astype(jnp.bfloat16), filter_out[:, lanes].astype(jnp.bfloat16))
+    taps = (taps * decay_of(features, channels, lanes)).astype(jnp.bfloat16)
+    scale = jnp.where(first_row((length // 2, 1)), 1.0 / length, 2.0 / length)
+    for part in range(2):
+        rows = slice(part * length // 2, (part + 1) * length // 2)
+        spec[rows, :] = mul(table[rows, :], taps) * scale
+
+
+def conv_kernel(cells, table, table_back, taps_spec, out, kv_spec):
+    length, width = kv_spec.shape
+    half = length // 2
+    columns = cells[...].reshape(length, width)
+    real, imag = mul(table[:half], columns), mul(table[half:], columns)
+    kv_spec[:half] = real
+    kv_spec[half:] = imag
+    real, imag = spectrum_product(real, imag, taps_spec[:half], taps_spec[half:], 1.0)
+    result = mul(table_back[:, :half], real.astype(jnp.bfloat16))
+    result += mul(table_back[:, half:], imag.astype(jnp.bfloat16))
+    out[...] = result.astype(out.dtype).reshape(out.shape)
+
+
+def conv_back_kernel(
+    cells,
+    table,
+    table_back,
+    taps_spec,
+    kv_spec,
+    features,
+    channels,
+    filter_in,
+    filter_out,
+    out,
+    grad_out,
+    grad_in,
+):
+    low = jnp.bfloat16
+    length, width = kv_spec.shape
+    half = length // 2
+    columns = cells[...].reshape(length, width)
+    back_real, back_imag = mul(table[:half], columns), mul(table[half:], columns)
+    real, imag = spectrum_product(back_real, back_imag, taps_spec[:half], taps_spec[half:], -1.0)
+    result = mul(table_back[:, :half], real.astype(low)) + mul(table_back[:, half:], imag.astype(low))
+    out[...] = result.astype(out.dtype).reshape(out.shape)
+    scale = jnp.where(first_row((half, 1)), 1.0 / length, 2.0 / length)
+    real, imag = spectrum_product(back_real, back_imag, kv_spec[:half], kv_spec[half:], -1.0)
+    real, imag = (real * scale).astype(low), (imag * scale).astype(low)
+    d_taps = mul(table_back[:, :half], real) + mul(table_back[:, half:], imag)
+    lanes = half_lanes(width)
+    scaled = (d_taps * decay_of(features, channels, lanes)).astype(low)
+    phases = phases_of(features[...], filter_in[...])
+    grad_out[...] = mul(jnp.sin(phases).astype(low), scaled, TN)
+    d_hidden = mul(scaled, filter_out[:, lanes].astype(low), NT) * jnp.cos(phases)
+    grad_in[...] = jnp.zeros_like(grad_in)
+    for i in range(filter_in.shape[0]):
+        grad_in[i : i + 1, :] = jnp.sum(features[:, i : i + 1] * d_hidden, axis=0, keepdims=True)
+
+
+def tile_at(packed, half, first):
+    return packed[half, :, first : first + packed.shape[1]]
+
+
+def qkv_kernel(x, packed, query, key, value, kv):
+    side = packed.shape[1]
+    count = kv.shape[0] // 2
+    row_len, width = kv.shape[1:]
+    for i in range(12):
+        block, half = i // 3, i // 6
+        part = mul(x[:, block * side : (block + 1) * side], tile_at(packed, half, (i % 6) * side))
+        target = (query, key, value)[i // 4]
+        at = (i % 4) * side
+        target[:, at : at + side] = part.astype(target.dtype)
+    for s in range(count):
+        rows = slice(s * row_len, (s + 1) * row_len)
+        for h in range(2):
+            lanes = slice(h * width, (h + 1) * width)
+            both = key[rows, lanes].astype(jnp.float32) * value[rows, lanes].astype(jnp.float32)
+            kv[2 * s + h] = both.astype(kv.dtype)
+
+
+def normalize(values):
+    centered = values - jnp.mean(values, axis=-1, keepdims=True)
+    spread = lax.rsqrt(jnp.mean(centered * centered, axis=-1, keepdims=True) + norm_eps)
+    return (centered * spread, spread)
+
+
+def normalize_back(gradient, unit, spread):
+    mean = jnp.mean(gradient, axis=-1, keepdims=True)
+    along = jnp.mean(gradient * unit, axis=-1, keepdims=True)
+    return (gradient - mean - unit * along) * spread
+
+
+def gelu_parts(v):
+    share = 0.5 + 0.5 * lax.erf(v * math.sqrt(0.5))
+    density = jnp.exp(-0.5 * v * v) * (1.0 / math.sqrt(2.0 * math.pi))
+    return (v * share, share + v * density)
+
+
+def layer_kernel(
+    conv,
+    query,
+    kv,
+    x,
+    cotangent,
+    vectors,
+    packed,
+    output,
+    d_first_out,
+    d_inner_out,
+    d_query,
+    grads,
+    sums,
+    gated_all,
+    normed_all,
+    d_branch_all,
+    d_down_all,
+    active_all,
+    d_gate_all,
+    d_up_all,
+    down_weights,
+):
+    wide, low = jnp.float32, jnp.bfloat16
+    side = packed.shape[1]
+    row_len, width = conv.shape[1:]
+    tokens = x.shape[0]
+    per_step = 2
+    rows_step = per_step * row_len
+    quarter = 4 * side
+    gain_one, bias_one = vectors[0:1], vectors[1:2]
+    gain_two, bias_two = vectors[2:3], vectors[3:4]
+    skip = vectors[4:5]
+    out_at, gate_at, up_at, down_at = 6 * side, 8 * side, 16 * side, 24 * side
+    for b in range(4):
+        for i in range(4):
+            down_weights[b, i * side : (i + 1) * side, :] = tile_at(
+                packed, b // 2, down_at + (4 * (b % 2) + i) * side
+            )
+    sums[...] = jnp.zeros_like(sums)
+
+    def cells(ref, step):
+        parts = ref[pl.ds(step * 2 * per_step, 2 * per_step)].astype(wide)
+        lines = [
+            jnp.concatenate([parts[2 * s], parts[2 * s + 1]], axis=1) for s in range(per_step)
+        ]
+        return jnp.concatenate(lines, axis=0)
+
+    def block(values, b):
+        return values[:, b * side : (b + 1) * side]
+
+    def add_sum(row, values):
+        sums[row : row + 1, :] += jnp.sum(values, axis=0, keepdims=True)
+
+    @pl.loop(0, tokens // rows_step)
+    def _(step):
+        rows = pl.ds(pl.multiple_of(step * rows_step, rows_step), rows_step)
+        kv_here = cells(kv, step)
+        inner = cells(conv, step) + skip * kv_here
+        query_here = query[rows, :].astype(wide)
+        gated = (query_here * inner).astype(low)
+        gated_all[rows, :] = gated
+        branch = jnp.concatenate(
+            [
+                mul(block(gated, b), tile_at(packed, b // 2, out_at + (b % 2) * side))
+                for b in range(4)
+            ],
+            axis=1,
+        )
+        unit_one, spread_one = normalize(x[rows, :].astype(wide) + branch)
+        normed = (unit_one * gain_one + bias_one).astype(low)
+        normed_all[rows, :] = normed
+        down = []
+        for b in range(4):
+            lanes = slice(b * quarter, (b + 1) * quarter)
+            at = (b % 2) * quarter
+            here = block(normed, b)
+            gate = mul(here, packed[b // 2, :, gate_at + at : gate_at + at + quarter])
+            up = mul(here, packed[b // 2, :, up_at + at : up_at + at + quarter])
+            curved, slope = gelu_parts(gate)
+            active = (curved * up).astype(low)
+            active_all[rows, lanes] = active
+            d_gate_all[rows, lanes] = (slope * up).astype(low)
+            d_up_all[rows, lanes] = curved.astype(low)
+            down.append(mul(active, down_weights[b]))
+        unit_two, spread_two = normalize(normed.astype(wide) + jnp.concatenate(down, axis=1))
+        output[rows, :] = (unit_two * gain_two + bias_two).astype(low)
+        cot = cotangent[rows, :].astype(wide)
+        add_sum(2, cot * unit_two)
+        add_sum(3, cot)
+        d_second = normalize_back(cot * gain_two, unit_two, spread_two)
+        d_down = d_second.astype(low)
+        d_down_all[rows, :] = d_down
+        d_normed = []
+        for b in range(4):
+            lanes = slice(b * quarter, (b + 1) * quarter)
+            at = (b % 2) * quarter
+            d_active = mul(block(d_down, b), down_weights[b], NT)
+            d_gate = (d_active * d_gate_all[rows, lanes].astype(wide)).astype(low)
+            d_up = (d_active * d_up_all[rows, lanes].astype(wide)).astype(low)
+            d_gate_all[rows, lanes] = d_gate
+            d_up_all[rows, lanes] = d_up
+            d_normed.append(
+                mul(d_gate, packed[b // 2, :, gate_at + at : gate_at + at + quarter], NT)
+                + mul(d_up, packed[b // 2, :, up_at + at : up_at + at + quarter], NT)
+            )
+        d_normed = d_second + jnp.concatenate(d_normed, axis=1)
+        add_sum(0, d_normed * unit_one)
+        add_sum(1, d_normed)
+        d_first = normalize_back(d_normed * gain_one, unit_one, spread_one)
+        d_first_out[rows, :] = d_first
+        d_branch = d_first.astype(low)
+        d_branch_all[rows, :] = d_branch
+        d_gated = jnp.concatenate(
+            [
+                mul(block(d_branch, b), tile_at(packed, b // 2, out_at + (b % 2) * side), NT)
+                for b in range(4)
+            ],
+            axis=1,
+        )
+        d_query[rows, :] = (d_gated * inner).astype(low)
+        d_inner = d_gated * query_here
+        add_sum(4, d_inner * kv_here)
+        d_inner = d_inner.astype(low)
+        for s in range(per_step):
+            for h in range(2):
+                d_inner_out[2 * (step * per_step + s) + h] = d_inner[
+                    s * row_len : (s + 1) * row_len, h * width : (h + 1) * width
+                ]
+
+    for b in range(4):
+        lanes = slice(b * quarter, (b + 1) * quarter)
+        at = (b % 2) * quarter
+        half = b // 2
+        mine = slice(b * side, (b + 1) * side)
+
+        def put(first, values):
+            first -= out_at
+            grads[half, :, first : first + values.shape[1]] = values.astype(low)
+
+        put(out_at + (b % 2) * side, mul(gated_all[:, mine], d_branch_all[:, mine], TN))
+        put(gate_at + at, mul(normed_all[:, mine], d_gate_all[:, lanes], TN))
+        put(up_at + at, mul(normed_all[:, mine], d_up_all[:, lanes], TN))
+        tall = mul(active_all[:, lanes], d_down_all[:, mine], TN)
+        for i in range(4):
+            put(down_at + at + i * side, tall[i * side : (i + 1) * side, :])
+
+
+def layer_call(conv, query, kv, x, cotangent, vectors, packed):
+    tokens, model = x.shape
+    _, side, width = packed.shape
+    low = jnp.bfloat16
+    shape = jax.ShapeDtypeStruct
+    hidden = 16 * side
+    return plain_call(
+        layer_kernel,
+        "layer",
+        (
+            shape((tokens, model), low),
+            shape((tokens, model), jnp.float32),
+            shape(kv.shape, low),
+            shape((tokens, model), low),
+            shape((2, side, width - 6 * side), low),
+            shape((8, model), jnp.float32),
+        ),
+        [pltpu.VMEM((tokens, model), low)] * 4
+        + [pltpu.VMEM((tokens, hidden), low)] * 3
+        + [pltpu.VMEM((4, 4 * side, side), low)],
+    )(conv, query, kv, x, cotangent, vectors, packed)
+
+
+def input_kernel(d_conv, d_inner, d_query, key, value, x, d_first, vectors, packed, in_grad, grads, d_qkv):
+    wide, low = jnp.float32, jnp.bfloat16
+    side = packed.shape[1]
+    row_len, width = d_conv.shape[1:]
+    model = x.shape[1]
+    d_qkv[:, :model] = d_query[...]
+    for s in range(d_conv.shape[0] // 2):
+        rows = slice(s * row_len, (s + 1) * row_len)
+        for h in range(2):
+            lanes = slice(h * width, (h + 1) * width)
+            cell = 2 * s + h
+            d_kv = d_conv[cell].astype(wide) + vectors[4:5, lanes] * d_inner[cell].astype(wide)
+            d_qkv[rows, model + h * width : model + (h + 1) * width] = (
+                d_kv * value[rows, lanes].astype(wide)
+            ).astype(low)
+            d_qkv[rows, 2 * model + h * width : 2 * model + (h + 1) * width] = (
+                d_kv * key[rows, lanes].astype(wide)
+            ).astype(low)
+    per_block = 3 * side
+    for b in range(4):
+        mine = slice(b * side, (b + 1) * side)
+        here = d_qkv[:, b * per_block : (b + 1) * per_block]
+        at = (b % 2) * per_block
+        weights = packed[b // 2, :, at : at + per_block]
+        in_grad[:, mine] = d_first[:, mine] + mul(here, weights, NT)
+        grads[b // 2, :, at : at + per_block] = mul(x[:, mine], here, TN).astype(low)
+
+
+def adam(weight, moment, second, average, gradient, rate, decay):
+    moment = beta_one * moment + (1.0 - beta_one) * gradient
+    second = beta_two * second + (1.0 - beta_two) * gradient * gradient
+    moment = moment * (1.0 / (1.0 - beta_one**STEP))
+    root = jnp.sqrt(second * (1.0 / (1.0 - beta_two**STEP)))
+    weight = weight - rate * (moment / (root + adam_eps) + decay * weight)
+    return (second, weight, keep_rate * average + (1.0 - keep_rate) * weight)
+
+
+def adam_kernel(scale, used, reduced, extra, *refs):
+    step = pl.program_id(0)
+    per_step, side, _ = refs[0].shape
+    tile_in, small_in, tile_out, small_out = refs[:4], refs[4:16], refs[16:20], refs[20:32]
+    for k in range(per_step):
+        keep = used[step * per_step + k] > 0
+        gradient = reduced[:, k * side : (k + 1) * side].astype(jnp.float32) * scale
+        tile_out[0][k] = gradient
+        fresh = adam(*(ref[k] for ref in tile_in), gradient, 0.1, 0.01)
+        for ref, values in zip(tile_out[1:], fresh):
+            ref[k] = jnp.where(keep, values, 0.0)
+
+    @pl.when(step == 0)
+    def _():
+        order, model = small_in[8].shape
+        width = model // 2
+        count = small_in[0].shape[0]
+        features = small_in[4].shape[0]
+        sums = extra[...].astype(jnp.float32) * scale
+        both = (sums[:, :width], sums[:, width:])
+        first = order + 8
+        gradients = (
+            jnp.concatenate([part[order : order + count] for part in both], axis=1),
+            both[0][first : first + features, :order],
+            jnp.concatenate([part[:order] for part in both], axis=1),
+        )
+        rates = ((0.4, 0.0), (0.4, 0.01), (0.1, 0.01))
+        for i, (gradient, rate) in enumerate(zip(gradients, rates)):
+            small_out[4 * i][...] = gradient
+            fresh = adam(*(ref[...] for ref in small_in[4 * i : 4 * i + 4]), gradient, *rate)
+            for ref, values in zip(small_out[4 * i + 1 : 4 * i + 4], fresh):
+                ref[...] = values
+
+
+def adam_call(scale, used, reduced, tile_state, small_state):
+    slots, side, _ = tile_state[0].shape
+    model = small_state[0].shape[1]
+    per_step = 2
+    tile = pl.BlockSpec((per_step, side, side), lambda i: (i, 0, 0))
+    small = [pl.BlockSpec(a.shape, lambda i: (0, 0)) for a in small_state]
+    shape = jax.ShapeDtypeStruct
+    return pl.pallas_call(
+        functools.partial(adam_kernel, scale),
+        grid=(slots // per_step,),
+        out_shape=tuple(shape(a.shape, a.dtype) for a in tile_state + small_state),
+        in_specs=[
+            SMEM,
+            pl.BlockSpec((side, per_step * side), lambda i: (0, i)),
+            pl.BlockSpec((side, model), lambda i: (0, slots * side // model)),
+        ]
+        + [tile] * 4
+        + small,
+        out_specs=[tile] * 4 + small,
+        compiler_params=pltpu.CompilerParams(vmem_limit_bytes=VMEM_LIMIT),
+        name="adam",
+    )(used, reduced, reduced, *tile_state, *small_state)
+
+
 def on_device_columns(
     tokens,
     cotangent,
@@ -817,205 +1250,102 @@
     out_average,
 ):
     seq_count, dev_rows, row_len, model_width = tokens.shape
-    owner_cap = tile_master.shape[0]
+    owner_cap, side, _ = tile_master.shape
     seq_devices = lax.axis_size("seq")
     grid_rows = dev_rows * seq_devices
     length = grid_rows * row_len
     seq_index = lax.axis_index("seq")
-    hidden_ratio = FF // D
-    quarter_hidden = FF // 4
+    width = model_width // 2
+    low, wide = jnp.bfloat16, jnp.float32
+    shape = jax.ShapeDtypeStruct
+    count = seq_count * row_len
+    order = filter_in.shape[1]
+    table_host = real_table(grid_rows, row_len)
+    table, table_back = jnp.asarray(table_host), jnp.asarray(np.ascontiguousarray(table_host.T))
+    features, channels = (
+        jnp.asarray(a) for a in filter_constants(grid_rows, row_len, model_width)
+    )
     slot_of_tile, tile_of_slot, slot_used = slot_maps(owners, owner_cap, owner_cap * seq_devices)
-    packed = gather_weights(owners, tile_master)
-    side = tile_master.shape[1]
-    lanes = 2 * side
-
-    def blocks_of(first, per_block):
-        part = packed[:, :, first * lanes : (first + per_block) * lanes]
-        part = part.reshape(2, side, 2, per_block * side).transpose(0, 2, 1, 3)
-        return part.reshape(4, side, per_block * side)
-
-    w_in, w_out = blocks_of(0, 3), blocks_of(3, 1)
-    w_gate_up = jnp.concatenate([blocks_of(4, 4), blocks_of(8, 4)], axis=2)
-    w_down = blocks_of(12, 4).reshape(4, side, 4, side).transpose(0, 2, 1, 3)
-    w_down = w_down.reshape(4, 4 * side, side)
-    halves = seq_devices // seq_count
-    width = model_width // halves
-    half_index = lax.rem(seq_index, halves)
-    grid_position = (
-        jnp.arange(grid_rows, dtype=jnp.int32)[:, None]
-        + grid_rows * jnp.arange(row_len, dtype=jnp.int32)[None, :]
-    )
-    position = grid_position.reshape(-1).astype(jnp.float32)
-    table = jnp.asarray(real_table(grid_rows, row_len))
-    first_bin = (jnp.arange(length // 2) == 0)[:, None]
-
-    def spread(field_in):
-        cells = field_in.reshape(seq_count, row_len, halves, width).transpose(0, 2, 1, 3)
-        cells = cells.reshape(seq_devices, row_len, width).astype(jnp.bfloat16)
-        return lax.all_to_all(cells, "seq", 0, 0, tiled=True).reshape(length, width)
-
-    def collect(field_in):
-        cells = field_in.astype(jnp.bfloat16).reshape(seq_devices, row_len, width)
-        cells = lax.all_to_all(cells, "seq", 0, 0, tiled=True)
-        cells = cells.reshape(seq_count, halves, row_len, width).transpose(0, 2, 1, 3)
-        return cells.reshape(-1, model_width).astype(jnp.float32)
-
-    def transform(columns):
-        spec = jnp.dot(table, columns.astype(jnp.bfloat16), preferred_element_type=jnp.float32)
-        return (spec[: length // 2], spec[length // 2 :])
-
-    def invert(real_part, imag_part):
-        weight = jnp.where(first_bin, 1.0 / length, 2.0 / length)
-        spec = jnp.concatenate([real_part * weight, imag_part * weight], axis=0)
-        return lax.dot_general(
-            table,
-            spec.astype(jnp.bfloat16),
-            (((0,), (0,)), ((), ())),
-            preferred_element_type=jnp.float32,
-        )
-
-    def product(one, two, conjugate):
-        one_real, one_imag = one
-        two_real, two_imag = two
-        cross = jnp.where(first_bin, 0.0, two_imag) * (-1.0 if conjugate else 1.0)
-        diag = jnp.where(first_bin, two_imag, two_real)
-        return (one_real * two_real - one_imag * cross, one_real * cross + one_imag * diag)
-
-    flat_tokens = tokens.reshape(-1, model_width)
-    qkv_all = block_apply(flat_tokens, w_in)
-    query_part = qkv_all[:, :model_width]
-    key_part = qkv_all[:, model_width : 2 * model_width]
-    value_part = qkv_all[:, 2 * model_width :]
-    kv_product = key_part * value_part
-
-    channel = half_index * width + jnp.arange(width, dtype=jnp.int32)
-    own_filter = lax.dynamic_slice_in_dim(filter_out, half_index * width, width, 1)
-
-    def own_taps(weight_one, weight_two):
-        return filter_taps_of(weight_one, weight_two, position, length, channel)
-
-    taps_own, filter_pull = jax.vjp(own_taps, filter_in, own_filter)
-    taps_spec = transform(taps_own)
-    kv_spec = transform(spread(kv_product))
-    conv_out = collect(invert(*product(kv_spec, taps_spec, False)))
-    skip_gain = vectors[4]
-    inner_sum = conv_out + skip_gain * kv_product
-    gated_out = (query_part * inner_sum).astype(jnp.bfloat16)
-    branch = block_apply(gated_out, w_out)
-    normed, first_pull = jax.vjp(
-        norm_rows, flat_tokens.astype(jnp.float32) + branch, vectors[0], vectors[1]
-    )
-    normed_low = normed.astype(jnp.bfloat16)
-    gate_up = block_apply(normed_low, w_gate_up).reshape(-1, 4, 2, quarter_hidden)
-    gate_value = gate_up[:, :, 0].reshape(-1, FF)
-    up_value = gate_up[:, :, 1].reshape(-1, FF)
-    active, active_pull = jax.vjp(glu_act, gate_value, up_value)
-    active_low = active.astype(jnp.bfloat16)
-    down_value = block_apply(active_low, w_down)
-    result, second_pull = jax.vjp(
-        norm_rows, normed_low.astype(jnp.float32) + down_value, vectors[2], vectors[3]
-    )
-    output = result.astype(jnp.bfloat16).reshape(tokens.shape)
-    d_second, d_gain_two, d_bias_two = second_pull(
-        cotangent.reshape(-1, model_width).astype(jnp.float32)
-    )
-    d_down = d_second.astype(jnp.bfloat16)
-    g_down = block_grad(active_low, d_down, hidden_ratio, 1)
-    d_gate, d_up = active_pull(block_back(d_down, w_down))
-    d_gate_up = jnp.stack(
-        [d_gate.reshape(-1, 4, quarter_hidden), d_up.reshape(-1, 4, quarter_hidden)], axis=2
-    )
-    d_gate_up = d_gate_up.reshape(-1, 2 * FF).astype(jnp.bfloat16)
-    gate_up_tiles = block_grad(normed_low, d_gate_up, 1, 2 * hidden_ratio).reshape(
-        4, 2, hidden_ratio, side, side
-    )
-    g_gate = gate_up_tiles[:, 0].reshape(-1, side, side)
-    g_up = gate_up_tiles[:, 1].reshape(-1, side, side)
-    d_normed = d_second + block_back(d_gate_up, w_gate_up)
-    d_first, d_gain_one, d_bias_one = first_pull(d_normed)
-    d_branch = d_first.astype(jnp.bfloat16)
-    g_out = block_grad(gated_out, d_branch, 1, 1)
-    d_gated = block_back(d_branch, w_out)
-    d_query = d_gated * inner_sum
-    d_inner = d_gated * query_part
-    d_skip = jnp.sum(d_inner * kv_product, axis=0)
-    back_spec = transform(spread(d_inner))
-    d_kv = collect(invert(*product(back_spec, taps_spec, True))) + skip_gain * d_inner
-    d_qkv = jnp.concatenate([d_query, d_kv * value_part, d_kv * key_part], axis=1).astype(
-        jnp.bfloat16
-    )
-    g_in = block_grad(flat_tokens, d_qkv, 1, 3)
-    in_grad = (d_first + block_back(d_qkv, w_in)).reshape(tokens.shape)
-    d_taps = invert(*product(back_spec, kv_spec, True))
-    g_filter_in, g_filter_half = filter_pull(d_taps)
-    def pack(tiles):
-        per_half = tiles.shape[0] // 2
-        return tiles.reshape(2, per_half, side, side).transpose(0, 2, 1, 3).reshape(2, side, -1)
-
-    slot_mask = slot_used.astype(jnp.float32)[:, None, None]
     first_slot = seq_index * owner_cap
-    vector_part = jnp.stack([d_gain_one, d_bias_one, d_gain_two, d_bias_two, d_skip])
-    order = filter_in.shape[1]
-    both = jnp.zeros((2, side, width), jnp.float32)
-    both = lax.dynamic_update_slice(both, g_filter_half[None], (half_index, 0, 0))
-    both = lax.dynamic_update_slice(
-        both, vector_part.reshape(5, 2, width).transpose(1, 0, 2), (0, order, 0)
-    )
-    both = lax.dynamic_update_slice(both, g_filter_in[None], (0, order + 8, 0))
-    packed_grads = jnp.concatenate(
-        [pack(g).astype(jnp.bfloat16) for g in (g_in, g_out, g_gate, g_up, g_down, )]
-        + [both.astype(jnp.bfloat16)],
-        axis=2,
-    )
     own_tile = lax.dynamic_slice_in_dim(tile_of_slot, first_slot, owner_cap, 0)
     own_used = lax.dynamic_slice_in_dim(slot_used.astype(jnp.int32), first_slot, owner_cap, 0)
-    reduced = reduce_grads(own_tile, own_used, packed_grads).astype(jnp.float32)
-    owned = reduced[:, : owner_cap * side].reshape(side, owner_cap, side).transpose(1, 0, 2)
-    extra = reduced[:, owner_cap * side :].reshape(side, 2, width).transpose(1, 0, 2)
-    out_sum = extra[:, :order].transpose(1, 0, 2).reshape(order, model_width)
-    vector_sum = extra[:, order : order + 5].transpose(1, 0, 2).reshape(5, model_width)
-    in_sum = extra[0, order + 8 : order + 13, :order]
-    tokens_all = seq_count * dev_rows * row_len * lax.axis_size("dp") * seq_devices
-    grad_scale = 1.0 / math.sqrt(tokens_all)
-    mine_mask = lax.dynamic_slice_in_dim(slot_mask, seq_index * owner_cap, owner_cap, 0)
-    tile_grad = owned * grad_scale
-    tile_new = adam_step(tile_master, tile_moment, tile_second, tile_average, tile_grad, 0.1, 0.01)
-    vector_grad = vector_sum * grad_scale
-    in_grad_filter = in_sum * grad_scale
-    out_grad_filter = out_sum * grad_scale
-    vector_new = adam_step(
-        vectors, vector_moment, vector_second, vector_average, vector_grad, 0.4, 0.0
-    )
-    in_new = adam_step(filter_in, in_moment, in_second, in_average, in_grad_filter, 0.4, 0.01)
-    out_new = adam_step(filter_out, out_moment, out_second, out_average, out_grad_filter, 0.1, 0.01)
-    return (
-        output,
-        in_grad,
-        tile_grad,
-        tile_new[0] * mine_mask,
-        tile_new[1] * mine_mask,
-        tile_new[2] * mine_mask,
-        vector_grad,
-        vector_new[0],
-        vector_new[1],
-        vector_new[2],
-        in_grad_filter,
-        in_new[0],
-        in_new[1],
-        in_new[2],
-        out_grad_filter,
-        out_new[0],
-        out_new[1],
-        out_new[2],
-    )
+    packed = gather_weights(owners, tile_master)
+    x = tokens.reshape(count, model_width)
+    cell_shape = (seq_devices, row_len, width)
+    taps_spec = plain_call(taps_kernel, "taps", shape((length, width), wide))(
+        features, channels, filter_in, filter_out, table
+    )
+    query, key, value, kv = plain_call(
+        qkv_kernel, "qkv", (shape(x.shape, low),) * 3 + (shape(cell_shape, low),)
+    )(x, packed)
+
+    def exchange(cells):
+        return lax.all_to_all(cells, "seq", 0, 0, tiled=True)
+
+    conv, kv_spec = plain_call(
+        conv_kernel, "conv", (shape(cell_shape, low), shape((length, width), wide))
+    )(exchange(kv), table, table_back, taps_spec)
+    output, d_first, d_inner, d_query, grads, sums = layer_call(
+        exchange(conv), query, kv, x, cotangent.reshape(count, model_width), vectors, packed
+    )
+    d_conv, grad_out, grad_in = plain_call(
+        conv_back_kernel,
+        "conv_back",
+        (shape(cell_shape, low), shape((order, width), wide), shape((8, order), wide)),
+    )(
+        exchange(d_inner),
+        table,
+        table_back,
+        taps_spec,
+        kv_spec,
+        features,
+        channels,
+        filter_in,
+        filter_out,
+    )
+    in_grad, grads_in = plain_call(
+        input_kernel,
+        "input_grad",
+        (shape(x.shape, wide), shape((2, side, 6 * side), low)),
+        [pltpu.VMEM((count, 3 * model_width), low)],
+    )(exchange(d_conv), d_inner, d_query, key, value, x, d_first, vectors, packed)
+    both = jnp.zeros((2, side, width), wide)
+    both = lax.dynamic_update_slice(both, grad_out[None], (lax.rem(seq_index, 2), 0, 0))
+    both = lax.dynamic_update_slice(
+        both, sums.reshape(8, 2, width).transpose(1, 0, 2), (0, order, 0)
+    )
+    both = lax.dynamic_update_slice(both, grad_in[None], (0, order + 8, 0))
+    packed_grads = jnp.concatenate([grads_in, grads, both.astype(low)], axis=2)
+    reduced = reduce_grads(own_tile, own_used, packed_grads)
+    tokens_all = count * lax.axis_size("dp") * seq_devices
+    updated = adam_call(
+        1.0 / math.sqrt(tokens_all),
+        own_used,
+        reduced,
+        (tile_master, tile_moment, tile_second, tile_average),
+        (
+            vectors,
+            vector_moment,
+            vector_second,
+            vector_average,
+            filter_in,
+            in_moment,
+            in_second,
+            in_average,
+            filter_out,
+            out_moment,
+            out_second,
+            out_average,
+        ),
+    )
+    return (output.reshape(tokens.shape), in_grad.reshape(tokens.shape), *updated)
 
 
 def on_device(*arrays):
     seq_count, dev_rows, row_len, model_width = arrays[0].shape
     seq_devices = lax.axis_size("seq")
-    fits = dev_rows == 1 and seq_devices % seq_count == 0 and seq_devices * row_len <= 2048
-    fits = fits and lax.axis_size("dp") == 4 and seq_devices == 2 * seq_count == 8
-    if fits and model_width % (128 * (seq_devices // seq_count)) == 0:
+    fits = dev_rows == 1 and lax.axis_size("dp") == 4 and seq_devices == 2 * seq_count == 8
+    if fits and row_len == 128 and model_width % 256 == 0:
         return on_device_columns(*arrays)
     return on_device_general(*arrays)
 

time: 443 us -> 287 us (0.65); the launches traced: 436 us -> 287 us
  local copies, waits for them, and re-layouts: 136 us -> 4.64 us
  other arithmetic: 79.8 us -> 3.96 us
  Pallas kernels: 115 us -> 188 us
  matrix products: 69.6 us -> 0 us
  blocking collectives: 0 us -> 50.3 us
  waiting for transfers between devices: 14.3 us -> 31.9 us
  starting transfers between devices: 18.9 us -> 7.09 us
    pallas_call x0 -> x7, Pallas kernels: none -> 72.8 us  [the longest x6 57.1 us: call(): pl.pallas_call(kernel, out_shape=out_shape, in_specs=[VMEM] * len(arrays)...]
    dot_general x26 -> x0, matrix products: 69.6 us -> none  [the longest x4 25.3 us: block_back(): jnp.einsum('nbo,bio->nbi', row_view, blocks, preferred_element_type=jnp.f...]
    all_to_all x0 -> x2, blocking collectives: none -> 50.3 us  [exchange(): return lax.all_to_all(cells, 'seq', 0, 0, tiled=True)]
    convert_element_type x23 -> x0, local copies, waits for them, and re-layouts: 39.5 us -> none  [the longest x13 20.1 us: on_device_columns(): pack(g).astype(jnp.bfloat16)]
    reshape x13 -> x0, local copies, waits for them, and re-layouts: 26.1 us -> none  [the longest x4 9.79 us: block_apply(): jnp.einsum('nbi,bio->nbo', row_view, blocks, preferred_element_type=jnp.f...]
    mul x6 -> x0, other arithmetic: 23.3 us -> none  [the longest x2 13.6 us: on_device_columns(): tile_new[2] * mine_mask]
    unnamed x260 -> x10, local copies, waits for them, and re-layouts: 23.9 us -> 1.77 us
    convert_element_type x6 -> x0, other arithmetic: 18.8 us -> none  [the longest x1 14.4 us: on_device_columns(): active_low = active.astype(jnp.bfloat16)]
  transfers between devices with their start and end apart: 4 -> 2, of which waited for: 2 -> 2; matrix products, arithmetic and copies ran while one was open for 21% -> 1% of each run, Pallas kernels for 0% -> 2%
where the time goes in v4:
time: 287 us
  Pallas kernels  188 us (66%)
  blocking collectives  50.3 us (18%)
  waiting for transfers between devices  31.9 us (11%)
  starting transfers between devices  7.09 us (2%)
  local copies, waits for them, and re-layouts  4.64 us (2%)
  other arithmetic  3.96 us (1%)
    pallas_call x1, Pallas kernels, reduce_grads(): pl.pallas_call(functools.partial(reduce_kernel, chunks), out_shape=jax.Sh...  67.5 us
    pallas_call x6, Pallas kernels, call(): pl.pallas_call(kernel, out_shape=out_shape, in_specs=[VMEM] * len(arrays)...  57.1 us
    all_to_all x2, blocking collectives, exchange(): return lax.all_to_all(cells, 'seq', 0, 0, tiled=True)  50.3 us
    pallas_call x1, Pallas kernels, gather_weights(): pl.pallas_call(functools.partial(gather_kernel, chunks), out_shape=jax.Sh...  47.3 us
    all_to_all x2, waiting for transfers between devices, exchange(): return lax.all_to_all(cells, 'seq', 0, 0, tiled=True)  31.9 us
    pallas_call x1, Pallas kernels, adam_call(): pl.pallas_call(functools.partial(adam_kernel, scale), grid=(slots // per_...  15.7 us
    all_to_all x2, starting transfers between devices, exchange(): return lax.all_to_all(cells, 'seq', 0, 0, tiled=True)  7.09 us
  transfers between devices with their start and end apart: 2, of which 2 were waited for; matrix products, arithmetic and copies ran while one was open for 1% of the time, Pallas kernels for 2%

profile of v4, /device:TPU:0, one launch (start us, length us, event | category | flops | bytes accessed | tf_op | source)
XLA Modules:
  0.0 286.5 jit_solution(18217435092808495551)
XLA Ops:
  0.7 47.3 %gather_weights.1.packed = bf16[2,192,6144]{2,1,0:T(8,128)(2,1)} custom-call(s32[64]{0:T(128)} %owners.1, f32[16,192,192]{2,1,0:T(8,128)} %refs_0_.1), custom_call_target="tpu_custom_call" | custom-call | tf_op jit(solution)/shard_map/gather_weights/pallas_call | solution.py:612
  47.9 5.0 %qkv.1 = (bf16[512,768]{1,0:T(8,128)(2,1)}, bf16[512,768]{1,0:T(8,128)(2,1)}, bf16[512,768]{1,0:T(8,128)(2,1)}, bf16[8,128,384]{2,1,0:T(8,128)(2,1)}) custom-call(bf16[512,768]{1,0:T(8,128)(2,1)} %bitcast.15, bf16[2,192,6144]{2,1,0:T(8,128)(2,1)} %gather_weights.1.packed), custom_call_target="tpu_custom_call" | custom-call | tf_op jit(solution)/shard_map/qkv/pallas_call | solution.py:811
  52.9 3.5 %all-to-all-start = ((bf16[8,128,384]{2,1,0:T(8,128)(2,1)}), bf16[8,128,384]{2,1,0:T(8,128)(2,1)S(1)}, u32[]{:S(2)}, u32[]{:S(2)}) async-start(bf16[8,128,384]{2,1,0:T(8,128)(2,1)} %get-tuple-element.51.kv), calls=%async_computation | async-start | bytes 1572864 | tf_op jit(solution)/shard_map/all_to_all | solution.py:1283
  56.4 6.5 %taps.1.taps_spec = f32[1024,384]{1,0:T(8,128)} custom-call(f32[1024,8]{1,0:T(8,128)} %constant.33.clone.features, f32[2,768]{1,0:T(2,128)} %constant.34.clone.channels, f32[5,128]{1,0:T(8,128)} %refs_8_.1, f32[128,768]{1,0:T(8,128)} %refs_12_.1, bf16[1024,1024]{1,0:T(8,128)(2,1)} %constant.31.clone.table), custom_call_target="tpu_custom_call" | custom-call | tf_op jit(solution)/shard_map/taps/pallas_call | solution.py:811
  63.0 14.3 %all-to-all-done.cells = bf16[8,128,384]{2,1,0:T(8,128)(2,1)S(1)} async-done(((bf16[8,128,384]{2,1,0:T(8,128)(2,1)}), bf16[8,128,384]{2,1,0:T(8,128)(2,1)S(1)}, u32[]{:S(2)}, u32[]{:S(2)}) %all-to-all-start) | async-done | bytes 786464 | tf_op jit(solution)/shard_map/all_to_all | solution.py:1283
  77.3 0.0 copy-start.2
  77.3 0.9 copy-done.2
  78.2 6.3 %conv.1 = (bf16[8,128,384]{2,1,0:T(8,128)(2,1)}, f32[1024,384]{1,0:T(8,128)}) custom-call(bf16[8,128,384]{2,1,0:T(8,128)(2,1)} %copy-done.2, bf16[1024,1024]{1,0:T(8,128)(2,1)} %constant.31.clone.table, bf16[1024,1024]{1,0:T(8,128)(2,1)} %constant.32.clone.table_back, f32[1024,384]{1,0:T(8,128)} %taps.1.taps_spec), custom_call_target="tpu_custom_call" | custom-call | tf_op jit(solution)/shard_map/conv/pallas_call | solution.py:811
  84.5 25.2 %all_to_all.20.conv = bf16[8,128,384]{2,1,0:T(8,128)(2,1)} all-to-all(bf16[8,128,384]{2,1,0:T(8,128)(2,1)} %get-tuple-element.52), channel_id=1, replica_groups=mesh['dp'=4,'seq'=8] {'seq'}, dimensions={0} | all-to-all | bytes 1572864 | tf_op jit(solution)/shard_map/all_to_all | solution.py:1283
  109.7 21.7 %layer.1 = (bf16[512,768]{1,0:T(8,128)(2,1)}, f32[512,768]{1,0:T(8,128)}, bf16[8,128,384]{2,1,0:T(8,128)(2,1)}, bf16[512,768]{1,0:T(8,128)(2,1)}, bf16[2,192,4992]{2,1,0:T(8,128)(2,1)}, /*index=5*/f32[8,768]{1,0:T(8,128)}) custom-call(bf16[8,128,384]{2,1,0:T(8,128)(2,1)} %all_to_all.20.conv, bf16[512,768]{1,0:T(8,128)(2,1)} %get-tuple-element.53.query, ...), custom_call_target="tpu_custom_call" | custom-call | tf_op jit(solution)/shard_map/layer/pallas_call | solution.py:811
  131.4 25.2 %all_to_all.21.cells = bf16[8,128,384]{2,1,0:T(8,128)(2,1)} all-to-all(bf16[8,128,384]{2,1,0:T(8,128)(2,1)} %get-tuple-element.55.d_inner), channel_id=1, replica_groups=mesh['dp'=4,'seq'=8] {'seq'}, dimensions={0} | all-to-all | bytes 1572864 | tf_op jit(solution)/shard_map/all_to_all | solution.py:1283
  156.6 0.0 copy-start.4
  156.6 0.0 copy-start.3
  156.6 10.0 %conv_back.1 = (bf16[8,128,384]{2,1,0:T(8,128)(2,1)}, f32[128,384]{1,0:T(8,128)}, f32[8,128]{1,0:T(8,128)}) custom-call(bf16[8,128,384]{2,1,0:T(8,128)(2,1)} %all_to_all.21.cells, bf16[1024,1024]{1,0:T(8,128)(2,1)} %constant.31.clone.table, bf16[1024,1024]{1,0:T(8,128)(2,1)} %constant.32.clone.table_back, f32[1024,384]{1,0:T(8,128)} %taps.1.taps_spec, ...), custom_call_target="tpu_custom_call" | custom-call | tf_op jit(solution)/shard_map/conv_back/pallas_call | solution.py:811
  166.5 3.5 %all-to-all-start.3 = ((bf16[8,128,384]{2,1,0:T(8,128)(2,1)}), bf16[8,128,384]{2,1,0:T(8,128)(2,1)S(1)}, u32[]{:S(2)}, u32[]{:S(2)}) async-start(bf16[8,128,384]{2,1,0:T(8,128)(2,1)} %get-tuple-element.57), calls=%async_computation.3 | async-start | bytes 1572864 | tf_op jit(solution)/shard_map/all_to_all | solution.py:1283
  170.1 0.0 copy-done.4
  170.1 0.2 convert_reduce_fusion
  170.3 0.1 fusion
  170.4 0.6 dynamic_slice.6.used
  171.0 0.1 select_reduce_fusion
  171.1 0.6 dynamic_slice.7.tile_of_slot
  171.7 1.0 bitcast_dynamic-update-slice_fusion
  172.7 0.0 copy-done.3
  172.7 0.7 bitcast_dynamic-update-slice_fusion.1
  173.4 17.6 %all-to-all-done.3.d_conv = bf16[8,128,384]{2,1,0:T(8,128)(2,1)S(1)} async-done(((bf16[8,128,384]{2,1,0:T(8,128)(2,1)}), bf16[8,128,384]{2,1,0:T(8,128)(2,1)S(1)}, u32[]{:S(2)}, u32[]{:S(2)}) %all-to-all-start.3) | async-done | bytes 786464 | tf_op jit(solution)/shard_map/all_to_all | solution.py:1283
  191.0 0.0 copy-start.1
  191.0 0.9 copy-done.1
  191.9 0.0 copy-start
  191.9 7.6 %input_grad.1 = (f32[512,768]{1,0:T(8,128)}, bf16[2,192,1152]{2,1,0:T(8,128)(2,1)}) custom-call(bf16[8,128,384]{2,1,0:T(8,128)(2,1)} %copy-done.1, bf16[8,128,384]{2,1,0:T(8,128)(2,1)} %get-tuple-element.55.d_inner, bf16[512,768]{1,0:T(8,128)(2,1)} %get-tuple-element.58.d_query, bf16[512,768]{1,0:T(8,128)(2,1)} %get-tuple-element.59.key, ...), custom_call_target="tpu_custom_call" | custom-call | tf_op jit(solution)/shard_map/input_grad/pallas_call | solution.py:811
  199.5 0.0 copy-done
  199.5 3.6 %pad_maximum_fusion.grads = bf16[2,192,6528]{2,1,0:T(8,128)(2,1)} fusion(bf16[2,192,384]{2,1,0:T(8,128)(2,1)S(1)} %bitcast_dynamic-update-slice_fusion.1, bf16[2,192,4992]{2,1,0:T(8,128)(2,1)S(1)} %copy-done, bf16[2,192,1152]{2,1,0:T(8,128)(2,1)} %get-tuple-element.63), kind=kLoop, calls=%fused_computation | loop fusion | flops 15040512 | bytes 10027008 | tf_op jit(solution)/shard_map/concatenate | solution.py:1318
  203.1 67.5 %reduce_grads.1.reduced.extra = bf16[192,3840]{1,0:T(8,128)(2,1)} custom-call(s32[16]{0:T(128)} %dynamic_slice.7.tile_of_slot, s32[16]{0:T(128)} %dynamic_slice.6.used, bf16[2,192,6528]{2,1,0:T(8,128)(2,1)} %pad_maximum_fusion.grads), custom_call_target="tpu_custom_call" | custom-call | tf_op jit(solution)/shard_map/reduce_grads/pallas_call | solution.py:766
  270.6 15.7 %adam.1 = (f32[16,192,192]{2,1,0:T(8,128)}, f32[16,192,192]{2,1,0:T(8,128)}, f32[16,192,192]{2,1,0:T(8,128)}, f32[16,192,192]{2,1,0:T(8,128)}, f32[5,768]{1,0:T(...) custom-call(s32[16]{0:T(128)} %dynamic_slice.6.used, ...), custom_call_target="tpu_custom_call" | custom-call | tf_op jit(solution)/shard_map/adam/pallas_call | solution.py:1214
  (4 shorter events, 0.0 us)
Async XLA Ops:
  52.9 24.4 %all-to-all-start = ((bf16[8,128,384]{2,1,0:T(8,128)(2,1)}), bf16[8,128,384]{2,1,0:T(8,128)(2,1)S(1)}, u32[]{:S(2)}, u32[]{:S(2)}) async-start(bf16[8,128,384]{2,1,0:T(8,128)(2,1)} %get-tuple-element.51.kv), calls=%async_computation | async-start | bytes 1572864 | tf_op jit(solution)/shard_map/all_to_all | solution.py:1283
  77.3 0.9 copy-start.2
  156.6 13.5 %copy-start.4 = (s32[64]{0:T(128)S(1)}, s32[64]{0:T(128)}, u32[]{:S(2)}) copy-start(s32[64]{0:T(128)} %owners.1) | copy-start | bytes 772
  156.6 16.1 %copy-start.3 = (f32[8,768]{1,0:T(8,128)S(1)}, f32[8,768]{1,0:T(8,128)}, u32[]{:S(2)}) copy-start(f32[8,768]{1,0:T(8,128)} %get-tuple-element.66) | copy-start | bytes 73732
  166.5 24.5 %all-to-all-start.3 = ((bf16[8,128,384]{2,1,0:T(8,128)(2,1)}), bf16[8,128,384]{2,1,0:T(8,128)(2,1)S(1)}, u32[]{:S(2)}, u32[]{:S(2)}) async-start(bf16[8,128,384]{2,1,0:T(8,128)(2,1)} %get-tuple-element.57), calls=%async_computation.3 | async-start | bytes 1572864 | tf_op jit(solution)/shard_map/all_to_all | solution.py:1283
  191.0 0.9 copy-start.1
  191.9 7.6 %copy-start = (bf16[2,192,4992]{2,1,0:T(8,128)(2,1)S(1)}, bf16[2,192,4992]{2,1,0:T(8,128)(2,1)}, u32[]{:S(2)}) copy-start(bf16[2,192,4992]{2,1,0:T(8,128)(2,1)} %get-tuple-element.64) | copy-start | bytes 11501572

commit v5 on v4

--- a/solution.py
+++ b/solution.py
@@ -388,6 +388,16 @@
 VMEM_LIMIT = 56 * 2**20
 
 
+def flip(index, bits):
+    at = 1
+    result = index
+    while at <= bits:
+        if bits & at:
+            result = result + at - 2 * at * lax.rem(lax.div(index, at), 2)
+        at *= 2
+    return result
+
+
 class Links:
     def __init__(self, send_sem, recv_sem):
         self.send_sem, self.recv_sem, self.used = send_sem, recv_sem, 0
@@ -410,14 +420,11 @@
 
     def meet(self):
         barrier = pltpu.get_barrier_semaphore()
-        for peer in (self.partner, self.to_near, self.to_far, self.to_inner):
+        peers = [(self.dp, flip(self.seq, bits)) for bits in range(1, 2 * self.deep)]
+        peers += [self.to_near, self.to_far]
+        for peer in peers:
             pl.semaphore_signal(barrier, inc=1, device_id=peer, device_id_type=MESH)
-
-        @pl.when(jnp.logical_not(self.at_end))
-        def _():
-            pl.semaphore_signal(barrier, inc=1, device_id=self.to_outer, device_id_type=MESH)
-
-        pl.semaphore_wait(barrier, jnp.where(self.at_end, 4, 5))
+        pl.semaphore_wait(barrier, len(peers))
 
     def copy(self, source, target, device):
         at = self.used
@@ -514,287 +521,6 @@
     return order
 
 
-def gather_kernel(
-    chunks,
-    owners,
-    master,
-    full,
-    own,
-    got,
-    base,
-    arrived,
-    leaving,
-    send_sem,
-    recv_sem,
-    chain_send,
-    chain_recv,
-):
-    links = Links(send_sem, recv_sem)
-    quarter = full.shape[1] // 4
-    tile_count, side = owners.shape[0], master.shape[2]
-    most = master.shape[0] - 1
-    rows = pl.ds(pl.multiple_of(links.dp * quarter, quarter), quarter)
-    near_rows = pl.ds(pl.multiple_of(links.near * quarter, quarter), quarter)
-    rank, place = jnp.int32(0), []
-    for i in range(tile_count):
-        mine = owners[i] == links.seq
-        place.append((jnp.minimum(rank, most), mine))
-        rank = rank + jnp.where(mine, 1, 0)
-    for half in range(2):
-        order = half_tiles(half)
-        for j in range(0, len(order), 2):
-            pair = []
-            for i in order[j : j + 2]:
-                at, mine = place[i]
-                pair.append(jnp.where(mine, master[at, rows, :], 0.0))
-            own[half, :, j * side : (j + 2) * side] = jnp.concatenate(pair, axis=1).astype(own.dtype)
-    links.meet()
-    swaps, planes = [], []
-    for at in chunks:
-        swaps.append(
-            links.copy(own.at[1 - links.core, :, at], got.at[:, at], links.partner)
-        )
-        mine = full.at[links.core, rows, at]
-        other = full.at[links.core, near_rows, at]
-        both = full.at[links.core, :, at]
-        planes.append(
-            (
-                links.copy(mine, mine, links.to_near),
-                links.copy(mine, mine, links.to_far),
-                links.copy(other, other, links.to_far),
-                links.copy(both, both, links.partner),
-            )
-        )
-        swaps[-1].start()
-    chain = Chain(links, base, arrived, leaving, chain_send, chain_recv, chunks)
-
-    def collect(k):
-        at = chunks[k]
-        swaps[k].wait()
-        base[:, at] = own[links.core, :, at] + got[:, at]
-        chain.begin(k)
-
-    def spread(k):
-        full[links.core, rows, chunks[k]] = chain.inward(k).astype(full.dtype)
-        planes[k][0].start()
-        planes[k][1].start()
-
-    def relay(k):
-        planes[k][0].wait_recv()
-        planes[k][2].start()
-
-    def share(k):
-        planes[k][1].wait_recv()
-        planes[k][2].wait_recv()
-        planes[k][3].start()
-
-    count = len(chunks)
-    for k in range(count):
-        collect(k)
-    for k in range(count + 4):
-        for stage, late in ((chain.outward, 0), (spread, 1), (relay, 2), (share, 4)):
-            if 0 <= k - late < count:
-                stage(k - late)
-    for k in range(count):
-        chain.finish(k)
-        for copy in planes[k][:3]:
-            copy.wait_send()
-        planes[k][3].wait()
-
-
-def gather_weights(owners, master):
-    slots, side, _ = master.shape
-    width = owners.shape[0] // 2 * side
-    chunks = cut(0, 640, 1152, 2816, 4480, width)
-    low = jnp.bfloat16
-    quarter = side // 4
-    count = len(chunks)
-    return pl.pallas_call(
-        functools.partial(gather_kernel, chunks),
-        out_shape=jax.ShapeDtypeStruct((2, side, width), low),
-        in_specs=[
-            pl.BlockSpec(memory_space=pltpu.SMEM),
-            pl.BlockSpec(memory_space=pltpu.VMEM),
-        ],
-        out_specs=pl.BlockSpec(memory_space=pltpu.VMEM),
-        scratch_shapes=[
-            pltpu.VMEM((2, quarter, width), low),
-            pltpu.VMEM((quarter, width), low),
-            pltpu.VMEM((quarter, width), low),
-            pltpu.VMEM((2, quarter, width), low),
-            pltpu.VMEM((2, quarter, width), low),
-            pltpu.SemaphoreType.DMA((5 * count,)),
-            pltpu.SemaphoreType.DMA((5 * count,)),
-            pltpu.SemaphoreType.DMA((2, count)),
-            pltpu.SemaphoreType.DMA((2, count)),
-        ],
-        compiler_params=pltpu.CompilerParams(
-            collective_id=0, has_side_effects=True, vmem_limit_bytes=VMEM_LIMIT
-        ),
-        name="gather_weights",
-    )(owners, master)
-
-
-def reduce_kernel(
-    chunks,
-    tile_of_slot,
-    used,
-    grads,
-    spread,
-    mine_sum,
-    got,
-    near_in,
-    far_in,
-    far_out,
-    base,
-    arrived,
-    leaving,
-    total,
-    by_tile,
-    send_sem,
-    recv_sem,
-    chain_send,
-    chain_recv,
-):
-    links = Links(send_sem, recv_sem)
-    side = grads.shape[1]
-    quarter = side // 4
-    wide = jnp.float32
-
-    def rows_of(index):
-        return pl.ds(pl.multiple_of(index * quarter, quarter), quarter)
-
-    links.meet()
-    swaps, nears, diagonals, fars, shares = [], [], [], [], []
-    for at in chunks:
-        swaps.append(links.copy(grads.at[1 - links.core, :, at], got.at[:, at], links.partner))
-        swaps[-1].start()
-        nears.append(
-            links.copy(mine_sum.at[rows_of(links.near), at], near_in.at[0, :, at], links.to_near)
-        )
-        diagonals.append(
-            links.copy(
-                mine_sum.at[rows_of(links.diagonal), at], near_in.at[1, :, at], links.to_near
-            )
-        )
-        fars.append(links.copy(far_out.at[:, at], far_in.at[:, at], links.to_far))
-        part = total.at[links.core, :, at]
-        shares.append(links.copy(part, part, links.partner))
-    chain = Chain(links, base, arrived, leaving, chain_send, chain_recv, chunks)
-
-    def merge_cores(k):
-        at = chunks[k]
-        swaps[k].wait()
-        mine_sum[:, at] = (
-            grads[links.core, :, at].astype(wide) + got[:, at].astype(wide)
-        ).astype(mine_sum.dtype)
-        diagonals[k].start()
-        nears[k].start()
-
-    def go_far(k):
-        at = chunks[k]
-        diagonals[k].wait_recv()
-        far_out[:, at] = (
-            mine_sum[rows_of(links.far), at].astype(wide) + near_in[1, :, at].astype(wide)
-        ).astype(far_out.dtype)
-        fars[k].start()
-
-    def collect(k):
-        at = chunks[k]
-        nears[k].wait_recv()
-        fars[k].wait_recv()
-        base[:, at] = (
-            mine_sum[rows_of(links.dp), at].astype(wide)
-            + near_in[0, :, at].astype(wide)
-            + far_in[:, at].astype(wide)
-        )
-        chain.begin(k)
-
-    def end(k):
-        total[links.core, :, chunks[k]] = chain.inward(k).astype(total.dtype)
-        shares[k].start()
-
-    count = len(chunks)
-    for k in range(count + 4):
-        stages = ((merge_cores, 0), (go_far, 1), (collect, 2), (chain.outward, 3), (end, 4))
-        for stage, late in stages:
-            if 0 <= k - late < count:
-                stage(k - late)
-    for share in shares:
-        share.wait()
-    for half in range(2):
-        for j, i in enumerate(half_tiles(half)):
-            by_tile[i] = total[half, :, j * side : (j + 1) * side].astype(wide)
-    slots = tile_of_slot.shape[0]
-    tiles_wide = slots * side
-    mine = rows_of(links.dp)
-    for s in range(0, slots, 2):
-        pair = [jnp.where(used[k] > 0, by_tile[tile_of_slot[k]], 0.0) for k in (s, s + 1)]
-        spread[mine, s * side : (s + 2) * side] = jnp.concatenate(pair, axis=1).astype(spread.dtype)
-    first_extra = by_tile.shape[0] // 2 * side
-    extra = total.shape[2] - first_extra
-    for half in range(2):
-        begin = tiles_wide + half * extra
-        spread[mine, begin : begin + extra] = total[half, :, first_extra:]
-    at_home, other = spread.at[mine, :], spread.at[rows_of(links.near), :]
-    first = links.copy(at_home, at_home, links.to_near)
-    second = links.copy(at_home, at_home, links.to_far)
-    relay = links.copy(other, other, links.to_far)
-    first.start()
-    second.start()
-    first.wait_recv()
-    relay.start()
-    second.wait_recv()
-    relay.wait()
-    first.wait_send()
-    second.wait_send()
-    for k in range(count):
-        nears[k].wait_send()
-        diagonals[k].wait_send()
-        fars[k].wait_send()
-        chain.finish(k)
-
-
-def reduce_grads(tile_of_slot, used, grads):
-    _, side, width = grads.shape
-    slots = tile_of_slot.shape[0]
-    extra = width - NTILES // 2 * side
-    chunks = cut(0, 1152, 2304, 3456, 4480, 5504, width)
-    low = jnp.bfloat16
-    quarter = side // 4
-    count = len(chunks)
-    return pl.pallas_call(
-        functools.partial(reduce_kernel, chunks),
-        out_shape=jax.ShapeDtypeStruct((side, slots * side + 2 * extra), low),
-        in_specs=[
-            pl.BlockSpec(memory_space=pltpu.SMEM),
-            pl.BlockSpec(memory_space=pltpu.SMEM),
-            pl.BlockSpec(memory_space=pltpu.VMEM),
-        ],
-        out_specs=pl.BlockSpec(memory_space=pltpu.VMEM),
-        scratch_shapes=[
-            pltpu.VMEM((side, width), low),
-            pltpu.VMEM((side, width), low),
-            pltpu.VMEM((2, quarter, width), low),
-            pltpu.VMEM((quarter, width), low),
-            pltpu.VMEM((quarter, width), low),
-            pltpu.VMEM((quarter, width), jnp.float32),
-            pltpu.VMEM((2, quarter, width), low),
-            pltpu.VMEM((2, quarter, width), low),
-            pltpu.VMEM((2, quarter, width), low),
-            pltpu.VMEM((NTILES, quarter, side), jnp.float32),
-            pltpu.SemaphoreType.DMA((5 * count + 3,)),
-            pltpu.SemaphoreType.DMA((5 * count + 3,)),
-            pltpu.SemaphoreType.DMA((2, count)),
-            pltpu.SemaphoreType.DMA((2, count)),
-        ],
-        compiler_params=pltpu.CompilerParams(
-            collective_id=1, has_side_effects=True, vmem_limit_bytes=VMEM_LIMIT
-        ),
-        name="reduce_grads",
-    )(tile_of_slot, used, grads)
-
-
 VMEM = pl.BlockSpec(memory_space=pltpu.VMEM)
 SMEM = pl.BlockSpec(memory_space=pltpu.SMEM)
 NN = (((1,), (0,)), ((), ()))
@@ -859,31 +585,6 @@
 def half_lanes(width):
     half = lax.rem(lax.axis_index("seq"), 2)
     return pl.ds(pl.multiple_of(half * width, width), width)
-
-
-def taps_kernel(features, channels, filter_in, filter_out, table, spec):
-    length, width = spec.shape
-    lanes = half_lanes(width)
-    hidden = jnp.sin(phases_of(features[...], filter_in[...]))
-    taps = mul(hidden.astype(jnp.bfloat16), filter_out[:, lanes].astype(jnp.bfloat16))
-    taps = (taps * decay_of(features, channels, lanes)).astype(jnp.bfloat16)
-    scale = jnp.where(first_row((length // 2, 1)), 1.0 / length, 2.0 / length)
-    for part in range(2):
-        rows = slice(part * length // 2, (part + 1) * length // 2)
-        spec[rows, :] = mul(table[rows, :], taps) * scale
-
-
-def conv_kernel(cells, table, table_back, taps_spec, out, kv_spec):
-    length, width = kv_spec.shape
-    half = length // 2
-    columns = cells[...].reshape(length, width)
-    real, imag = mul(table[:half], columns), mul(table[half:], columns)
-    kv_spec[:half] = real
-    kv_spec[half:] = imag
-    real, imag = spectrum_product(real, imag, taps_spec[:half], taps_spec[half:], 1.0)
-    result = mul(table_back[:, :half], real.astype(jnp.bfloat16))
-    result += mul(table_back[:, half:], imag.astype(jnp.bfloat16))
-    out[...] = result.astype(out.dtype).reshape(out.shape)
 
 
 def conv_back_kernel(
@@ -924,24 +625,6 @@
 
 def tile_at(packed, half, first):
     return packed[half, :, first : first + packed.shape[1]]
-
-
-def qkv_kernel(x, packed, query, key, value, kv):
-    side = packed.shape[1]
-    count = kv.shape[0] // 2
-    row_len, width = kv.shape[1:]
-    for i in range(12):
-        block, half = i // 3, i // 6
-        part = mul(x[:, block * side : (block + 1) * side], tile_at(packed, half, (i % 6) * side))
-        target = (query, key, value)[i // 4]
-        at = (i % 4) * side
-        target[:, at : at + side] = part.astype(target.dtype)
-    for s in range(count):
-        rows = slice(s * row_len, (s + 1) * row_len)
-        for h in range(2):
-            lanes = slice(h * width, (h + 1) * width)
-            both = key[rows, lanes].astype(jnp.float32) * value[rows, lanes].astype(jnp.float32)
-            kv[2 * s + h] = both.astype(kv.dtype)
 
 
 def normalize(values):
@@ -1228,6 +911,495 @@
     )(used, reduced, reduced, *tile_state, *small_state)
 
 
+class Exchange:
+    def __init__(self, links, cells, columns, send_sem, recv_sem):
+        self.links, self.cells, self.columns = links, cells, columns
+        self.send_sem, self.recv_sem = send_sem, recv_sem
+
+    def copy(self, bits):
+        links = self.links
+        peer = flip(links.seq, bits)
+        return pltpu.make_async_remote_copy(
+            src_ref=self.cells.at[peer],
+            dst_ref=self.columns.at[links.seq],
+            send_sem=self.send_sem.at[bits],
+            recv_sem=self.recv_sem.at[bits],
+            device_id=(links.dp, peer),
+            device_id_type=MESH,
+        )
+
+    def send(self, *bits):
+        for b in bits:
+            if b == 0:
+                me = self.links.seq
+                self.columns[me] = self.cells[me]
+            else:
+                self.copy(b).start()
+
+    def arrived(self, *bits):
+        for b in bits:
+            if b:
+                peer = flip(self.links.seq, b)
+                pltpu.make_async_remote_copy(
+                    src_ref=self.cells.at[peer],
+                    dst_ref=self.columns.at[peer],
+                    send_sem=self.send_sem.at[b],
+                    recv_sem=self.recv_sem.at[b],
+                    device_id=(self.links.dp, peer),
+                    device_id_type=MESH,
+                ).wait_recv()
+
+    def sent(self):
+        for b in range(1, self.cells.shape[0]):
+            self.copy(b).wait_send()
+
+
+def columns_of_chip(columns, chip):
+    pair = columns[pl.ds(2 * chip, 2)]
+    return pair.reshape(2 * pair.shape[1], pair.shape[2])
+
+
+def transform_arrivals(exchange, table, spec):
+    step = 2 * exchange.columns.shape[1]
+    for near in range(exchange.links.deep):
+        exchange.arrived(2 * near, 2 * near + 1)
+        chip = flip(exchange.links.z, near)
+        lanes = pl.ds(pl.multiple_of(chip * step, step), step)
+        part = mul(table[:, lanes], columns_of_chip(exchange.columns, chip))
+        if near:
+            spec[...] += part
+        else:
+            spec[...] = part
+
+
+def send_inverse(exchange, table_back, filtered):
+    row_len = exchange.cells.shape[1]
+    for near in reversed(range(exchange.links.deep)):
+        chip = flip(exchange.links.z, near)
+        rows = pl.ds(pl.multiple_of(chip * 2 * row_len, 2 * row_len), 2 * row_len)
+        part = mul(table_back[rows, :], filtered[...]).astype(exchange.cells.dtype)
+        exchange.cells[pl.ds(2 * chip, 2)] = part.reshape(2, row_len, part.shape[1])
+        exchange.send(2 * near, 2 * near + 1)
+
+
+def forward_kernel(
+    chunks,
+    first_chunks,
+    owners,
+    master,
+    x,
+    features,
+    channels,
+    filter_in,
+    filter_out,
+    table_hbm,
+    table_back_hbm,
+    full,
+    query,
+    key,
+    value,
+    kv,
+    conv,
+    taps_spec,
+    kv_spec,
+    own,
+    got,
+    base,
+    arrived,
+    leaving,
+    table,
+    table_back,
+    hidden,
+    taps,
+    columns,
+    filtered,
+    cells_back,
+    table_sem,
+    send_sem,
+    recv_sem,
+    chain_send,
+    chain_recv,
+    field_send,
+    field_recv,
+    back_send,
+    back_recv,
+):
+    low, wide = jnp.bfloat16, jnp.float32
+    links = Links(send_sem, recv_sem)
+    loads = (
+        pltpu.make_async_copy(table_hbm, table, table_sem.at[0]),
+        pltpu.make_async_copy(table_back_hbm, table_back, table_sem.at[1]),
+    )
+    for load in loads:
+        load.start()
+    quarter = full.shape[1] // 4
+    tile_count, side = owners.shape[0], master.shape[2]
+    most = master.shape[0] - 1
+    rows = pl.ds(pl.multiple_of(links.dp * quarter, quarter), quarter)
+    near_rows = pl.ds(pl.multiple_of(links.near * quarter, quarter), quarter)
+    rank, place = jnp.int32(0), []
+    for i in range(tile_count):
+        mine = owners[i] == links.seq
+        place.append((jnp.minimum(rank, most), mine))
+        rank = rank + jnp.where(mine, 1, 0)
+    for half in range(2):
+        order = half_tiles(half)
+        for j in range(0, len(order), 2):
+            pair = []
+            for i in order[j : j + 2]:
+                at, mine = place[i]
+                pair.append(jnp.where(mine, master[at, rows, :], 0.0))
+            own[half, :, j * side : (j + 2) * side] = jnp.concatenate(pair, axis=1).astype(own.dtype)
+    links.meet()
+    swaps, planes = [], []
+    for at in chunks:
+        swaps.append(
+            links.copy(own.at[1 - links.core, :, at], got.at[:, at], links.partner)
+        )
+        mine = full.at[links.core, rows, at]
+        other = full.at[links.core, near_rows, at]
+        both = full.at[links.core, :, at]
+        planes.append(
+            (
+                links.copy(mine, mine, links.to_near),
+                links.copy(mine, mine, links.to_far),
+                links.copy(other, other, links.to_far),
+                links.copy(both, both, links.partner),
+            )
+        )
+        swaps[-1].start()
+    chain = Chain(links, base, arrived, leaving, chain_send, chain_recv, chunks)
+    length, width = kv_spec.shape
+    lanes = half_lanes(width)
+    half_length = length // 2
+
+    def hidden_step():
+        hidden[...] = jnp.sin(phases_of(features[...], filter_in[...])).astype(low)
+
+    def taps_step(part):
+        span = slice(part * length // 4, (part + 1) * length // 4)
+        decay = jnp.exp(-features[span, 0:1] * channels[0:1, lanes]) * channels[1:2, lanes]
+        values = mul(hidden[span, :], filter_out[:, lanes].astype(low))
+        taps[span, :] = (values * decay).astype(low)
+
+    def spectrum_step(part):
+        span = slice(part * length // 4, (part + 1) * length // 4)
+        scale = jnp.where(first_row((length // 4, 1)), 1.0 / length, 2.0 / length)
+        if part % 2:
+            scale = 2.0 / length
+        taps_spec[span, :] = mul(table[span, :], taps[...]) * scale
+
+    def wait_table():
+        loads[0].wait()
+
+    fill = [hidden_step]
+    fill += [functools.partial(taps_step, i) for i in range(4)]
+    fill += [wait_table]
+    fill += [functools.partial(spectrum_step, i) for i in range(4)]
+    fill.reverse()
+
+    def fill_in(steps=1):
+        for _ in range(steps):
+            if fill:
+                fill.pop()()
+
+    def collect(k):
+        at = chunks[k]
+        swaps[k].wait()
+        base[:, at] = own[links.core, :, at] + got[:, at]
+        chain.begin(k)
+
+    def spread(k):
+        full[links.core, rows, chunks[k]] = chain.inward(k).astype(full.dtype)
+        planes[k][0].start()
+        planes[k][1].start()
+
+    def relay(k):
+        planes[k][0].wait_recv()
+        planes[k][2].start()
+
+    def share(k):
+        planes[k][1].wait_recv()
+        planes[k][2].wait_recv()
+        planes[k][3].start()
+
+    count = len(chunks)
+    fill_in(1)
+    for k in range(count):
+        collect(k)
+    stages = ((chain.outward, 0), (spread, 1), (relay, 2), (share, 4))
+    steps = [
+        [(stage, k - late) for stage, late in stages if 0 <= k - late < count]
+        for k in range(count + 4)
+    ]
+    before, after = steps[: first_chunks + 4], steps[first_chunks + 4 :]
+    for step in before:
+        fill_in(2)
+        for stage, k in step:
+            stage(k)
+    for k in range(first_chunks):
+        planes[k][3].wait_recv()
+    fill_in(len(fill))
+
+    row_len = kv.shape[1]
+    seqs = kv.shape[0] // 2
+    outbound = Exchange(links, kv, columns, field_send, field_recv)
+    for pair, bits in ((links.inner, (6, 7, 4, 5)), (links.outer, (2, 3, 1, 0))):
+        span = pl.ds(pl.multiple_of(pair * (seqs // 2) * row_len, row_len), seqs // 2 * row_len)
+        for i in range(12):
+            block = i // 3
+            part = mul(x[span, block * side : (block + 1) * side], tile_at(full, i // 6, (i % 6) * side))
+            target = (query, key, value)[i // 4]
+            at = (i % 4) * side
+            target[span, at : at + side] = part.astype(target.dtype)
+        for s in range(seqs // 2):
+            line = pl.ds(pl.multiple_of((pair * (seqs // 2) + s) * row_len, row_len), row_len)
+            for h in range(2):
+                part = slice(h * width, (h + 1) * width)
+                both = key[line, part].astype(wide) * value[line, part].astype(wide)
+                kv[2 * (pair * (seqs // 2) + s) + h] = both.astype(kv.dtype)
+        outbound.send(*bits)
+    for step in after:
+        for stage, k in step:
+            stage(k)
+    transform_arrivals(outbound, table, kv_spec)
+    real, imag = spectrum_product(
+        kv_spec[:half_length],
+        kv_spec[half_length:],
+        taps_spec[:half_length],
+        taps_spec[half_length:],
+        1.0,
+    )
+    filtered[:half_length] = real.astype(low)
+    filtered[half_length:] = imag.astype(low)
+    loads[1].wait()
+    inbound = Exchange(links, cells_back, conv, back_send, back_recv)
+    send_inverse(inbound, table_back, filtered)
+    for k in range(count):
+        chain.finish(k)
+        for copy in planes[k]:
+            copy.wait_send()
+        if k >= first_chunks:
+            planes[k][3].wait_recv()
+    outbound.sent()
+    inbound.arrived(*range(1, 2 * seqs))
+    inbound.sent()
+
+
+def forward_call(owners, master, x, features, channels, filter_in, filter_out, table, table_back, cells):
+    slots, side, _ = master.shape
+    width = owners.shape[0] // 2 * side
+    chunks = cut(0, 640, 1152, 2816, 4480, width)
+    low, wide = jnp.bfloat16, jnp.float32
+    quarter = side // 4
+    count = len(chunks)
+    devices, row_len, columns = cells
+    length = devices * row_len
+    shape = jax.ShapeDtypeStruct
+    anywhere = pl.BlockSpec(memory_space=pl.ANY)
+    spec = shape((length, columns), wide)
+    rows = shape(x.shape, low)
+    return pl.pallas_call(
+        functools.partial(forward_kernel, chunks, 2),
+        out_shape=(
+            shape((2, side, width), low),
+            rows,
+            rows,
+            rows,
+            shape(cells, low),
+            shape(cells, low),
+            spec,
+            spec,
+        ),
+        in_specs=[SMEM] + [VMEM] * 6 + [anywhere] * 2,
+        out_specs=(VMEM,) * 8,
+        scratch_shapes=[
+            pltpu.VMEM((2, quarter, width), low),
+            pltpu.VMEM((quarter, width), low),
+            pltpu.VMEM((quarter, width), low),
+            pltpu.VMEM((2, quarter, width), low),
+            pltpu.VMEM((2, quarter, width), low),
+            pltpu.VMEM((length, length), low),
+            pltpu.VMEM((length, length), low),
+            pltpu.VMEM((length, filter_in.shape[1]), low),
+            pltpu.VMEM((length, columns), low),
+            pltpu.VMEM(cells, low),
+            pltpu.VMEM((length, columns), low),
+            pltpu.VMEM(cells, low),
+            pltpu.SemaphoreType.DMA((2,)),
+            pltpu.SemaphoreType.DMA((5 * count,)),
+            pltpu.SemaphoreType.DMA((5 * count,)),
+            pltpu.SemaphoreType.DMA((2, count)),
+            pltpu.SemaphoreType.DMA((2, count)),
+        ]
+        + [pltpu.SemaphoreType.DMA((devices,))] * 4,
+        compiler_params=pltpu.CompilerParams(
+            collective_id=0, has_side_effects=True, vmem_limit_bytes=VMEM_LIMIT
+        ),
+        name="forward",
+    )(owners, master, x, features, channels, filter_in, filter_out, table, table_back)
+
+
+def reduce_kernel(
+    chunks,
+    tile_of_slot,
+    used,
+    grads,
+    spread,
+    mine_sum,
+    got,
+    near_in,
+    far_in,
+    far_out,
+    base,
+    arrived,
+    leaving,
+    total,
+    by_tile,
+    send_sem,
+    recv_sem,
+    chain_send,
+    chain_recv,
+):
+    links = Links(send_sem, recv_sem)
+    side = grads.shape[1]
+    quarter = side // 4
+    wide = jnp.float32
+
+    def rows_of(index):
+        return pl.ds(pl.multiple_of(index * quarter, quarter), quarter)
+
+    links.meet()
+    swaps, nears, diagonals, fars, shares = [], [], [], [], []
+    for at in chunks:
+        swaps.append(links.copy(grads.at[1 - links.core, :, at], got.at[:, at], links.partner))
+        swaps[-1].start()
+        nears.append(
+            links.copy(mine_sum.at[rows_of(links.near), at], near_in.at[0, :, at], links.to_near)
+        )
+        diagonals.append(
+            links.copy(
+                mine_sum.at[rows_of(links.diagonal), at], near_in.at[1, :, at], links.to_near
+            )
+        )
+        fars.append(links.copy(far_out.at[:, at], far_in.at[:, at], links.to_far))
+        part = total.at[links.core, :, at]
+        shares.append(links.copy(part, part, links.partner))
+    chain = Chain(links, base, arrived, leaving, chain_send, chain_recv, chunks)
+
+    def merge_cores(k):
+        at = chunks[k]
+        swaps[k].wait()
+        mine_sum[:, at] = (
+            grads[links.core, :, at].astype(wide) + got[:, at].astype(wide)
+        ).astype(mine_sum.dtype)
+        diagonals[k].start()
+        nears[k].start()
+
+    def go_far(k):
+        at = chunks[k]
+        diagonals[k].wait_recv()
+        far_out[:, at] = (
+            mine_sum[rows_of(links.far), at].astype(wide) + near_in[1, :, at].astype(wide)
+        ).astype(far_out.dtype)
+        fars[k].start()
+
+    def collect(k):
+        at = chunks[k]
+        nears[k].wait_recv()
+        fars[k].wait_recv()
+        base[:, at] = (
+            mine_sum[rows_of(links.dp), at].astype(wide)
+            + near_in[0, :, at].astype(wide)
+            + far_in[:, at].astype(wide)
+        )
+        chain.begin(k)
+
+    def end(k):
+        total[links.core, :, chunks[k]] = chain.inward(k).astype(total.dtype)
+        shares[k].start()
+
+    count = len(chunks)
+    for k in range(count + 4):
+        stages = ((merge_cores, 0), (go_far, 1), (collect, 2), (chain.outward, 3), (end, 4))
+        for stage, late in stages:
+            if 0 <= k - late < count:
+                stage(k - late)
+    for share in shares:
+        share.wait()
+    for half in range(2):
+        for j, i in enumerate(half_tiles(half)):
+            by_tile[i] = total[half, :, j * side : (j + 1) * side].astype(wide)
+    slots = tile_of_slot.shape[0]
+    tiles_wide = slots * side
+    mine = rows_of(links.dp)
+    for s in range(0, slots, 2):
+        pair = [jnp.where(used[k] > 0, by_tile[tile_of_slot[k]], 0.0) for k in (s, s + 1)]
+        spread[mine, s * side : (s + 2) * side] = jnp.concatenate(pair, axis=1).astype(spread.dtype)
+    first_extra = by_tile.shape[0] // 2 * side
+    extra = total.shape[2] - first_extra
+    for half in range(2):
+        begin = tiles_wide + half * extra
+        spread[mine, begin : begin + extra] = total[half, :, first_extra:]
+    at_home, other = spread.at[mine, :], spread.at[rows_of(links.near), :]
+    first = links.copy(at_home, at_home, links.to_near)
+    second = links.copy(at_home, at_home, links.to_far)
+    relay = links.copy(other, other, links.to_far)
+    first.start()
+    second.start()
+    first.wait_recv()
+    relay.start()
+    second.wait_recv()
+    relay.wait()
+    first.wait_send()
+    second.wait_send()
+    for k in range(count):
+        nears[k].wait_send()
+        diagonals[k].wait_send()
+        fars[k].wait_send()
+        chain.finish(k)
+
+
+def reduce_grads(tile_of_slot, used, grads):
+    _, side, width = grads.shape
+    slots = tile_of_slot.shape[0]
+    extra = width - NTILES // 2 * side
+    chunks = cut(0, 1152, 2304, 3456, 4480, 5504, width)
+    low = jnp.bfloat16
+    quarter = side // 4
+    count = len(chunks)
+    return pl.pallas_call(
+        functools.partial(reduce_kernel, chunks),
+        out_shape=jax.ShapeDtypeStruct((side, slots * side + 2 * extra), low),
+        in_specs=[
+            pl.BlockSpec(memory_space=pltpu.SMEM),
+            pl.BlockSpec(memory_space=pltpu.SMEM),
+            pl.BlockSpec(memory_space=pltpu.VMEM),
+        ],
+        out_specs=pl.BlockSpec(memory_space=pltpu.VMEM),
+        scratch_shapes=[
+            pltpu.VMEM((side, width), low),
+            pltpu.VMEM((side, width), low),
+            pltpu.VMEM((2, quarter, width), low),
+            pltpu.VMEM((quarter, width), low),
+            pltpu.VMEM((quarter, width), low),
+            pltpu.VMEM((quarter, width), jnp.float32),
+            pltpu.VMEM((2, quarter, width), low),
+            pltpu.VMEM((2, quarter, width), low),
+            pltpu.VMEM((2, quarter, width), low),
+            pltpu.VMEM((NTILES, quarter, side), jnp.float32),
+            pltpu.SemaphoreType.DMA((5 * count + 3,)),
+            pltpu.SemaphoreType.DMA((5 * count + 3,)),
+            pltpu.SemaphoreType.DMA((2, count)),
+            pltpu.SemaphoreType.DMA((2, count)),
+        ],
+        compiler_params=pltpu.CompilerParams(
+            collective_id=1, has_side_effects=True, vmem_limit_bytes=VMEM_LIMIT
+        ),
+        name="reduce_grads",
+    )(tile_of_slot, used, grads)
+
+
 def on_device_columns(
     tokens,
     cotangent,
@@ -1269,24 +1441,26 @@
     first_slot = seq_index * owner_cap
     own_tile = lax.dynamic_slice_in_dim(tile_of_slot, first_slot, owner_cap, 0)
     own_used = lax.dynamic_slice_in_dim(slot_used.astype(jnp.int32), first_slot, owner_cap, 0)
-    packed = gather_weights(owners, tile_master)
     x = tokens.reshape(count, model_width)
     cell_shape = (seq_devices, row_len, width)
-    taps_spec = plain_call(taps_kernel, "taps", shape((length, width), wide))(
-        features, channels, filter_in, filter_out, table
-    )
-    query, key, value, kv = plain_call(
-        qkv_kernel, "qkv", (shape(x.shape, low),) * 3 + (shape(cell_shape, low),)
-    )(x, packed)
 
     def exchange(cells):
         return lax.all_to_all(cells, "seq", 0, 0, tiled=True)
 
-    conv, kv_spec = plain_call(
-        conv_kernel, "conv", (shape(cell_shape, low), shape((length, width), wide))
-    )(exchange(kv), table, table_back, taps_spec)
+    packed, query, key, value, kv, conv, taps_spec, kv_spec = forward_call(
+        owners,
+        tile_master,
+        x,
+        features,
+        channels,
+        filter_in,
+        filter_out,
+        table,
+        table_back,
+        cell_shape,
+    )
     output, d_first, d_inner, d_query, grads, sums = layer_call(
-        exchange(conv), query, kv, x, cotangent.reshape(count, model_width), vectors, packed
+        conv, query, kv, x, cotangent.reshape(count, model_width), vectors, packed
     )
     d_conv, grad_out, grad_in = plain_call(
         conv_back_kernel,

time: 287 us -> 256 us (0.89)
  blocking collectives: 50.3 us -> 25.7 us
  waiting for transfers between devices: 31.9 us -> 17.5 us
  Pallas kernels: 188 us -> 200 us
  starting transfers between devices: 7.09 us -> 3.55 us
    pallas_call x1, Pallas kernels: 47.3 us -> 78 us  [forward_call(): pl.pallas_call(functools.partial(forward_kernel, chunks, 2), out_shape=(s...]
    all_to_all x2 -> x1, blocking collectives: 50.3 us -> 25.7 us  [exchange(): return lax.all_to_all(cells, 'seq', 0, 0, tiled=True)]
    pallas_call x6 -> x3, Pallas kernels: 57.1 us -> 39.5 us  [call(): pl.pallas_call(kernel, out_shape=out_shape, in_specs=[VMEM] * len(arrays)...]
    all_to_all x2 -> x1, waiting for transfers between devices: 31.9 us -> 17.5 us  [exchange(): return lax.all_to_all(cells, 'seq', 0, 0, tiled=True)]
    all_to_all x2 -> x1, starting transfers between devices: 7.09 us -> 3.55 us  [exchange(): return lax.all_to_all(cells, 'seq', 0, 0, tiled=True)]
  transfers between devices with their start and end apart: 2 -> 1, of which waited for: 2 -> 1; matrix products, arithmetic and copies ran while one was open for 1% -> 1% of each run, Pallas kernels for 2% -> 0%
where the time goes in v5:
time: 256 us; the launch traced here: 255 us
  Pallas kernels  200 us (78%)
  blocking collectives  25.7 us (10%)
  waiting for transfers between devices  17.5 us (7%)
  other arithmetic  3.93 us (2%)
  local copies, waits for them, and re-layouts  3.88 us (2%)
  starting transfers between devices  3.55 us (1%)
    pallas_call x1, Pallas kernels, forward_call(): pl.pallas_call(functools.partial(forward_kernel, chunks, 2), out_shape=(s...  78 us
    pallas_call x1, Pallas kernels, reduce_grads(): pl.pallas_call(functools.partial(reduce_kernel, chunks), out_shape=jax.Sh...  66.4 us
    pallas_call x3, Pallas kernels, call(): pl.pallas_call(kernel, out_shape=out_shape, in_specs=[VMEM] * len(arrays)...  39.5 us
    all_to_all x1, blocking collectives, exchange(): return lax.all_to_all(cells, 'seq', 0, 0, tiled=True)  25.7 us
    all_to_all x1, waiting for transfers between devices, exchange(): return lax.all_to_all(cells, 'seq', 0, 0, tiled=True)  17.5 us
    pallas_call x1, Pallas kernels, adam_call(): pl.pallas_call(functools.partial(adam_kernel, scale), grid=(slots // per_...  15.7 us
  transfers between devices with their start and end apart: 1, of which 1 were waited for; matrix products, arithmetic and copies ran while one was open for 1% of the time, Pallas kernels for 0%

profile of v5, /device:TPU:0, one launch (start us, length us, event | category | flops | bytes accessed | tf_op | source)
XLA Modules:
  0.0 255.1 jit_solution(5207548685544997987)
XLA Ops:
  0.7 78.0 %forward.1 = (bf16[2,192,6144]{2,1,0:T(8,128)(2,1)}, bf16[512,768]{1,0:T(8,128)(2,1)}, bf16[512,768]{1,0:T(8,128)(2,1)}, bf16[512,768]{1,0:T(8,128)(2,1)}, bf16[...) custom-call(s32[64]{0:T(128)} %owners.1, ...), custom_call_target="tpu_custom_call" | custom-call | tf_op jit(solution)/shard_map/forward/pallas_call | solution.py:1202
  78.6 21.9 %layer.1 = (bf16[512,768]{1,0:T(8,128)(2,1)}, f32[512,768]{1,0:T(8,128)}, bf16[8,128,384]{2,1,0:T(8,128)(2,1)}, bf16[512,768]{1,0:T(8,128)(2,1)}, bf16[2,192,4992]{2,1,0:T(8,128)(2,1)}, /*index=5*/f32[8,768]{1,0:T(8,128)}) custom-call(bf16[8,128,384]{2,1,0:T(8,128)(2,1)} %get-tuple-element.53.conv, bf16[512,768]{1,0:T(8,128)(2,1)} %get-tuple-element.54.query, ...), custom_call_target="tpu_custom_call" | custom-call | tf_op jit(solution)/shard_map/layer/pallas_call | solution.py:537
  100.5 25.7 %all_to_all.10.cells = bf16[8,128,384]{2,1,0:T(8,128)(2,1)} all-to-all(bf16[8,128,384]{2,1,0:T(8,128)(2,1)} %get-tuple-element.58.d_inner), channel_id=1, replica_groups=mesh['dp'=4,'seq'=8] {'seq'}, dimensions={0} | all-to-all | bytes 1572864 | tf_op jit(solution)/shard_map/all_to_all | solution.py:1448
  126.2 0.0 copy-start.3
  126.2 0.0 copy-start.2
  126.2 10.0 %conv_back.1 = (bf16[8,128,384]{2,1,0:T(8,128)(2,1)}, f32[128,384]{1,0:T(8,128)}, f32[8,128]{1,0:T(8,128)}) custom-call(bf16[8,128,384]{2,1,0:T(8,128)(2,1)} %all_to_all.10.cells, bf16[1024,1024]{1,0:T(8,128)(2,1)} %constant.31.clone.table_hbm.table, bf16[1024,1024]{1,0:T(8,128)(2,1)} %constant.32.clone.table_back_hbm.table_back, ...), custom_call_target="tpu_custom_call" | custom-call | tf_op jit(solution)/shard_map/conv_back/pallas_call | solution.py:537
  136.1 3.5 %all-to-all-start.1 = ((bf16[8,128,384]{2,1,0:T(8,128)(2,1)}), bf16[8,128,384]{2,1,0:T(8,128)(2,1)S(1)}, u32[]{:S(2)}, u32[]{:S(2)}) async-start(bf16[8,128,384]{2,1,0:T(8,128)(2,1)} %get-tuple-element.61), calls=%async_computation.1 | async-start | bytes 1572864 | tf_op jit(solution)/shard_map/all_to_all | solution.py:1448
  139.7 0.0 copy-done.3
  139.7 0.2 convert_reduce_fusion
  139.9 0.1 fusion
  140.0 0.6 dynamic_slice.6.used
  140.7 0.1 select_reduce_fusion
  140.8 0.6 dynamic_slice.7.tile_of_slot
  141.4 1.0 bitcast_dynamic-update-slice_fusion
  142.3 0.0 copy-done.2
  142.4 0.7 bitcast_dynamic-update-slice_fusion.1
  143.1 17.5 %all-to-all-done.1.d_conv = bf16[8,128,384]{2,1,0:T(8,128)(2,1)S(1)} async-done(((bf16[8,128,384]{2,1,0:T(8,128)(2,1)}), bf16[8,128,384]{2,1,0:T(8,128)(2,1)S(1)}, u32[]{:S(2)}, u32[]{:S(2)}) %all-to-all-start.1) | async-done | bytes 786464 | tf_op jit(solution)/shard_map/all_to_all | solution.py:1448
  160.6 0.0 copy-start.1
  160.6 0.9 copy-done.1
  161.5 0.0 copy-start
  161.6 7.6 %input_grad.1 = (f32[512,768]{1,0:T(8,128)}, bf16[2,192,1152]{2,1,0:T(8,128)(2,1)}) custom-call(bf16[8,128,384]{2,1,0:T(8,128)(2,1)} %copy-done.1, bf16[8,128,384]{2,1,0:T(8,128)(2,1)} %get-tuple-element.58.d_inner, bf16[512,768]{1,0:T(8,128)(2,1)} %get-tuple-element.62.d_query, bf16[512,768]{1,0:T(8,128)(2,1)} %get-tuple-element.63.key, ...), custom_call_target="tpu_custom_call" | custom-call | tf_op jit(solution)/shard_map/input_grad/pallas_call | solution.py:537
  169.2 0.0 copy-done
  169.2 3.6 %pad_maximum_fusion.grads = bf16[2,192,6528]{2,1,0:T(8,128)(2,1)} fusion(bf16[2,192,384]{2,1,0:T(8,128)(2,1)S(1)} %bitcast_dynamic-update-slice_fusion.1, bf16[2,192,4992]{2,1,0:T(8,128)(2,1)S(1)} %copy-done, bf16[2,192,1152]{2,1,0:T(8,128)(2,1)} %get-tuple-element.67), kind=kLoop, calls=%fused_computation | loop fusion | flops 15040512 | bytes 10027008 | tf_op jit(solution)/shard_map/concatenate | solution.py:1492
  172.7 66.4 %reduce_grads.1.reduced.extra = bf16[192,3840]{1,0:T(8,128)(2,1)} custom-call(s32[16]{0:T(128)} %dynamic_slice.7.tile_of_slot, s32[16]{0:T(128)} %dynamic_slice.6.used, bf16[2,192,6528]{2,1,0:T(8,128)(2,1)} %pad_maximum_fusion.grads), custom_call_target="tpu_custom_call" | custom-call | tf_op jit(solution)/shard_map/reduce_grads/pallas_call | solution.py:1371
  239.1 15.7 %adam.1 = (f32[16,192,192]{2,1,0:T(8,128)}, f32[16,192,192]{2,1,0:T(8,128)}, f32[16,192,192]{2,1,0:T(8,128)}, f32[16,192,192]{2,1,0:T(8,128)}, f32[5,768]{1,0:T(...) custom-call(s32[16]{0:T(128)} %dynamic_slice.6.used, ...), custom_call_target="tpu_custom_call" | custom-call | tf_op jit(solution)/shard_map/adam/pallas_call | solution.py:897
  (4 shorter events, 0.0 us)
Async XLA Ops:
  126.2 13.5 %copy-start.3 = (s32[64]{0:T(128)S(1)}, s32[64]{0:T(128)}, u32[]{:S(2)}) copy-start(s32[64]{0:T(128)} %owners.1) | copy-start | bytes 772
  126.2 16.2 %copy-start.2 = (f32[8,768]{1,0:T(8,128)S(1)}, f32[8,768]{1,0:T(8,128)}, u32[]{:S(2)}) copy-start(f32[8,768]{1,0:T(8,128)} %get-tuple-element.70) | copy-start | bytes 73732
  136.1 24.5 %all-to-all-start.1 = ((bf16[8,128,384]{2,1,0:T(8,128)(2,1)}), bf16[8,128,384]{2,1,0:T(8,128)(2,1)S(1)}, u32[]{:S(2)}, u32[]{:S(2)}) async-start(bf16[8,128,384]{2,1,0:T(8,128)(2,1)} %get-tuple-element.61), calls=%async_computation.1 | async-start | bytes 1572864 | tf_op jit(solution)/shard_map/all_to_all | solution.py:1448
  160.6 0.9 copy-start.1
  161.5 7.6 %copy-start = (bf16[2,192,4992]{2,1,0:T(8,128)(2,1)S(1)}, bf16[2,192,4992]{2,1,0:T(8,128)(2,1)}, u32[]{:S(2)}) copy-start(bf16[2,192,4992]{2,1,0:T(8,128)(2,1)} %get-tuple-element.68) | copy-start | bytes 11501572

commit v6 on v5

--- a/solution.py
+++ b/solution.py
@@ -585,42 +585,6 @@
 def half_lanes(width):
     half = lax.rem(lax.axis_index("seq"), 2)
     return pl.ds(pl.multiple_of(half * width, width), width)
-
-
-def conv_back_kernel(
-    cells,
-    table,
-    table_back,
-    taps_spec,
-    kv_spec,
-    features,
-    channels,
-    filter_in,
-    filter_out,
-    out,
-    grad_out,
-    grad_in,
-):
-    low = jnp.bfloat16
-    length, width = kv_spec.shape
-    half = length // 2
-    columns = cells[...].reshape(length, width)
-    back_real, back_imag = mul(table[:half], columns), mul(table[half:], columns)
-    real, imag = spectrum_product(back_real, back_imag, taps_spec[:half], taps_spec[half:], -1.0)
-    result = mul(table_back[:, :half], real.astype(low)) + mul(table_back[:, half:], imag.astype(low))
-    out[...] = result.astype(out.dtype).reshape(out.shape)
-    scale = jnp.where(first_row((half, 1)), 1.0 / length, 2.0 / length)
-    real, imag = spectrum_product(back_real, back_imag, kv_spec[:half], kv_spec[half:], -1.0)
-    real, imag = (real * scale).astype(low), (imag * scale).astype(low)
-    d_taps = mul(table_back[:, :half], real) + mul(table_back[:, half:], imag)
-    lanes = half_lanes(width)
-    scaled = (d_taps * decay_of(features, channels, lanes)).astype(low)
-    phases = phases_of(features[...], filter_in[...])
-    grad_out[...] = mul(jnp.sin(phases).astype(low), scaled, TN)
-    d_hidden = mul(scaled, filter_out[:, lanes].astype(low), NT) * jnp.cos(phases)
-    grad_in[...] = jnp.zeros_like(grad_in)
-    for i in range(filter_in.shape[0]):
-        grad_in[i : i + 1, :] = jnp.sum(features[:, i : i + 1] * d_hidden, axis=0, keepdims=True)
 
 
 def tile_at(packed, half, first):
@@ -816,34 +780,6 @@
     )(conv, query, kv, x, cotangent, vectors, packed)
 
 
-def input_kernel(d_conv, d_inner, d_query, key, value, x, d_first, vectors, packed, in_grad, grads, d_qkv):
-    wide, low = jnp.float32, jnp.bfloat16
-    side = packed.shape[1]
-    row_len, width = d_conv.shape[1:]
-    model = x.shape[1]
-    d_qkv[:, :model] = d_query[...]
-    for s in range(d_conv.shape[0] // 2):
-        rows = slice(s * row_len, (s + 1) * row_len)
-        for h in range(2):
-            lanes = slice(h * width, (h + 1) * width)
-            cell = 2 * s + h
-            d_kv = d_conv[cell].astype(wide) + vectors[4:5, lanes] * d_inner[cell].astype(wide)
-            d_qkv[rows, model + h * width : model + (h + 1) * width] = (
-                d_kv * value[rows, lanes].astype(wide)
-            ).astype(low)
-            d_qkv[rows, 2 * model + h * width : 2 * model + (h + 1) * width] = (
-                d_kv * key[rows, lanes].astype(wide)
-            ).astype(low)
-    per_block = 3 * side
-    for b in range(4):
-        mine = slice(b * side, (b + 1) * side)
-        here = d_qkv[:, b * per_block : (b + 1) * per_block]
-        at = (b % 2) * per_block
-        weights = packed[b // 2, :, at : at + per_block]
-        in_grad[:, mine] = d_first[:, mine] + mul(here, weights, NT)
-        grads[b // 2, :, at : at + per_block] = mul(x[:, mine], here, TN).astype(low)
-
-
 def adam(weight, moment, second, average, gradient, rate, decay):
     moment = beta_one * moment + (1.0 - beta_one) * gradient
     second = beta_two * second + (1.0 - beta_two) * gradient * gradient
@@ -853,13 +789,18 @@
     return (second, weight, keep_rate * average + (1.0 - keep_rate) * weight)
 
 
-def adam_kernel(scale, used, reduced, extra, *refs):
+def adam_kernel(scale, tile_of_slot, used, reduced, *refs):
     step = pl.program_id(0)
-    per_step, side, _ = refs[0].shape
+    per_step, side, _ = refs[3].shape
+    late, extra, refs = refs[:per_step], refs[per_step], refs[per_step + 1 :]
     tile_in, small_in, tile_out, small_out = refs[:4], refs[4:16], refs[16:20], refs[20:32]
     for k in range(per_step):
-        keep = used[step * per_step + k] > 0
-        gradient = reduced[:, k * side : (k + 1) * side].astype(jnp.float32) * scale
+        slot = step * per_step + k
+        keep, tile = used[slot] > 0, tile_of_slot[slot]
+        pair = late[k][0]
+        from_late = jnp.where(lax.rem(tile, 2) == 0, pair[:, :side], pair[:, side:])
+        gradient = jnp.where(tile < 12, from_late, reduced[:, k * side : (k + 1) * side])
+        gradient = jnp.where(keep, gradient.astype(jnp.float32) * scale, 0.0)
         tile_out[0][k] = gradient
         fresh = adam(*(ref[k] for ref in tile_in), gradient, 0.1, 0.01)
         for ref, values in zip(tile_out[1:], fresh):
@@ -868,16 +809,13 @@
     @pl.when(step == 0)
     def _():
         order, model = small_in[8].shape
-        width = model // 2
         count = small_in[0].shape[0]
-        features = small_in[4].shape[0]
+        count_in = small_in[4].shape[0]
         sums = extra[...].astype(jnp.float32) * scale
-        both = (sums[:, :width], sums[:, width:])
-        first = order + 8
         gradients = (
-            jnp.concatenate([part[order : order + count] for part in both], axis=1),
-            both[0][first : first + features, :order],
-            jnp.concatenate([part[:order] for part in both], axis=1),
+            jnp.concatenate([sums[h, order : order + count] for h in range(2)], axis=1),
+            sums[0, order + 8 : order + 8 + count_in, :order],
+            jnp.concatenate([sums[h, :order] for h in range(2)], axis=1),
         )
         rates = ((0.4, 0.0), (0.4, 0.01), (0.1, 0.01))
         for i, (gradient, rate) in enumerate(zip(gradients, rates)):
@@ -887,28 +825,38 @@
                 ref[...] = values
 
 
-def adam_call(scale, used, reduced, tile_state, small_state):
+def adam_call(scale, tile_of_slot, used, reduced, late, tile_state, small_state):
     slots, side, _ = tile_state[0].shape
-    model = small_state[0].shape[1]
+    width = small_state[0].shape[1] // 2
     per_step = 2
-    tile = pl.BlockSpec((per_step, side, side), lambda i: (i, 0, 0))
-    small = [pl.BlockSpec(a.shape, lambda i: (0, 0)) for a in small_state]
+    tile = pl.BlockSpec((per_step, side, side), lambda i, *_: (i, 0, 0))
+    small = [pl.BlockSpec(a.shape, lambda i, *_: (0, 0)) for a in small_state]
     shape = jax.ShapeDtypeStruct
+
+    def late_block(k):
+        def place(i, tiles, _):
+            at = jnp.minimum(tiles[i * per_step + k], 11)
+            return (at // 6, 0, at % 6 // 2)
+
+        return pl.BlockSpec((1, side, 2 * side), place)
+
+    first_extra = 6 * side // width
     return pl.pallas_call(
         functools.partial(adam_kernel, scale),
-        grid=(slots // per_step,),
         out_shape=tuple(shape(a.shape, a.dtype) for a in tile_state + small_state),
-        in_specs=[
-            SMEM,
-            pl.BlockSpec((side, per_step * side), lambda i: (0, i)),
-            pl.BlockSpec((side, model), lambda i: (0, slots * side // model)),
-        ]
-        + [tile] * 4
-        + small,
-        out_specs=[tile] * 4 + small,
+        grid_spec=pltpu.PrefetchScalarGridSpec(
+            num_scalar_prefetch=2,
+            grid=(slots // per_step,),
+            in_specs=[pl.BlockSpec((side, per_step * side), lambda i, *_: (0, i))]
+            + [late_block(k) for k in range(per_step)]
+            + [pl.BlockSpec((2, side, width), lambda i, *_: (0, 0, first_extra))]
+            + [tile] * 4
+            + small,
+            out_specs=[tile] * 4 + small,
+        ),
         compiler_params=pltpu.CompilerParams(vmem_limit_bytes=VMEM_LIMIT),
         name="adam",
-    )(used, reduced, reduced, *tile_state, *small_state)
+    )(tile_of_slot, used, reduced, *(late,) * per_step, late, *tile_state, *small_state)
 
 
 class Exchange:
@@ -960,16 +908,20 @@
 
 
 def transform_arrivals(exchange, table, spec):
+    for near in range(exchange.links.deep):
+        transform_pair(exchange, table, spec, near)
+
+
+def transform_pair(exchange, table, spec, near):
     step = 2 * exchange.columns.shape[1]
-    for near in range(exchange.links.deep):
-        exchange.arrived(2 * near, 2 * near + 1)
-        chip = flip(exchange.links.z, near)
-        lanes = pl.ds(pl.multiple_of(chip * step, step), step)
-        part = mul(table[:, lanes], columns_of_chip(exchange.columns, chip))
-        if near:
-            spec[...] += part
-        else:
-            spec[...] = part
+    exchange.arrived(2 * near, 2 * near + 1)
+    chip = flip(exchange.links.z, near)
+    lanes = pl.ds(pl.multiple_of(chip * step, step), step)
+    part = mul(table[:, lanes], columns_of_chip(exchange.columns, chip))
+    if near:
+        spec[...] += part
+    else:
+        spec[...] = part
 
 
 def send_inverse(exchange, table_back, filtered):
@@ -1159,10 +1111,14 @@
                 both = key[line, part].astype(wide) * value[line, part].astype(wide)
                 kv[2 * (pair * (seqs // 2) + s) + h] = both.astype(kv.dtype)
         outbound.send(*bits)
-    for step in after:
+    for near in range(links.deep):
+        transform_pair(outbound, table, kv_spec, near)
+        if near < len(after):
+            for stage, k in after[near]:
+                stage(k)
+    for step in after[links.deep :]:
         for stage, k in step:
             stage(k)
-    transform_arrivals(outbound, table, kv_spec)
     real, imag = spectrum_product(
         kv_spec[:half_length],
         kv_spec[half_length:],
@@ -1240,144 +1196,49 @@
     )(owners, master, x, features, channels, filter_in, filter_out, table, table_back)
 
 
-def reduce_kernel(
-    chunks,
-    tile_of_slot,
-    used,
-    grads,
-    spread,
-    mine_sum,
-    got,
-    near_in,
-    far_in,
-    far_out,
-    base,
-    arrived,
-    leaving,
-    total,
-    by_tile,
-    send_sem,
-    recv_sem,
-    chain_send,
-    chain_recv,
-):
-    links = Links(send_sem, recv_sem)
-    side = grads.shape[1]
-    quarter = side // 4
-    wide = jnp.float32
-
-    def rows_of(index):
-        return pl.ds(pl.multiple_of(index * quarter, quarter), quarter)
-
-    links.meet()
-    swaps, nears, diagonals, fars, shares = [], [], [], [], []
-    for at in chunks:
-        swaps.append(links.copy(grads.at[1 - links.core, :, at], got.at[:, at], links.partner))
-        swaps[-1].start()
-        nears.append(
-            links.copy(mine_sum.at[rows_of(links.near), at], near_in.at[0, :, at], links.to_near)
-        )
-        diagonals.append(
-            links.copy(
-                mine_sum.at[rows_of(links.diagonal), at], near_in.at[1, :, at], links.to_near
+class Reducer:
+    def __init__(self, links, grads, scratch, chunks):
+        (
+            self.mine_sum,
+            self.got,
+            self.near_in,
+            self.far_in,
+            self.far_out,
+            self.base,
+            arrived,
+            leaving,
+            chain_send,
+            chain_recv,
+        ) = scratch
+        self.links, self.grads, self.chunks = links, grads, chunks
+        self.count = len(chunks)
+        self.quarter = self.base.shape[0]
+        self.chain = Chain(links, self.base, arrived, leaving, chain_send, chain_recv, chunks)
+        self.swaps, self.nears, self.diagonals, self.fars = [], [], [], []
+        for at in chunks:
+            self.swaps.append(
+                links.copy(grads.at[1 - links.core, :, at], self.got.at[:, at], links.partner)
             )
-        )
-        fars.append(links.copy(far_out.at[:, at], far_in.at[:, at], links.to_far))
-        part = total.at[links.core, :, at]
-        shares.append(links.copy(part, part, links.partner))
-    chain = Chain(links, base, arrived, leaving, chain_send, chain_recv, chunks)
-
-    def merge_cores(k):
-        at = chunks[k]
-        swaps[k].wait()
-        mine_sum[:, at] = (
-            grads[links.core, :, at].astype(wide) + got[:, at].astype(wide)
-        ).astype(mine_sum.dtype)
-        diagonals[k].start()
-        nears[k].start()
-
-    def go_far(k):
-        at = chunks[k]
-        diagonals[k].wait_recv()
-        far_out[:, at] = (
-            mine_sum[rows_of(links.far), at].astype(wide) + near_in[1, :, at].astype(wide)
-        ).astype(far_out.dtype)
-        fars[k].start()
-
-    def collect(k):
-        at = chunks[k]
-        nears[k].wait_recv()
-        fars[k].wait_recv()
-        base[:, at] = (
-            mine_sum[rows_of(links.dp), at].astype(wide)
-            + near_in[0, :, at].astype(wide)
-            + far_in[:, at].astype(wide)
-        )
-        chain.begin(k)
-
-    def end(k):
-        total[links.core, :, chunks[k]] = chain.inward(k).astype(total.dtype)
-        shares[k].start()
-
-    count = len(chunks)
-    for k in range(count + 4):
-        stages = ((merge_cores, 0), (go_far, 1), (collect, 2), (chain.outward, 3), (end, 4))
-        for stage, late in stages:
-            if 0 <= k - late < count:
-                stage(k - late)
-    for share in shares:
-        share.wait()
-    for half in range(2):
-        for j, i in enumerate(half_tiles(half)):
-            by_tile[i] = total[half, :, j * side : (j + 1) * side].astype(wide)
-    slots = tile_of_slot.shape[0]
-    tiles_wide = slots * side
-    mine = rows_of(links.dp)
-    for s in range(0, slots, 2):
-        pair = [jnp.where(used[k] > 0, by_tile[tile_of_slot[k]], 0.0) for k in (s, s + 1)]
-        spread[mine, s * side : (s + 2) * side] = jnp.concatenate(pair, axis=1).astype(spread.dtype)
-    first_extra = by_tile.shape[0] // 2 * side
-    extra = total.shape[2] - first_extra
-    for half in range(2):
-        begin = tiles_wide + half * extra
-        spread[mine, begin : begin + extra] = total[half, :, first_extra:]
-    at_home, other = spread.at[mine, :], spread.at[rows_of(links.near), :]
-    first = links.copy(at_home, at_home, links.to_near)
-    second = links.copy(at_home, at_home, links.to_far)
-    relay = links.copy(other, other, links.to_far)
-    first.start()
-    second.start()
-    first.wait_recv()
-    relay.start()
-    second.wait_recv()
-    relay.wait()
-    first.wait_send()
-    second.wait_send()
-    for k in range(count):
-        nears[k].wait_send()
-        diagonals[k].wait_send()
-        fars[k].wait_send()
-        chain.finish(k)
-
-
-def reduce_grads(tile_of_slot, used, grads):
-    _, side, width = grads.shape
-    slots = tile_of_slot.shape[0]
-    extra = width - NTILES // 2 * side
-    chunks = cut(0, 1152, 2304, 3456, 4480, 5504, width)
-    low = jnp.bfloat16
-    quarter = side // 4
-    count = len(chunks)
-    return pl.pallas_call(
-        functools.partial(reduce_kernel, chunks),
-        out_shape=jax.ShapeDtypeStruct((side, slots * side + 2 * extra), low),
-        in_specs=[
-            pl.BlockSpec(memory_space=pltpu.SMEM),
-            pl.BlockSpec(memory_space=pltpu.SMEM),
-            pl.BlockSpec(memory_space=pltpu.VMEM),
-        ],
-        out_specs=pl.BlockSpec(memory_space=pltpu.VMEM),
-        scratch_shapes=[
+            self.nears.append(
+                links.copy(
+                    self.mine_sum.at[self.rows_of(links.near), at],
+                    self.near_in.at[0, :, at],
+                    links.to_near,
+                )
+            )
+            self.diagonals.append(
+                links.copy(
+                    self.mine_sum.at[self.rows_of(links.diagonal), at],
+                    self.near_in.at[1, :, at],
+                    links.to_near,
+                )
+            )
+            self.fars.append(links.copy(self.far_out.at[:, at], self.far_in.at[:, at], links.to_far))
+
+    @staticmethod
+    def scratch(side, width, count):
+        low, quarter = jnp.bfloat16, side // 4
+        return [
             pltpu.VMEM((side, width), low),
             pltpu.VMEM((side, width), low),
             pltpu.VMEM((2, quarter, width), low),
@@ -1386,18 +1247,384 @@
             pltpu.VMEM((quarter, width), jnp.float32),
             pltpu.VMEM((2, quarter, width), low),
             pltpu.VMEM((2, quarter, width), low),
-            pltpu.VMEM((2, quarter, width), low),
-            pltpu.VMEM((NTILES, quarter, side), jnp.float32),
-            pltpu.SemaphoreType.DMA((5 * count + 3,)),
-            pltpu.SemaphoreType.DMA((5 * count + 3,)),
             pltpu.SemaphoreType.DMA((2, count)),
             pltpu.SemaphoreType.DMA((2, count)),
-        ],
+        ]
+
+    def rows_of(self, index):
+        return pl.ds(pl.multiple_of(index * self.quarter, self.quarter), self.quarter)
+
+    def swap(self, k):
+        self.swaps[k].start()
+
+    def swap_half(self, k, half):
+        @pl.when(self.links.core != half)
+        def _():
+            self.swaps[k].start()
+
+    def merge_cores(self, k):
+        at, wide = self.chunks[k], jnp.float32
+        self.swaps[k].wait_recv()
+        self.mine_sum[:, at] = (
+            self.grads[self.links.core, :, at].astype(wide) + self.got[:, at].astype(wide)
+        ).astype(self.mine_sum.dtype)
+        self.diagonals[k].start()
+        self.nears[k].start()
+
+    def go_far(self, k):
+        at, wide = self.chunks[k], jnp.float32
+        self.diagonals[k].wait_recv()
+        self.far_out[:, at] = (
+            self.mine_sum[self.rows_of(self.links.far), at].astype(wide)
+            + self.near_in[1, :, at].astype(wide)
+        ).astype(self.far_out.dtype)
+        self.fars[k].start()
+
+    def collect(self, k):
+        at, wide = self.chunks[k], jnp.float32
+        self.nears[k].wait_recv()
+        self.fars[k].wait_recv()
+        self.base[:, at] = (
+            self.mine_sum[self.rows_of(self.links.dp), at].astype(wide)
+            + self.near_in[0, :, at].astype(wide)
+            + self.far_in[:, at].astype(wide)
+        )
+        self.chain.begin(k)
+
+    def outward(self, k):
+        self.chain.outward(k)
+
+    def finish(self, k):
+        self.swaps[k].wait_send()
+        self.nears[k].wait_send()
+        self.diagonals[k].wait_send()
+        self.fars[k].wait_send()
+        self.chain.finish(k)
+
+
+def run_stages(count, *stages):
+    for step in range(count + max(lag for _, lag in stages)):
+        for stage, lag in stages:
+            if 0 <= step - lag < count:
+                stage(step - lag)
+
+
+def backward_kernel(
+    chunks,
+    late_chunks,
+    tile_of_slot,
+    used,
+    d_inner,
+    grads,
+    sums,
+    taps_spec,
+    kv_spec,
+    features,
+    channels,
+    filter_in,
+    filter_out,
+    key,
+    value,
+    x,
+    d_first,
+    d_query,
+    vectors,
+    packed_hbm,
+    table_hbm,
+    table_back_hbm,
+    in_grad,
+    spread,
+    late_full,
+    columns,
+    cells_back,
+    d_conv,
+    spec,
+    filtered,
+    d_qkv,
+    table,
+    table_back,
+    packed,
+    late,
+    total,
+    by_tile,
+    table_sem,
+    send_sem,
+    recv_sem,
+    field_send,
+    field_recv,
+    back_send,
+    back_recv,
+    *scratch,
+):
+    low, wide = jnp.bfloat16, jnp.float32
+    links = Links(send_sem, recv_sem)
+    loads = (
+        pltpu.make_async_copy(table_hbm, table, table_sem.at[0]),
+        pltpu.make_async_copy(table_back_hbm, table_back, table_sem.at[1]),
+        pltpu.make_async_copy(
+            packed_hbm.at[:, :, pl.ds(0, packed.shape[2])], packed, table_sem.at[2]
+        ),
+    )
+    for load in loads:
+        load.start()
+    side = grads.shape[1]
+    quarter = side // 4
+    length, width = kv_spec.shape
+    half_length = length // 2
+    row_len = d_inner.shape[1]
+    model = x.shape[1]
+    devices = d_inner.shape[0]
+    early = Reducer(links, grads, scratch[: len(scratch) // 2], chunks)
+    tail = Reducer(links, late, scratch[len(scratch) // 2 :], late_chunks)
+    links.meet()
+    outbound = Exchange(links, d_inner, columns, field_send, field_recv)
+    outbound.send(6, 7, 4, 5, 2, 3, 1, 0)
+    for k in range(early.count):
+        early.swap(k)
+    late[...] = jnp.zeros_like(late)
+
+    for k in range(early.count):
+        early.merge_cores(k)
+    loads[0].wait()
+    per_pair = -(-early.count // links.deep)
+    for near in range(links.deep):
+        transform_pair(outbound, table, spec, near)
+        for k in range(near * per_pair, min((near + 1) * per_pair, early.count)):
+            early.go_far(k)
+    loads[1].wait()
+    real, imag = spectrum_product(
+        spec[:half_length],
+        spec[half_length:],
+        taps_spec[:half_length],
+        taps_spec[half_length:],
+        -1.0,
+    )
+    filtered[:half_length] = real.astype(low)
+    filtered[half_length:] = imag.astype(low)
+    inbound = Exchange(links, cells_back, d_conv, back_send, back_recv)
+    send_inverse(inbound, table_back, filtered)
+
+    def early_total(k):
+        total[links.core, :, chunks[k]] = early.chain.inward(k).astype(total.dtype)
+        shares[k].start()
+
+    shares = []
+    for at in chunks:
+        part = total.at[links.core, :, at]
+        shares.append(links.copy(part, part, links.partner))
+
+    scale = jnp.where(first_row((half_length, 1)), 1.0 / length, 2.0 / length)
+    real, imag = spectrum_product(
+        spec[:half_length], spec[half_length:], kv_spec[:half_length], kv_spec[half_length:], -1.0
+    )
+    filtered[:half_length] = (real * scale).astype(low)
+    filtered[half_length:] = (imag * scale).astype(low)
+    lanes = half_lanes(width)
+    scaled = mul(table_back[...], filtered[...]) * decay_of(features, channels, lanes)
+    scaled = scaled.astype(low)
+    phases = phases_of(features[...], filter_in[...])
+    order = filter_in.shape[1]
+    first_late = 6 * side
+    late[links.core, 0:order, first_late:] = mul(jnp.sin(phases).astype(low), scaled, TN).astype(low)
+    d_hidden = mul(scaled, filter_out[:, lanes].astype(low), NT) * jnp.cos(phases)
+    lines = [
+        jnp.sum(features[:, i : i + 1] * d_hidden, axis=0, keepdims=True)
+        for i in range(filter_in.shape[0])
+    ]
+    lines.append(jnp.zeros((8 - len(lines), order), wide))
+    in_lines = jnp.concatenate(lines, axis=0)
+    for half in range(2):
+        vector_lines = sums[:, half * width : (half + 1) * width]
+        if half == 0:
+            other = jnp.concatenate([in_lines, jnp.zeros((8, width - order), wide)], axis=1)
+        else:
+            other = jnp.zeros((8, width), wide)
+        both = jnp.concatenate([vector_lines, other], axis=0)
+        late[half, order : order + 16, first_late:] = both.astype(low)
+
+    d_qkv[:, :model] = d_query[...]
+    pair_rows = 2 * row_len
+
+    def fill_rows(pair):
+        for s in range(devices // 4):
+            line = pl.ds(pl.multiple_of((pair * (devices // 4) + s) * row_len, row_len), row_len)
+            for h in range(2):
+                part = slice(h * width, (h + 1) * width)
+                cell = 2 * (pair * (devices // 4) + s) + h
+                d_kv = d_conv[cell].astype(wide) + vectors[4:5, part] * d_inner[cell].astype(wide)
+                d_qkv[line, model + h * width : model + (h + 1) * width] = (
+                    d_kv * value[line, part].astype(wide)
+                ).astype(low)
+                d_qkv[line, 2 * model + h * width : 2 * model + (h + 1) * width] = (
+                    d_kv * key[line, part].astype(wide)
+                ).astype(low)
+
+    for k in range(early.count):
+        early.collect(k)
+    inbound.arrived(1, 2, 3)
+    fill_rows(links.outer)
+    inbound.arrived(4, 5, 6, 7)
+    fill_rows(links.inner)
+    early.outward(0)
+    per_block = 3 * side
+    for b in range(4):
+        mine = slice(b * side, (b + 1) * side)
+        here = d_qkv[:, b * per_block : (b + 1) * per_block]
+        at = (b % 2) * per_block
+        late[b // 2, :, at : at + per_block] = mul(x[:, mine], here, TN).astype(low)
+        if b % 2:
+            for k in range(tail.count):
+                tail.swap_half(k, b // 2)
+        early.outward(b + 1)
+        early_total(b)
+    for k in range(tail.count):
+        tail.merge_cores(k)
+    early_total(early.count - 1)
+    for share in shares:
+        share.wait()
+    for half in range(2):
+        for j, i in enumerate(half_tiles(half)):
+            if i >= 12:
+                at = (j - 6) * side
+                by_tile[i - 12] = total[half, :, at : at + side].astype(wide)
+    for k in range(tail.count):
+        tail.go_far(k)
+    slots = tile_of_slot.shape[0]
+    mine = early.rows_of(links.dp)
+    for s in range(0, slots, 2):
+        pair = []
+        for k in (s, s + 1):
+            values = by_tile[jnp.maximum(tile_of_slot[k] - 12, 0)]
+            pair.append(jnp.where(used[k] > 0, values, 0.0))
+        spread[mine, s * side : (s + 2) * side] = jnp.concatenate(pair, axis=1).astype(spread.dtype)
+    for k in range(tail.count):
+        tail.collect(k)
+    planes = []
+    for at in late_chunks:
+        at_home = late_full.at[links.core, mine, at]
+        other = late_full.at[links.core, early.rows_of(links.near), at]
+        both = late_full.at[links.core, :, at]
+        planes.append(
+            (
+                links.copy(at_home, at_home, links.to_near),
+                links.copy(at_home, at_home, links.to_far),
+                links.copy(other, other, links.to_far),
+                links.copy(both, both, links.partner),
+            )
+        )
+    at_home, other = spread.at[mine, :], spread.at[early.rows_of(links.near), :]
+    slot_copies = (
+        links.copy(at_home, at_home, links.to_near),
+        links.copy(at_home, at_home, links.to_far),
+        links.copy(other, other, links.to_far),
+    )
+    slot_copies[0].start()
+    slot_copies[1].start()
+
+    def input_gradient(b):
+        mine = slice(b * side, (b + 1) * side)
+        here = d_qkv[:, b * per_block : (b + 1) * per_block]
+        at = (b % 2) * per_block
+        weights = packed[b // 2, :, at : at + per_block]
+        in_grad[:, mine] = d_first[:, mine] + mul(here, weights, NT)
+
+    loads[2].wait()
+    input_gradient(0)
+    for k in range(tail.count):
+        tail.outward(k)
+    input_gradient(1)
+    slot_copies[0].wait_recv()
+    slot_copies[2].start()
+    for k in range(tail.count):
+        late_full[links.core, mine, late_chunks[k]] = tail.chain.inward(k).astype(late_full.dtype)
+        planes[k][0].start()
+        planes[k][1].start()
+    input_gradient(2)
+    for k in range(tail.count):
+        planes[k][0].wait_recv()
+        planes[k][2].start()
+    input_gradient(3)
+    for k in range(tail.count):
+        planes[k][1].wait_recv()
+        planes[k][2].wait_recv()
+        planes[k][3].start()
+    slot_copies[1].wait_recv()
+    slot_copies[2].wait_recv()
+    for copies in planes:
+        for copy in copies[:3]:
+            copy.wait_send()
+        copies[3].wait()
+    for copy in slot_copies:
+        copy.wait_send()
+    outbound.sent()
+    inbound.sent()
+    for k in range(early.count):
+        early.finish(k)
+    for k in range(tail.count):
+        tail.finish(k)
+
+
+def backward_call(tile_of_slot, used, d_inner, grads, sums, tables, filter_arrays, rows, packed):
+    _, side, width = grads.shape
+    devices, row_len, columns = d_inner.shape
+    length = devices * row_len
+    tokens, model = rows[2].shape
+    slots = tile_of_slot.shape[0]
+    late_width = 6 * side + columns
+    chunks = cut(0, 1152, 2176, 3200, 4096, width)
+    late_chunks = cut(0, 512, 1024, late_width)
+    low, wide = jnp.bfloat16, jnp.float32
+    quarter = side // 4
+    shape = jax.ShapeDtypeStruct
+    anywhere = pl.BlockSpec(memory_space=pl.ANY)
+    cells = pltpu.VMEM(d_inner.shape, low)
+    copies = 5 * len(chunks) + 8 * len(late_chunks) + 3
+    return pl.pallas_call(
+        functools.partial(backward_kernel, chunks, late_chunks),
+        out_shape=(
+            shape((tokens, model), wide),
+            shape((side, slots * side), low),
+            shape((2, side, late_width), low),
+        ),
+        in_specs=[SMEM] * 2
+        + [VMEM] * 15
+        + [anywhere] * 3,
+        out_specs=(VMEM,) * 3,
+        scratch_shapes=[
+            cells,
+            cells,
+            cells,
+            pltpu.VMEM((length, columns), wide),
+            pltpu.VMEM((length, columns), low),
+            pltpu.VMEM((tokens, 3 * model), low),
+            pltpu.VMEM((length, length), low),
+            pltpu.VMEM((length, length), low),
+            pltpu.VMEM((2, side, 6 * side), low),
+            pltpu.VMEM((2, side, late_width), low),
+            pltpu.VMEM((2, quarter, width), low),
+            pltpu.VMEM((NTILES - 12, quarter, side), wide),
+            pltpu.SemaphoreType.DMA((3,)),
+            pltpu.SemaphoreType.DMA((copies,)),
+            pltpu.SemaphoreType.DMA((copies,)),
+        ]
+        + [pltpu.SemaphoreType.DMA((devices,))] * 4
+        + Reducer.scratch(side, width, len(chunks))
+        + Reducer.scratch(side, late_width, len(late_chunks)),
         compiler_params=pltpu.CompilerParams(
             collective_id=1, has_side_effects=True, vmem_limit_bytes=VMEM_LIMIT
         ),
-        name="reduce_grads",
-    )(tile_of_slot, used, grads)
+        name="backward",
+    )(
+        tile_of_slot,
+        used,
+        d_inner,
+        grads,
+        sums,
+        *filter_arrays,
+        *rows,
+        packed,
+        *tables,
+    )
 
 
 def on_device_columns(
@@ -1444,9 +1671,6 @@
     x = tokens.reshape(count, model_width)
     cell_shape = (seq_devices, row_len, width)
 
-    def exchange(cells):
-        return lax.all_to_all(cells, "seq", 0, 0, tiled=True)
-
     packed, query, key, value, kv, conv, taps_spec, kv_spec = forward_call(
         owners,
         tile_master,
@@ -1462,40 +1686,24 @@
     output, d_first, d_inner, d_query, grads, sums = layer_call(
         conv, query, kv, x, cotangent.reshape(count, model_width), vectors, packed
     )
-    d_conv, grad_out, grad_in = plain_call(
-        conv_back_kernel,
-        "conv_back",
-        (shape(cell_shape, low), shape((order, width), wide), shape((8, order), wide)),
-    )(
-        exchange(d_inner),
-        table,
-        table_back,
-        taps_spec,
-        kv_spec,
-        features,
-        channels,
-        filter_in,
-        filter_out,
-    )
-    in_grad, grads_in = plain_call(
-        input_kernel,
-        "input_grad",
-        (shape(x.shape, wide), shape((2, side, 6 * side), low)),
-        [pltpu.VMEM((count, 3 * model_width), low)],
-    )(exchange(d_conv), d_inner, d_query, key, value, x, d_first, vectors, packed)
-    both = jnp.zeros((2, side, width), wide)
-    both = lax.dynamic_update_slice(both, grad_out[None], (lax.rem(seq_index, 2), 0, 0))
-    both = lax.dynamic_update_slice(
-        both, sums.reshape(8, 2, width).transpose(1, 0, 2), (0, order, 0)
-    )
-    both = lax.dynamic_update_slice(both, grad_in[None], (0, order + 8, 0))
-    packed_grads = jnp.concatenate([grads_in, grads, both.astype(low)], axis=2)
-    reduced = reduce_grads(own_tile, own_used, packed_grads)
+    in_grad, reduced, late = backward_call(
+        own_tile,
+        own_used,
+        d_inner,
+        grads,
+        sums,
+        (table, table_back),
+        (taps_spec, kv_spec, features, channels, filter_in, filter_out),
+        (key, value, x, d_first, d_query, vectors),
+        packed,
+    )
     tokens_all = count * lax.axis_size("dp") * seq_devices
     updated = adam_call(
         1.0 / math.sqrt(tokens_all),
+        own_tile,
         own_used,
         reduced,
+        late,
         (tile_master, tile_moment, tile_second, tile_average),
         (
             vectors,

time: 256 us -> 210 us (0.82)
  blocking collectives: 25.7 us -> 0 us
  waiting for transfers between devices: 17.5 us -> 0 us
  Pallas kernels: 200 us -> 207 us
  other arithmetic: 3.93 us -> 0.37 us
  starting transfers between devices: 3.55 us -> 0 us
    all_to_all x1 -> x0, blocking collectives: 25.7 us -> none  [exchange(): return lax.all_to_all(cells, 'seq', 0, 0, tiled=True)]
    pallas_call x2, Pallas kernels: 82.1 us -> 107 us  [the longest x1 90.6 us: backward_call(): pl.pallas_call(functools.partial(backward_kernel, chunks, late_chunks), o...]
    all_to_all x1 -> x0, waiting for transfers between devices: 17.5 us -> none  [exchange(): return lax.all_to_all(cells, 'seq', 0, 0, tiled=True)]
    pallas_call x3 -> x1, Pallas kernels: 39.5 us -> 22 us  [call(): pl.pallas_call(kernel, out_shape=out_shape, in_specs=[VMEM] * len(arrays)...]
    concatenate x1 -> x0, other arithmetic: 3.55 us -> none  [on_device_columns(): packed_grads = jnp.concatenate([grads_in, grads, both.astype(low)], axis=2)]
    all_to_all x1 -> x0, starting transfers between devices: 3.55 us -> none  [exchange(): return lax.all_to_all(cells, 'seq', 0, 0, tiled=True)]
  transfers between devices with their start and end apart: 1 -> 0, of which waited for: 1 -> 0; matrix products, arithmetic and copies ran while one was open for 1% -> 0% of each run, Pallas kernels for 0% -> 0%
where the time goes in v6:
time: 210 us
  Pallas kernels  207 us (99%)
  local copies, waits for them, and re-layouts  2.42 us (1%)
    pallas_call x1, Pallas kernels, backward_call(): pl.pallas_call(functools.partial(backward_kernel, chunks, late_chunks), o...  90.6 us
    pallas_call x1, Pallas kernels, forward_call(): pl.pallas_call(functools.partial(forward_kernel, chunks, 2), out_shape=(s...  78 us
    pallas_call x1, Pallas kernels, call(): pl.pallas_call(kernel, out_shape=out_shape, in_specs=[VMEM] * len(arrays)...  22 us
    pallas_call x1, Pallas kernels, adam_call(): pl.pallas_call(functools.partial(adam_kernel, scale), out_shape=tuple((sh...  15.9 us

profile of v6, /device:TPU:0, one launch (start us, length us, event | category | flops | bytes accessed | tf_op | source)
XLA Modules:
  0.0 210.0 jit_solution(15965650331121783072)
XLA Ops:
  0.7 78.0 %forward.1 = (bf16[2,192,6144]{2,1,0:T(8,128)(2,1)}, bf16[512,768]{1,0:T(8,128)(2,1)}, bf16[512,768]{1,0:T(8,128)(2,1)}, bf16[512,768]{1,0:T(8,128)(2,1)}, bf16[...) custom-call(s32[64]{0:T(128)} %owners.1, ...), custom_call_target="tpu_custom_call" | custom-call | tf_op jit(solution)/shard_map/forward/pallas_call | solution.py:1158
  78.7 0.0 copy-start.1
  78.7 22.0 %layer.1 = (bf16[512,768]{1,0:T(8,128)(2,1)}, f32[512,768]{1,0:T(8,128)}, bf16[8,128,384]{2,1,0:T(8,128)(2,1)}, bf16[512,768]{1,0:T(8,128)(2,1)}, bf16[2,192,4992]{2,1,0:T(8,128)(2,1)}, /*index=5*/f32[8,768]{1,0:T(8,128)}) custom-call(bf16[8,128,384]{2,1,0:T(8,128)(2,1)} %get-tuple-element.51.conv, bf16[512,768]{1,0:T(8,128)(2,1)} %get-tuple-element.52.query, ...), custom_call_target="tpu_custom_call" | custom-call | tf_op jit(solution)/shard_map/layer/pallas_call | solution.py:537
  100.6 0.0 copy-done.1
  100.6 0.2 convert_reduce_fusion
  100.8 0.1 select_reduce_fusion
  100.9 0.6 dynamic_slice.6.tile_of_slot
  101.5 0.1 fusion
  101.6 0.7 dynamic_slice.7.used
  102.3 90.6 %backward.1 = (f32[512,768]{1,0:T(8,128)}, bf16[192,3072]{1,0:T(8,128)(2,1)}, bf16[2,192,1536]{2,1,0:T(8,128)(2,1)}) custom-call(s32[16]{0:T(128)} %dynamic_slice.6.tile_of_slot, s32[16]{0:T(128)} %dynamic_slice.7.used, bf16[8,128,384]{2,1,0:T(8,128)(2,1)} %get-tuple-element.56.d_inner, bf16[2,192,4992]{2,1,0:T(8,128)(2,1)} %get-tuple-element.57.grads, ...), custom_call_target="tpu_custom_call" | custom-call | tf_op jit(solution)/shard_map/backward/pallas_call | solution.py:1582
  192.9 0.0 copy-start
  192.9 15.9 %adam.1 = (f32[16,192,192]{2,1,0:T(8,128)}, f32[16,192,192]{2,1,0:T(8,128)}, f32[16,192,192]{2,1,0:T(8,128)}, f32[16,192,192]{2,1,0:T(8,128)}, f32[5,768]{1,0:T(...) custom-call(s32[16]{0:T(128)} %dynamic_slice.6.tile_of_slot, ...), custom_call_target="tpu_custom_call" | custom-call | tf_op jit(solution)/shard_map/adam/pallas_call | solution.py:844
  208.9 0.0 copy-done
  208.9 1.1 copy.46
  (2 shorter events, 0.0 us)
Async XLA Ops:
  78.7 22.0 %copy-start.1 = (s32[64]{0:T(128)S(1)}, s32[64]{0:T(128)}, u32[]{:S(2)}) copy-start(s32[64]{0:T(128)} %owners.1) | copy-start | bytes 772
  192.9 16.0 %copy-start = (f32[512,768]{1,0:T(8,128)S(1)}, f32[512,768]{1,0:T(8,128)}, u32[]{:S(2)}) copy-start(f32[512,768]{1,0:T(8,128)} %get-tuple-element.65) | copy-start | bytes 4718596
